TPU v7x, 32 devices: a whole 2x2x4 slice. The times are simulated.
32 devices in a mesh: fsdp: 2 (over x), ctx: 4 (over y, core), tp: 4 (over z).
Axes of the slice: x: 2, y: 2, z: 4, core: 2. Of those that a mesh axis runs over, the one named last changes fastest.
Arguments:
- inputs: bfloat16 [8192, 2048], P(('fsdp', 'ctx'), 'tp'), may hold values from -6 to 6
- cotangent: bfloat16 [8192, 2048], P(('fsdp', 'ctx'), 'tp'), may hold values from -6 to 6
- first_gain: float32 [2048], replicated, may hold values from 0.5 to 1.5
- first_bias: float32 [2048], replicated, may hold values from -4 to 4
- qkv_weight: bfloat16 [2048, 3, 2048], P(('fsdp', 'ctx'), None, 'tp'), may hold values from -0.125 to 0.125
- qkv_bias: float32 [3, 2048], P(None, 'tp'), may hold values from -6 to 6
- out_weight: bfloat16 [2048, 2048], P('tp', ('fsdp', 'ctx')), may hold values from -0.75 to 0.75
- second_gain: float32 [2048], replicated, may hold values from 0.5 to 1.5
- second_bias: float32 [2048], replicated, may hold values from -4 to 4
- gate_weight: bfloat16 [2048, 5632], P(('fsdp', 'ctx'), 'tp'), may hold values from -0.125 to 0.125
- up_weight: bfloat16 [2048, 5632], P(('fsdp', 'ctx'), 'tp'), may hold values from -0.125 to 0.125
- down_weight: bfloat16 [5632, 2048], P('tp', ('fsdp', 'ctx')), may hold values from -0.078125 to 0.078125
- lengths: int32 [2, 8], P('fsdp'), may hold values from 0 to 2048, as said below
- fill_counts: int32 [2, 4], P('fsdp'), may hold values from 614 to 1024, as said below
Outputs:
- layer_out: bfloat16 [8192, 2048], P(('fsdp', 'ctx'), 'tp')
- grad_inputs: bfloat16 [8192, 2048], P(('fsdp', 'ctx'), 'tp')
- grad_first_gain: float32 [2048], replicated
- grad_first_bias: float32 [2048], replicated
- grad_qkv_weight: float32 [2048, 3, 2048], P(('fsdp', 'ctx'), None, 'tp')
- grad_qkv_bias: float32 [3, 2048], P(None, 'tp')
- grad_out_weight: float32 [2048, 2048], P('tp', ('fsdp', 'ctx'))
- grad_second_gain: float32 [2048], replicated
- grad_second_bias: float32 [2048], replicated
- grad_gate_weight: float32 [2048, 5632], P(('fsdp', 'ctx'), 'tp')
- grad_up_weight: float32 [2048, 5632], P(('fsdp', 'ctx'), 'tp')
- grad_down_weight: float32 [5632, 2048], P('tp', ('fsdp', 'ctx'))
Inputs may be any that keep to these rules, and one draw needn't show every extreme that they name: fill_counts[f, c] is the number of leading rows of block c of group f that hold tokens; the other rows of the block are padding; in every group some block is full. lengths[f, :] are the lengths of the 8 sequences packed in order into the token-holding rows of group f, block after block; they sum to the group's token-holding rows; a zero is an empty sequence; one sequence of every group is 2048 tokens long and has rows in the group's first and last block.
All inputs are finite; a program needn't handle non-finite values.
Results may differ from a plain program's by a relative error of at most 0.025.
Values may be sent and summed in bfloat16 or wider, within the bound.
No kernel may reach another device: no remote copies, remote signals or barrier semaphores. Data moves between devices by JAX's collectives and lax.ppermute only.
A program may use at most 256 MiB of HBM per device.

v0:
```python
import functools

import jax
import jax.numpy as jnp
from jax import lax
from jax.experimental import pallas as pl
from jax.experimental.pallas import tpu as pltpu
from jax.sharding import PartitionSpec as P

HEAD_DIM = 64
ROT = 16
EPSILON = 1e-05
NEGATIVE = -1e30
FLOOR = -1e20
VMEM_LIMIT = 56 * 1024 * 1024
TILE_Q = 512
TILE_K = 512
STRIP = 32
CHUNKS = 2
HALVES = 2

F32 = jnp.float32
BF16 = jnp.bfloat16


def layout(lengths, fill_counts, block_rows):
    blocks_count = fill_counts.shape[0]
    seq_count = lengths.shape[0]
    slot_index = jnp.arange(blocks_count * block_rows, dtype=jnp.int32)
    block_of = slot_index // block_rows
    within = slot_index - block_of * block_rows
    chooser = block_of[:, None] == jnp.arange(blocks_count, dtype=jnp.int32)[None, :]
    fill_here = jnp.sum(jnp.where(chooser, fill_counts[None, :], 0), axis=1)
    before = jnp.cumsum(fill_counts) - fill_counts
    before_here = jnp.sum(jnp.where(chooser, before[None, :], 0), axis=1)
    validity = within < fill_here
    used_index = before_here + within
    seq_ends = jnp.cumsum(lengths)
    sequence = jnp.sum((used_index[:, None] >= seq_ends[None, :]).astype(jnp.int32), axis=1)
    seq_starts = seq_ends - lengths
    picker = sequence[:, None] == jnp.arange(seq_count, dtype=jnp.int32)[None, :]
    start_here = jnp.sum(jnp.where(picker, seq_starts[None, :], 0), axis=1)
    after = before + fill_counts
    start_block = jnp.sum((seq_starts[:, None] >= after[None, :]).astype(jnp.int32), axis=1)
    start_block = jnp.minimum(start_block, blocks_count - 1)
    block_pick = start_block[:, None] == jnp.arange(blocks_count, dtype=jnp.int32)[None, :]
    start_before = jnp.sum(jnp.where(block_pick, before[None, :], 0), axis=1)
    start_slot = start_block * block_rows + seq_starts - start_before
    slot_here = jnp.sum(jnp.where(picker, start_slot[None, :], 0), axis=1)
    first_key = jnp.where(validity, slot_here, 0).astype(jnp.int32)
    last_key = jnp.where(validity, slot_index, -1).astype(jnp.int32)
    return (validity, used_index - start_here, first_key, last_key)


def rotary_tables(position):
    half = ROT // 2
    lane = jnp.arange(2 * HEAD_DIM, dtype=jnp.int32) % HEAD_DIM
    frequency = 10000.0 ** (-(2.0 * (lane % half).astype(F32)) / ROT)
    angles = position.astype(F32)[:, None] * frequency[None, :]
    cosine, sine = jnp.cos(angles), jnp.sin(angles)
    lane = lane[None, :]
    return (
        jnp.where(lane < ROT, cosine, 1.0),
        jnp.where(lane < half, -sine, 0.0),
        jnp.where((lane >= half) & (lane < ROT), sine, 0.0),
    )


def params(**extra):
    return pltpu.CompilerParams(vmem_limit_bytes=VMEM_LIMIT, **extra)


def takes(microseconds):
    return pl.CostEstimate(
        flops=int(microseconds * 1e8), bytes_accessed=0, transcendentals=0
    )


def whole(shape):
    return pl.BlockSpec(shape, lambda *_: (0,) * len(shape))


def anywhere(count):
    return [pl.BlockSpec(memory_space=pl.ANY)] * count


def write_half(out, values, half, unit):
    if unit % 128:
        out[...] = values[:, : out.shape[1]]
        return
    for block in range(out.shape[1] // unit):
        first = pl.multiple_of((2 * block + half) * unit, unit)
        out[:, block * unit : (block + 1) * unit] = values[:, pl.ds(first, unit)]


def dot(left, right):
    return jnp.dot(left, right, preferred_element_type=F32)


def dot_turned(left, right):
    return lax.dot_general(left, right, (((1,), (1,)), ((), ())), preferred_element_type=F32)


def tie(value, *needed):
    def kernel(*refs):
        del refs

    return pl.pallas_call(
        kernel,
        in_specs=anywhere(1 + len(needed)),
        out_specs=pl.BlockSpec(memory_space=pl.ANY),
        out_shape=jax.ShapeDtypeStruct(value.shape, value.dtype),
        input_output_aliases={0: 0},
        name="tie",
    )(value, *needed)


def add_kernel(left, right, *refs):
    refs[-1][...] = (left[...].astype(F32) + right[...].astype(F32)).astype(BF16)


def add(left, right, *needed):
    rows, columns = left.shape
    strip = min(rows, 512)
    block = pl.BlockSpec((strip, columns), lambda i: (i, 0))
    return pl.pallas_call(
        add_kernel,
        grid=(rows // strip,),
        in_specs=[block, block] + anywhere(len(needed)),
        out_specs=block,
        out_shape=jax.ShapeDtypeStruct(left.shape, BF16),
        compiler_params=params(),
        cost_estimate=takes(10),
        name="ring_add",
    )(left, right, *needed)


def project_kernel(tp, chunks, per, unit, place, *refs):
    rings, refs = refs[: tp * chunks], refs[tp * chunks :]
    gain, bias, weight, weight_bias, cosine, sine_up, sine_down = refs[:7]
    low, full, half, here, near, far, stack = refs[7:]
    outs = [here, near] + [far.at[way] for way in range(far.shape[0])]
    rows, width = low.shape[0] // chunks, rings[0].shape[1]
    depth = tp * width
    wide = here.shape[1]
    piece = wide // 3
    step = pl.program_id(0)

    @pl.when(pl.program_id(0) == 0)
    def _():
        strip = 128
        for start in range(0, rows * chunks, strip):
            chunk, first = start // rows, start % rows
            blocks = rings[chunk * tp : (chunk + 1) * tp]
            at = slice(start, start + strip)
            inner = slice(first, first + strip)
            parts = [block[inner, :].astype(F32) for block in blocks]
            centre = sum(jnp.sum(part, axis=1, keepdims=True) for part in parts) / depth
            parts = [part - centre for part in parts]
            spread = sum(jnp.sum(part * part, axis=1, keepdims=True) for part in parts) / depth
            scaling = lax.rsqrt(spread + EPSILON)
            for step in range(tp):
                owner = lax.rem(place[0] - step + tp, tp)
                columns = pl.ds(pl.multiple_of(owner * width, width), width)
                low[at, columns] = (
                    parts[step] * scaling * gain[:, columns] + bias[:, columns]
                ).astype(BF16)
                full[at, columns] = blocks[step][inner, :]
        write_half(half, low, 1 - lax.rem(place[1], 2), unit)
        share = rings[0].shape[0] - rows
        for chunk in range(chunks):
            for step in range(tp):
                owner = lax.rem(place[0] - step + tp, tp)
                stack[owner, chunk * share : (chunk + 1) * share, :] = rings[chunk * tp + step][
                    rows:, :
                ]

    product = dot(low[...], weight[...]) + weight_bias[...]
    groups = []
    for group in range(per):
        parts = []
        for part in range(3):
            first = (group * 3 + part) * piece
            values = product[:, first : first + piece]
            if part < 2:
                values = (
                    values * cosine[...]
                    + pltpu.roll(values, piece - ROT // 2, 1) * sine_up[...]
                    + pltpu.roll(values, ROT // 2, 1) * sine_down[...]
                )
            parts.append(values.astype(BF16))
        groups.append(parts)
    flip = lax.rem(place[1], per)
    for way, out in enumerate(outs):
        for group in range(per):

            @pl.when((step == way // per) & (jnp.bitwise_xor(group, flip) == way % per))
            def _():
                for part in range(3):
                    out[:, part * piece : (part + 1) * piece] = groups[group][part]


def project(rings, place, gain, bias, weight, weight_bias, tables, nctx, unit):
    chunks, tp = len(rings), len(rings[0])
    rows, width = tables[0].shape[0], rings[0][0].shape[1]
    depth = tp * width
    total = weight.shape[1]
    wide = total // nctx
    per = 2 if nctx % 2 == 0 else 1
    grid_spec = pltpu.PrefetchScalarGridSpec(
        num_scalar_prefetch=1,
        grid=(nctx // per,),
        in_specs=[whole(rings[0][0].shape)] * (tp * chunks)
        + [whole((1, depth))] * 2
        + [
            pl.BlockSpec((depth, per * wide), lambda i, s: (0, jnp.bitwise_xor(i, s[1] // per))),
            pl.BlockSpec((1, per * wide), lambda i, s: (0, jnp.bitwise_xor(i, s[1] // per))),
        ]
        + [whole((rows, 2 * HEAD_DIM))] * 3,
        out_specs=[whole((rows, depth))] * 2
        + [whole((rows, depth // 2))]
        + [whole((rows, wide))] * 2
        + [whole((nctx - 2, rows, wide)), whole((tp, unit, width))],
    )
    return pl.pallas_call(
        functools.partial(project_kernel, tp, chunks, per, unit),
        grid_spec=grid_spec,
        out_shape=[
            jax.ShapeDtypeStruct((rows, depth), BF16),
            jax.ShapeDtypeStruct((rows, depth), BF16),
            jax.ShapeDtypeStruct((rows, depth // 2), BF16),
        ]
        + [jax.ShapeDtypeStruct((rows, wide), BF16)] * 2
        + [
            jax.ShapeDtypeStruct((nctx - 2, rows, wide), BF16),
            jax.ShapeDtypeStruct((tp, unit, width), BF16),
        ],
        compiler_params=params(),
        cost_estimate=takes(60),
        name="project",
    )(
        place,
        *[block for blocks in rings for block in blocks],
        gain,
        bias,
        weight,
        weight_bias,
        *tables,
    )


def stack_heads(tile, heads):
    lane = lax.broadcasted_iota(jnp.int32, tile.shape, 1) // HEAD_DIM
    return jnp.concatenate(
        [jnp.where(lane == head, tile, jnp.zeros_like(tile)) for head in range(heads)], axis=0
    )


def load_pieces(place, pieces, nctx, held, block_rows):
    chunk_rows = pieces[0].shape[0]
    chunks = len(pieces) // nctx
    for chunk in range(chunks):
        for step in range(nctx):
            source = jnp.bitwise_xor(place, step)
            first = source * block_rows + chunk * chunk_rows
            held[pl.ds(pl.multiple_of(first, chunk_rows), chunk_rows), :] = pieces[
                chunk * nctx + step
            ][...]


def attend_kernel(nctx, heads, count, extra, block_rows, place, lows, ends, bounds, *refs):
    pieces = refs[:count]
    out, sent, logs, held, turned, total, high, sums, raw, chances = refs[count + extra :]
    tile_q, tile_k = out.shape[0], turned.shape[2]
    width = heads * HEAD_DIM
    index = pl.program_id(0)

    @pl.when(index == 0)
    def _():
        load_pieces(place[0], pieces, nctx, held, block_rows)
        for tile in range(turned.shape[0]):
            turned[tile] = jnp.transpose(held[tile * tile_k : (tile + 1) * tile_k, 2 * width :])

    query_rows = pl.ds(pl.multiple_of(index * tile_q, tile_q), tile_q)
    queries = stack_heads(held[query_rows, :width] * jnp.asarray(HEAD_DIM**-0.5, BF16), heads)
    total[...] = jnp.zeros_like(total)
    high[...] = jnp.full_like(high, FLOOR)
    sums[...] = jnp.zeros_like(sums)
    first_key, last_key = bounds[0:1, :], bounds[1:2, :]

    def one(tile, _):
        start = tile * tile_k
        keys = held[pl.ds(pl.multiple_of(start, tile_k), tile_k), width : 2 * width]
        last = jnp.minimum(last_key, ends[tile] - 1) - start
        first = first_key - start
        for head in range(heads):
            raw[head] = dot_turned(keys, queries[head * tile_q : (head + 1) * tile_q])
        for head in range(heads):
            peaks = jnp.broadcast_to(high[head], (8, tile_q))
            for begin in range(0, tile_k, STRIP):
                scores = raw[head, begin : begin + STRIP, :]
                row = lax.broadcasted_iota(jnp.int32, scores.shape, 0) + begin
                scores = jnp.where((row <= last) & (row >= first), scores, NEGATIVE)
                raw[head, begin : begin + STRIP, :] = scores
                for group in range(0, STRIP, 8):
                    peaks = jnp.maximum(peaks, scores[group : group + 8])
            highest = jnp.max(peaks, axis=0, keepdims=True)
            partial = jnp.zeros((8, tile_q), F32)
            for begin in range(0, tile_k, STRIP):
                raised = jnp.exp(raw[head, begin : begin + STRIP, :] - highest)
                chances[head, begin : begin + STRIP, :] = raised.astype(BF16)
                for group in range(0, STRIP, 8):
                    partial = partial + raised[group : group + 8]
            shrink = jnp.exp(high[head] - highest)
            sums[head] = sums[head] * shrink + jnp.sum(partial, axis=0, keepdims=True)
            values = turned[tile, head * HEAD_DIM : (head + 1) * HEAD_DIM, :]
            total[head] = total[head] * shrink + dot(values, chances[head])
            high[head] = highest
        return 0

    upper = (index * tile_q + tile_q - 1) // tile_k + 1
    lax.fori_loop(lows[index], upper, one, 0)
    results = []
    for head in range(heads):
        found = sums[head] > 0.0
        safe = jnp.where(found, sums[head], 1.0)
        results.append(total[head] * jnp.where(found, 1.0 / safe, 0.0))
        logs[head : head + 1, :] = jnp.where(found, high[head] + jnp.log(safe), 0.0)
    result = jnp.transpose(jnp.concatenate(results, axis=0)).astype(BF16)
    out[...] = result
    sent[...] = result


def attend(pieces, place, lows, ends, bounds, nctx, block_rows, *needed):
    total_rows = nctx * block_rows
    width = pieces[0].shape[1] // 3
    heads = width // HEAD_DIM
    steps = total_rows // TILE_Q
    grid_spec = pltpu.PrefetchScalarGridSpec(
        num_scalar_prefetch=3,
        grid=(steps,),
        in_specs=[pl.BlockSpec((2, TILE_Q), lambda i, *_: (0, i))]
        + [whole(piece.shape) for piece in pieces]
        + anywhere(len(needed)),
        out_specs=[
            pl.BlockSpec((TILE_Q, width), lambda i, *_: (i, 0)),
            pl.BlockSpec((TILE_Q, width), lambda i, *_: (i, 0)),
            pl.BlockSpec((heads, TILE_Q), lambda i, *_: (0, i)),
        ],
        scratch_shapes=[
            pltpu.VMEM((total_rows, 3 * width), BF16),
            pltpu.VMEM((total_rows // TILE_K, width, TILE_K), BF16),
            pltpu.VMEM((heads, HEAD_DIM, TILE_Q), F32),
            pltpu.VMEM((heads, 1, TILE_Q), F32),
            pltpu.VMEM((heads, 1, TILE_Q), F32),
            pltpu.VMEM((heads, TILE_K, TILE_Q), F32),
            pltpu.VMEM((heads, TILE_K, TILE_Q), BF16),
        ],
    )
    return pl.pallas_call(
        functools.partial(attend_kernel, nctx, heads, len(pieces), len(needed), block_rows),
        grid_spec=grid_spec,
        out_shape=[
            jax.ShapeDtypeStruct((total_rows, width), BF16),
            jax.ShapeDtypeStruct((total_rows, width), BF16),
            jax.ShapeDtypeStruct((heads, total_rows), F32),
        ],
        compiler_params=params(),
        cost_estimate=takes(200),
        name="attend",
    )(place, lows, ends, bounds, *pieces, *needed)


def attend_back_kernel(
    nctx, heads, count, extra, block_rows, place, lows, ends, bounds, logs, *refs
):
    pieces, refs = refs[:count], refs[count:]
    grad, attended, refs = refs[0], refs[1], refs[2 + extra :]
    here, near, far, refs = *refs[:3], refs[3:]
    held, turned, grad_keys, grad_values, grad_query, raw, raw_grad, chances, steps, merged = refs
    tile_q, tile_k = grad.shape[0], turned.shape[2]
    width = grad.shape[1]
    index = pl.program_id(0)
    scale = jnp.asarray(HEAD_DIM**-0.5, BF16)

    @pl.when(index == 0)
    def _():
        load_pieces(place[0], pieces, nctx, held, block_rows)
        for tile in range(turned.shape[0]):
            turned[tile] = jnp.transpose(
                held[tile * tile_k : (tile + 1) * tile_k, width : 2 * width]
            )
        grad_keys[...] = jnp.zeros_like(grad_keys)
        grad_values[...] = jnp.zeros_like(grad_values)

    query_rows = pl.ds(pl.multiple_of(index * tile_q, tile_q), tile_q)
    queries = stack_heads(held[query_rows, :width] * scale, heads)
    incoming = stack_heads(grad[...], heads)
    product = jnp.transpose(grad[...].astype(F32) * attended[...].astype(F32))
    centres = [
        jnp.sum(product[head * HEAD_DIM : (head + 1) * HEAD_DIM, :], axis=0, keepdims=True)
        for head in range(heads)
    ]
    first_key, last_key = bounds[0:1, :], bounds[1:2, :]
    grad_query[...] = jnp.zeros_like(grad_query)

    def one(tile, _):
        start = tile * tile_k
        key_rows = pl.ds(pl.multiple_of(start, tile_k), tile_k)
        last = jnp.minimum(last_key, ends[tile] - 1) - start
        first = first_key - start
        by_head = [slice(head * tile_q, (head + 1) * tile_q) for head in range(heads)]
        for head in range(heads):
            raw[head] = dot_turned(held[key_rows, width : 2 * width], queries[by_head[head]])
            raw_grad[head] = dot_turned(held[key_rows, 2 * width :], incoming[by_head[head]])
        for head in range(heads):
            for begin in range(0, tile_k, STRIP):
                at = slice(begin, begin + STRIP)
                row = lax.broadcasted_iota(jnp.int32, (STRIP, tile_q), 0) + begin
                allowed = (row <= last) & (row >= first)
                scores = raw[head, at, :] - logs[head : head + 1, :]
                chance = jnp.exp(jnp.where(allowed, scores, NEGATIVE))
                chances[head, at, :] = chance.astype(BF16)
                steps[head, at, :] = (chance * (raw_grad[head, at, :] - centres[head])).astype(BF16)
            grad_values[key_rows, :] += dot(chances[head], incoming[by_head[head]])
            grad_keys[key_rows, :] += dot(steps[head], queries[by_head[head]])
            keys = turned[tile, head * HEAD_DIM : (head + 1) * HEAD_DIM, :]
            grad_query[head] += dot(keys, steps[head])
        return 0

    upper = (index * tile_q + tile_q - 1) // tile_k + 1
    lax.fori_loop(lows[index], upper, one, 0)
    result = jnp.concatenate([grad_query[head] for head in range(heads)], axis=0)
    merged[query_rows, :width] = (jnp.transpose(result) * HEAD_DIM**-0.5).astype(BF16)

    @pl.when(index == pl.num_programs(0) - 1)
    def _():
        merged[:, width : 2 * width] = grad_keys[...].astype(BF16)
        merged[:, 2 * width :] = grad_values[...].astype(BF16)
        outs = [here, near] + [far.at[way] for way in range(nctx - 2)]
        for way, out in enumerate(outs):
            first = jnp.bitwise_xor(place[0], way) * block_rows
            out[...] = merged[pl.ds(pl.multiple_of(first, block_rows), block_rows), :]


def attend_back(pieces, place, lows, ends, bounds, logs, grad, attended, nctx, block_rows, *needed):
    total_rows, width = grad.shape
    heads = width // HEAD_DIM
    by_tile = pl.BlockSpec((TILE_Q, width), lambda i, *_: (i, 0))
    sent = (block_rows, 3 * width)
    sent = [sent, sent, (nctx - 2, *sent)]
    grid_spec = pltpu.PrefetchScalarGridSpec(
        num_scalar_prefetch=3,
        grid=(total_rows // TILE_Q,),
        in_specs=[
            pl.BlockSpec((2, TILE_Q), lambda i, *_: (0, i)),
            pl.BlockSpec((heads, TILE_Q), lambda i, *_: (0, i)),
        ]
        + [whole(piece.shape) for piece in pieces]
        + [by_tile] * 2
        + anywhere(len(needed)),
        out_specs=[whole(shape) for shape in sent],
        scratch_shapes=[
            pltpu.VMEM((total_rows, 3 * width), BF16),
            pltpu.VMEM((total_rows // TILE_K, width, TILE_K), BF16),
            pltpu.VMEM((total_rows, width), F32),
            pltpu.VMEM((total_rows, width), F32),
            pltpu.VMEM((heads, HEAD_DIM, TILE_Q), F32),
            pltpu.VMEM((heads, TILE_K, TILE_Q), F32),
            pltpu.VMEM((heads, TILE_K, TILE_Q), F32),
            pltpu.VMEM((heads, TILE_K, TILE_Q), BF16),
            pltpu.VMEM((heads, TILE_K, TILE_Q), BF16),
            pltpu.VMEM((total_rows, 3 * width), BF16),
        ],
    )
    return pl.pallas_call(
        functools.partial(
            attend_back_kernel, nctx, heads, len(pieces), len(needed), block_rows
        ),
        grid_spec=grid_spec,
        out_shape=[jax.ShapeDtypeStruct(shape, BF16) for shape in sent],
        compiler_params=params(),
        cost_estimate=takes(250),
        name="attend_back",
    )(place, lows, ends, bounds, logs, *pieces, grad, attended, *needed)


def mix_kernel(nctx, count, place, heads_in, weight, source, gain, bias, *refs):
    returned, mixed, *lows = refs[count:]
    rows, depth = mixed.shape
    step = pl.program_id(0)
    left = jnp.concatenate([heads_in[c, 0] for c in range(nctx)], axis=1)
    returned[...] = left

    @pl.when(step == 0)
    def _():
        mixed[...] = source[...].astype(F32)

    mixed[...] += dot_turned(left, weight[0])

    @pl.when(step == pl.num_programs(0) - 1)
    def _():
        values = mixed[...]
        values = values - jnp.mean(values, axis=1, keepdims=True)
        scaling = lax.rsqrt(jnp.mean(values * values, axis=1, keepdims=True) + EPSILON)
        values = (values * scaling * gain[...] + bias[...]).astype(BF16)
        part_rows = lows[0].shape[0]
        for part, low in enumerate(lows):
            low[...] = values[part * part_rows : (part + 1) * part_rows]


def mix(heads_in, weight, full, gain, bias, place, parts, *needed):
    nctx, tp, rows, piece = heads_in.shape
    depth = full.shape[1]
    head_width = nctx * piece
    grid_spec = pltpu.PrefetchScalarGridSpec(
        num_scalar_prefetch=1,
        grid=(tp,),
        in_specs=[
            pl.BlockSpec((nctx, 1, rows, piece), lambda k, s: (0, k, 0, 0)),
            pl.BlockSpec((1, depth, head_width), lambda k, s: (k, 0, 0)),
            pl.BlockSpec((rows, depth), lambda k, s: (s[0], 0)),
            whole((1, depth)),
            whole((1, depth)),
        ]
        + anywhere(len(needed)),
        out_specs=[
            pl.BlockSpec((rows, head_width), lambda k, s: (0, k)),
            whole((rows, depth)),
        ]
        + [whole((rows // parts, depth))] * parts,
    )
    return pl.pallas_call(
        functools.partial(mix_kernel, nctx, len(needed)),
        grid_spec=grid_spec,
        out_shape=[
            jax.ShapeDtypeStruct((rows, tp * head_width), BF16),
            jax.ShapeDtypeStruct((rows, depth), F32),
        ]
        + [jax.ShapeDtypeStruct((rows // parts, depth), BF16)] * parts,
        compiler_params=params(),
        cost_estimate=takes(50),
        name="mix",
    )(place, heads_in, weight, full, gain, bias, *needed)


def feed_kernel(cuts, parts, tp, first_one, place, low, cot, mixed, source, *refs):
    refs = refs[-(5 + parts + 4) :]
    kept, grad_gate, grad_up, hidden, out = refs[:5]
    partials, held, sems = refs[5 : 5 + parts], refs[-4:-1], refs[-1]
    unit = source.shape[1] // 3
    width = out.shape[2]

    def copies(index):
        first, size = cuts[index]
        at = pl.ds(first, size)
        return [
            pltpu.make_async_copy(
                source.at[:, pl.ds(which * unit, unit), at],
                held[which].at[:, :, at],
                sems.at[index * 3 + which],
            )
            for which in range(3)
        ]

    for index in range(len(cuts)):
        for copy in copies(index):
            copy.start()
    kept[...] = low[...]
    rows, depth = kept.shape[0] // parts, kept.shape[1]
    grads = jnp.concatenate([cot[block] for block in range(tp)], axis=1)
    for index, (first, size) in enumerate(cuts):
        for copy in copies(index):
            copy.wait()
        at = slice(first, first + size)
        gate_weight, up_weight, down_weight = [w[:, :, at].reshape(depth, size) for w in held]
        gate = dot(kept[...], gate_weight)
        up = dot(kept[...], up_weight)
        sigma = 1.0 / (1.0 + jnp.exp(-gate))
        active = gate * sigma
        hidden[:, at] = (active * up).astype(BF16)
        grad = dot(grads, down_weight)
        grad_gate[:, at] = (grad * up * sigma * (1.0 + gate * (1.0 - sigma))).astype(BF16)
        grad_up[:, at] = (grad * active).astype(BF16)
    gate_weight, up_weight, down_weight = [w[...].reshape(depth, w.shape[2]) for w in held]
    product = dot_turned(grad_gate[...], gate_weight) + dot_turned(grad_up[...], up_weight)
    for part in range(parts):
        partials[part][...] = product[part * rows : (part + 1) * rows].astype(BF16)
    values = dot_turned(hidden[...], down_weight)
    if first_one:
        values = values + mixed[...]
    for block in range(tp):
        out[block] = values[:, block * width : (block + 1) * width].astype(BF16)


def feed(low, cot, mixed, weights, step, tp, place, held, parts, *needed):
    rows, depth = low.shape
    part_rows = rows // parts
    blocks, triple, hidden = weights.shape
    cuts = []
    while sum(size for _, size in cuts) < hidden:
        first = sum(size for _, size in cuts)
        cuts.append((first, min(512, hidden - first)))
    by_owner = lambda columns: pl.BlockSpec(
        (rows, columns), lambda i, s: (lax.rem(s[0] - step + tp, tp), 0)
    )
    width = depth // tp
    blocks_of_owner = pl.BlockSpec(
        (tp, rows, width), lambda i, s: (0, lax.rem(s[0] - step + tp, tp), 0)
    )
    grid_spec = pltpu.PrefetchScalarGridSpec(
        num_scalar_prefetch=1,
        grid=(1,),
        in_specs=[whole((rows, depth)), blocks_of_owner, whole(mixed.shape)]
        + anywhere(1 + len(held) + len(needed)),
        out_specs=[by_owner(depth)]
        + [by_owner(hidden)] * 3
        + [blocks_of_owner]
        + [whole((part_rows, depth))] * parts,
        scratch_shapes=[pltpu.VMEM((blocks, triple // 3, hidden), BF16)] * 3
        + [pltpu.SemaphoreType.DMA((3 * len(cuts),))],
    )
    return pl.pallas_call(
        functools.partial(feed_kernel, tuple(cuts), parts, tp, step == 0),
        grid_spec=grid_spec,
        out_shape=[
            jax.ShapeDtypeStruct((tp * rows, columns), BF16)
            for columns in (depth, hidden, hidden, hidden)
        ]
        + [jax.ShapeDtypeStruct((tp, tp * rows, width), BF16)]
        + [jax.ShapeDtypeStruct((part_rows, depth), BF16)] * parts,
        input_output_aliases={5 + index: index for index in range(len(held))},
        compiler_params=params(),
        cost_estimate=takes(100),
        name="feed",
    )(place, low, cot, mixed, weights, *held, *needed)


def blame_halves(lefts, rights, place, unit, *needed, held=(), offset=0, total=None):
    rows, other = rights[0].shape
    picked = lefts[1].shape[1] // unit
    chosen = pl.BlockSpec((rows, unit), lambda j, s: (0, 2 * (j ^ s[3]) + s[1] % 2))
    if lefts[0].ndim == 3:
        per = lefts[0].shape[2] // unit
        chosen = pl.BlockSpec(
            (1, rows, unit),
            lambda j, s: (
                (2 * (j ^ s[3]) + s[1] % 2) // per,
                0,
                lax.rem(2 * (j ^ s[3]) + s[1] % 2, per),
            ),
        )
    cut = pl.BlockSpec((rows, unit), lambda j, s: (0, j ^ s[3]))
    shapes = [(2, unit // 2, total or other)] * 4

    def kernel(place, left_here, left_there, right_here, right_there, *refs):
        outs, spare, sems = refs[len(held) + len(needed) : -2], refs[-2], refs[-1]
        product = 0.0
        for left, right in ((left_here, right_here), (left_there, right_there)):
            ours = left[0] if len(left.shape) == 3 else left[...]
            product = product + lax.dot_general(
                ours, right[...], (((0,), (0,)), ((), ())), preferred_element_type=F32
            )
        product = product.astype(BF16)
        for j in range(picked):

            @pl.when(pl.program_id(0) == j)
            def _():
                first, second = spare.at[j // 2, j % 2], spare.at[2 + j % 2, j // 2]
                first[...], second[...] = product[: unit // 2], product[unit // 2 :]

        @pl.when(pl.program_id(0) == picked - 1)
        def _():
            moves = [
                pltpu.make_async_copy(
                    spare.at[index], out.at[:, :, pl.ds(offset, other)], sems.at[index]
                )
                for index, out in enumerate(outs)
            ]
            for move in moves:
                move.start()
            for move in moves:
                move.wait()

    grid_spec = pltpu.PrefetchScalarGridSpec(
        num_scalar_prefetch=1,
        grid=(picked,),
        in_specs=[chosen, cut]
        + [whole((rows, other))] * 2
        + anywhere(len(held) + len(needed)),
        out_specs=anywhere(4),
        scratch_shapes=[
            pltpu.VMEM((4, 2, unit // 2, other), BF16),
            pltpu.SemaphoreType.DMA((4,)),
        ],
    )
    place = jnp.concatenate([place, place[2:3] * 2 + place[1:2] // 2])
    return pl.pallas_call(
        kernel,
        grid_spec=grid_spec,
        out_shape=[jax.ShapeDtypeStruct(shape, BF16) for shape in shapes],
        input_output_aliases={5 + index: index for index in range(len(held))},
        compiler_params=params(),
        cost_estimate=takes(60),
        name="blame_halves",
    )(place, *lefts, *rights, *held, *needed)


def blame(left, right, *needed):
    rows, columns = left.shape
    if right.ndim == 3:
        steps, other = right.shape[0], right.shape[2]
        in_specs = [whole((rows, columns)), pl.BlockSpec((1, rows, other), lambda j: (j, 0, 0))]
        target, shape = pl.BlockSpec((columns, other), lambda j: (0, j)), (columns, steps * other)
    else:
        steps, other = 4, right.shape[1]
        in_specs = [pl.BlockSpec((rows, columns // steps), lambda j: (0, j)), whole((rows, other))]
        target, shape = pl.BlockSpec((columns // steps, other), lambda j: (j, 0)), (columns, other)

    def kernel(left, right, *refs):
        theirs = right[0] if len(right.shape) == 3 else right[...]
        refs[-1][...] = lax.dot_general(
            left[...], theirs, (((0,), (0,)), ((), ())), preferred_element_type=F32
        ).astype(BF16)

    return pl.pallas_call(
        kernel,
        grid=(steps,),
        in_specs=in_specs + anywhere(len(needed)),
        out_specs=target,
        out_shape=jax.ShapeDtypeStruct(shape, BF16),
        compiler_params=params(),
        cost_estimate=takes(60),
        name="blame",
    )(left, right, *needed)


def turn_kernel(nctx, count, parts, unit, place, *refs):
    arrived, own = refs[:parts], refs[parts : 2 * parts]
    mixed, cot, gain = refs[2 * parts : 2 * parts + 3]
    weight, refs = refs[2 * parts + 3], refs[2 * parts + 4 + count :]
    out, grad_mixed, grad_low, gain_grad, shift_grad, half = refs
    rows, depth = mixed.shape
    piece = out.shape[3]

    @pl.when(pl.program_id(0) == 0)
    def _():
        incoming = jnp.concatenate(
            [there[...].astype(F32) + here[...].astype(F32) for there, here in zip(arrived, own)]
        )
        values = mixed[...]
        values = values - jnp.mean(values, axis=1, keepdims=True)
        scaling = lax.rsqrt(jnp.mean(values * values, axis=1, keepdims=True) + EPSILON)
        normed = values * scaling
        shift_grad[...] = jnp.sum(incoming, axis=0, keepdims=True)
        gain_grad[...] = jnp.sum(incoming * normed, axis=0, keepdims=True)
        scaled = incoming * gain[...]
        grads = jnp.concatenate([cot[block] for block in range(cot.shape[0])], axis=1)
        total = grads.astype(F32) + scaling * (
            scaled
            - jnp.mean(scaled, axis=1, keepdims=True)
            - normed * jnp.mean(scaled * normed, axis=1, keepdims=True)
        )
        grad_mixed[...] = total
        grad_low[...] = total.astype(BF16)
        write_half(half, grad_low, 1 - lax.rem(place[1], 2), unit)

    product = dot(grad_low[...], weight[0])
    for c in range(nctx):
        out[c, 0] = product[:, c * piece : (c + 1) * piece].astype(BF16)


def turn(arrived, own, mixed, cot, gain, weight, place, nctx, tp, unit, *needed):
    rows, depth = mixed.shape
    parts = len(arrived)
    head_width = weight.shape[2]
    piece = head_width // nctx
    grid_spec = pltpu.PrefetchScalarGridSpec(
        num_scalar_prefetch=1,
        grid=(tp,),
        in_specs=[whole((rows // parts, depth))] * (2 * parts)
        + [whole((rows, depth))]
        + [
            pl.BlockSpec((tp, rows, depth // tp), lambda k, s: (0, s[0], 0)),
            whole((1, depth)),
            pl.BlockSpec((1, depth, head_width), lambda k, s: (k, 0, 0)),
        ]
        + anywhere(len(needed)),
        out_specs=[
            pl.BlockSpec((nctx, 1, rows, piece), lambda k, s: (0, k, 0, 0)),
            whole((rows, depth)),
            whole((rows, depth)),
            whole((1, depth)),
            whole((1, depth)),
            whole((rows, depth // 2)),
        ],
    )
    return pl.pallas_call(
        functools.partial(turn_kernel, nctx, len(needed), parts, unit),
        grid_spec=grid_spec,
        out_shape=[
            jax.ShapeDtypeStruct((nctx, tp, rows, piece), BF16),
            jax.ShapeDtypeStruct((rows, depth), F32),
            jax.ShapeDtypeStruct((rows, depth), BF16),
            jax.ShapeDtypeStruct((1, depth), F32),
            jax.ShapeDtypeStruct((1, depth), F32),
            jax.ShapeDtypeStruct((rows, depth // 2), BF16),
        ],
        compiler_params=params(),
        cost_estimate=takes(60),
        name="turn",
    )(place, *arrived, *own, mixed, cot, gain, weight, *needed)


def finish_kernel(nctx, tp, extra_count, place, *refs):
    pieces = refs[:nctx]
    cosine, sine_up, sine_down, full, extra, gain = refs[nctx : nctx + 6]
    weight, refs = refs[nctx + 6], refs[nctx + 7 + extra_count :]
    outs = refs[:tp]
    low, bias_grad, gain_grad, shift_grad, spare = refs[tp:]
    rows, wide = pieces[0].shape
    piece = wide // 3
    width = outs[0].shape[1]
    strip = spare.shape[0]
    extra_rows = extra.shape[0]

    @pl.when(pl.program_id(0) == 0)
    def _():
        bias_grad[...] = jnp.zeros_like(bias_grad)
        gain_grad[...] = jnp.zeros_like(gain_grad)
        shift_grad[...] = jnp.zeros_like(shift_grad)

    for step in range(nctx):
        source = jnp.bitwise_xor(place[1], step)
        for part in range(3):
            values = pieces[step][:, part * piece : (part + 1) * piece].astype(F32)
            if part < 2:
                values = (
                    values * cosine[...]
                    - pltpu.roll(values, piece - ROT // 2, 1) * sine_up[...]
                    - pltpu.roll(values, ROT // 2, 1) * sine_down[...]
                )
            columns = pl.ds(pl.multiple_of(source * wide + part * piece, piece), piece)
            bias_grad[:, columns] += jnp.sum(values, axis=0, keepdims=True)
            low[:, columns] = values.astype(BF16)

    incoming = dot_turned(low[...], weight[...])
    source = full[...].astype(F32)
    source = source - jnp.mean(source, axis=1, keepdims=True)
    scaling = lax.rsqrt(jnp.mean(source * source, axis=1, keepdims=True) + EPSILON)
    normed = source * scaling
    shift_grad[...] += jnp.sum(incoming, axis=0, keepdims=True)
    gain_grad[...] += jnp.sum(incoming * normed, axis=0, keepdims=True)
    scaled = incoming * gain[...]
    spare[...] = scaling * (
        scaled
        - jnp.mean(scaled, axis=1, keepdims=True)
        - normed * jnp.mean(scaled * normed, axis=1, keepdims=True)
    )
    first = pl.program_id(0) * strip
    wanted = place[0] * extra_rows

    if strip <= extra_rows:

        @pl.when((first >= wanted) & (first < wanted + extra_rows))
        def _():
            spare[...] += extra[pl.ds(pl.multiple_of(first - wanted, strip), strip), :]

    else:

        @pl.when((wanted >= first) & (wanted < first + strip))
        def _():
            spare[pl.ds(pl.multiple_of(wanted - first, extra_rows), extra_rows), :] += extra[...]

    for step, out in enumerate(outs):
        owner = lax.rem(place[0] - step + tp, tp)
        out[...] = spare[:, pl.ds(pl.multiple_of(owner * width, width), width)].astype(BF16)


def finish(pieces, place, tables, full, extra, gain, weight, tp, *needed):
    rows, wide = pieces[0].shape
    depth = full.shape[1]
    total = weight.shape[1]
    strip = 256
    steps = rows // strip
    width = depth // tp
    nctx = len(pieces)
    by_rows = lambda columns: pl.BlockSpec((strip, columns), lambda i, s: (i, 0))
    grid_spec = pltpu.PrefetchScalarGridSpec(
        num_scalar_prefetch=1,
        grid=(steps,),
        in_specs=[by_rows(wide)] * nctx
        + [by_rows(2 * HEAD_DIM)] * 3
        + [
            by_rows(depth),
            whole(extra.shape),
            whole((1, depth)),
        ]
        + [whole(weight.shape)]
        + anywhere(len(needed)),
        out_specs=[by_rows(width)] * tp
        + [
            by_rows(total),
            whole((1, total)),
            whole((1, depth)),
            whole((1, depth)),
        ],
        scratch_shapes=[pltpu.VMEM((strip, depth), F32)],
    )
    return pl.pallas_call(
        functools.partial(finish_kernel, nctx, tp, len(needed)),
        grid_spec=grid_spec,
        out_shape=[jax.ShapeDtypeStruct((rows, width), BF16)] * tp
        + [
            jax.ShapeDtypeStruct((rows, total), BF16),
            jax.ShapeDtypeStruct((1, total), F32),
            jax.ShapeDtypeStruct((1, depth), F32),
            jax.ShapeDtypeStruct((1, depth), F32),
        ],
        compiler_params=params(),
        cost_estimate=takes(70),
        name="finish",
    )(place, *pieces, *tables, full, extra, gain, weight, *needed)


def join(rings, place, unit):
    parts, tp = len(rings), len(rings[0])
    rows, width = rings[0][0].shape

    def kernel(place, *refs):
        for part in range(parts):
            for step in range(tp):
                owner = lax.rem(place[0] - step + tp, tp)
                refs[-2][owner, part * rows : (part + 1) * rows, :] = refs[part * tp + step][...]
        per, half = width // unit, 1 - lax.rem(place[1], 2)
        for block in range(tp * per // 2):
            index = 2 * block + half if unit % 128 == 0 else 0
            first = pl.multiple_of(lax.rem(index, per) * unit, unit)
            if unit % 128:
                first = 0
            refs[-1][:, block * unit : (block + 1) * unit] = refs[-2][
                lax.div(index, per), :, pl.ds(first, unit)
            ]

    grid_spec = pltpu.PrefetchScalarGridSpec(
        num_scalar_prefetch=1,
        grid=(1,),
        in_specs=[whole((rows, width))] * (parts * tp),
        out_specs=[whole((tp, parts * rows, width)), whole((parts * rows, tp * width // 2))],
    )
    return pl.pallas_call(
        kernel,
        grid_spec=grid_spec,
        out_shape=[
            jax.ShapeDtypeStruct((tp, parts * rows, width), BF16),
            jax.ShapeDtypeStruct((parts * rows, tp * width // 2), BF16),
        ],
        compiler_params=params(),
        cost_estimate=takes(10),
        name="join",
    )(place, *[block for blocks in rings for block in blocks])


def pack_kernel(gate, up, down, out):
    rows = gate.shape[0]
    out[:rows] = gate[...]
    out[rows : 2 * rows] = up[...]
    out[2 * rows :] = jnp.transpose(down[...])


def pack(gate, up, down):
    rows, columns = gate.shape
    return pl.pallas_call(
        pack_kernel,
        out_shape=jax.ShapeDtypeStruct((3 * rows, columns), BF16),
        compiler_params=params(),
        cost_estimate=takes(10),
        name="pack",
    )(gate, up, down)


def contract_rows(left, right):
    return lax.dot_general(left, right, (((0,), (0,)), ((), ())), preferred_element_type=F32)


def pick(stack, index):
    return lax.dynamic_index_in_dim(stack, index, 0, keepdims=False)


def shards(
    nfsdp,
    nctx,
    tp,
    inputs,
    cotangent,
    first_gain,
    first_bias,
    qkv_weight,
    qkv_bias,
    out_weight,
    second_gain,
    second_bias,
    gate_weight,
    up_weight,
    down_weight,
    lengths,
    fill_counts,
):
    data = ("fsdp", "ctx")
    ndata = nfsdp * nctx
    block_rows, width = inputs.shape
    depth = tp * width
    half_depth = depth // 2
    unit = depth // ndata
    tensor_index = lax.axis_index("tp").astype(jnp.int32)
    context_index = lax.axis_index("ctx").astype(jnp.int32)
    fsdp_index = lax.axis_index("fsdp").astype(jnp.int32)
    part_rows = block_rows // tp
    chunk_rows = block_rows // CHUNKS
    head_width = qkv_weight.shape[2]
    piece = head_width // nctx
    wide = 3 * piece

    square = nfsdp == 2 and nctx == 4 and unit % 128 == 0
    place = jnp.stack([tensor_index, context_index, fsdp_index])

    def shift(value, step):
        return lax.ppermute(value, "tp", [(i, (i + step) % tp) for i in range(tp)])

    def swap(value, step):
        return lax.ppermute(value, "ctx", [(i, i ^ step) for i in range(nctx)])

    core_index = context_index % 2
    groups = [list(range(0, ndata, 2)), list(range(1, ndata, 2))]
    def mate(value):
        return swap(value, 1)

    def send(here, near, far, *needed):
        far = swap(far, 2)
        return [here, swap(near, 1), far[0], swap(tie(far[1], *needed), 1)]

    def scatter_half(value, axis):
        return lax.psum_scatter(
            value, data, scatter_dimension=axis, tiled=True, axis_index_groups=groups
        )

    def scatter(value, axis):
        return lax.psum_scatter(value, data, scatter_dimension=axis, tiled=True)

    def cross(value):
        return lax.ppermute(value, "fsdp", [(i, i ^ 1) for i in range(nfsdp)])

    def square_once(parts):
        near, far, low, high = parts
        return total(near, cross(far)), total(low, swap(high, 2))

    def square_twice(first, second):
        first = first[0].astype(F32) + swap(first[1], 2).astype(F32)
        second = second[0].astype(F32) + cross(second[1]).astype(F32)
        return jnp.concatenate([first, second], axis=0)

    def total(left, right):
        return (left.astype(F32) + right.astype(F32)).astype(BF16)

    owners = [(tensor_index - step + tp) % tp for step in range(tp)]

    own_qkv = (
        qkv_weight.reshape(-1, 3, nctx, piece).transpose(0, 2, 1, 3).reshape(-1, 3 * head_width)
    )
    full_qkv = lax.all_gather(own_qkv, data, axis=0, tiled=True)
    own_feed = pack(gate_weight, up_weight, down_weight)
    feed_weights = lax.all_gather(own_feed, data, axis=0, tiled=True).reshape(ndata, 3 * unit, -1)

    validity, position, first_key, last_key = layout(lengths[0], fill_counts[0], block_rows)
    own_position = lax.dynamic_slice_in_dim(position, context_index * block_rows, block_rows, 0)
    tables = rotary_tables(own_position)
    bounds = jnp.stack([first_key, last_key])
    tile_first = first_key[::TILE_Q]
    tile_count = tile_first.shape[0]
    lows = jnp.where(validity[::TILE_Q], tile_first // TILE_K, tile_count * TILE_Q).astype(jnp.int32)
    key_block = jnp.arange(0, nctx * block_rows, TILE_K, dtype=jnp.int32) // block_rows
    ends = (
        key_block * block_rows
        + jnp.sum(
            jnp.where(
                key_block[:, None] == jnp.arange(nctx, dtype=jnp.int32)[None, :],
                fill_counts[0][None, :],
                0,
            ),
            axis=1,
        )
    ).astype(jnp.int32)

    flat_bias = qkv_bias.reshape(3, nctx, piece).transpose(1, 0, 2).reshape(1, -1)
    gain_one, bias_one = first_gain[None], first_bias[None]
    gain_two, bias_two = second_gain[None], second_bias[None]

    rings = [[inputs[c * chunk_rows : (c + 1) * chunk_rows]] for c in range(CHUNKS)]
    share = unit // CHUNKS
    for chunk in range(CHUNKS):
        carried = out_weight.T[chunk * share : (chunk + 1) * share]
        rings[chunk][0] = jnp.concatenate([rings[chunk][0], carried], axis=0)
    for chunk in range(CHUNKS):
        for _ in range(tp - 1):
            rings[chunk].append(shift(rings[chunk][-1], 1))
            if len(rings[chunk]) == 2:
                rings[chunk][-1] = tie(rings[chunk][-1], own_feed)
    all_low, full, low_half, *outgoing, stack = project(
        rings, place, gain_one, bias_one, full_qkv, flat_bias, tables, nctx, unit
    )
    full_out = lax.all_gather(stack, data, axis=1, tiled=True)

    cot = tie(cotangent, *[blocks[-1] for blocks in rings])
    cot_rings = [[cot[c * chunk_rows : (c + 1) * chunk_rows]] for c in range(CHUNKS)]
    for blocks in cot_rings:
        for _ in range(tp - 1):
            blocks.append(shift(blocks[-1], 1))
    pieces = send(*outgoing, *[blocks[max(tp - 2, 0)] for blocks in cot_rings])

    attended, outgoing, logs = attend(
        pieces,
        place[1:2],
        lows,
        ends,
        bounds,
        nctx,
        block_rows,
        feed_weights,
    )
    cot, cot_half = join(cot_rings, place, unit)
    arrived = lax.all_to_all(
        tie(outgoing, *[blocks[-1] for blocks in cot_rings]).reshape(nctx * tp, part_rows, piece),
        ("ctx", "tp"),
        split_axis=0,
        concat_axis=0,
        tiled=True,
    )
    returned, mixed, second_low = mix(
        arrived.reshape(nctx, tp, part_rows, piece),
        full_out,
        full,
        gain_two,
        bias_two,
        place,
        1,
    )

    arrived, held, partials, travelling = second_low, [], [], None
    for step in range(tp):
        coming = shift(arrived, 1) if step < tp - 1 else None
        needed = travelling if step == tp - 1 and step > 2 else []
        *held, first, second = feed(
            arrived, cot, mixed, feed_weights, step, tp, place, held, HALVES, *needed
        )
        partials.append([first, second])
        if step == 1 % tp:
            travelling = partials[step]
        elif step > 1:
            travelling = [
                total(shift(value, 1), kept) for value, kept in zip(travelling, partials[step])
            ]
        if step == 0 and coming is not None:
            coming = tie(coming, partials[0][0])
        arrived = coming
    all_second, all_gate, all_up, hidden, feedforward = held

    last = [shift(value, 1) for value in travelling]
    half_gate = blame(all_second, all_gate, *travelling)
    half_up = blame(all_second, all_up, *travelling)
    grad_heads, grad_mixed, mixed_low, gain_grad_two, shift_grad_two, mixed_half = turn(
        last,
        partials[0],
        mixed,
        cot,
        gain_two,
        full_out,
        place,
        nctx,
        tp,
        unit,
        half_gate,
        half_up,
    )
    grad_heads = lax.all_to_all(
        grad_heads.reshape(nctx * tp, part_rows, piece),
        ("ctx", "tp"),
        split_axis=0,
        concat_axis=0,
        tiled=True,
    ).reshape(nctx * block_rows, piece)

    total_gate = scatter(tie(half_gate, mixed_low), 0).astype(F32)
    half_out = blame(mixed_low, returned)
    total_out = scatter(tie(half_out, grad_heads), 0)
    total_up = scatter(tie(half_up, grad_heads), 0)

    feedforward = tie(feedforward, grad_heads)
    inner = hidden.shape[1]
    both = inner + 3 * head_width
    if square:
        parts = blame_halves(
            (cot, mate(cot_half)), (hidden, mate(hidden)), place, unit, total=both
        )
        half_down = parts[0]
    else:
        half_down = blame(hidden, cot)
        total_down = scatter(half_down, 1).astype(F32)
    layer_out = [pick(feedforward, owners[1 % tp])]
    for step in range(1, tp):
        kept = pick(feedforward, owners[(step + 1) % tp])
        if step == 2:
            layer_out.append(add(shift(layer_out[-1], 1), kept, half_down))
        else:
            layer_out.append(total(shift(layer_out[-1], 1), kept))

    grad_pieces = attend_back(
        pieces, place[1:2], lows, ends, bounds, logs, grad_heads, attended, nctx, block_rows, half_out
    )
    arrived = send(*grad_pieces, *layer_out[max(tp - 2, 0) : tp - 1])
    layer_out = layer_out[-1]
    low_halves = mate(low_half) if square else low_half
    needed = [layer_out, low_halves]
    *partial, all_grad, bias_grad, gain_grad, shift_grad = finish(
        arrived, place, tables, full, grad_mixed, gain_one, full_qkv, tp, *needed
    )
    if square:
        parts = blame_halves(
            (all_low, low_halves),
            (all_grad, mate(all_grad)),
            place,
            unit,
            held=parts,
            offset=inner,
            total=both,
        )
    else:
        parts = []
    def exchange(value, axis, steps, size):
        for step in steps:
            value = value + lax.ppermute(value, axis, [(i, i ^ step) for i in range(size)])
        return value

    def powers(first, size):
        return [1 << bit for bit in range(first, size.bit_length() - 1)]

    small = jnp.concatenate([gain_grad, shift_grad, gain_grad_two, shift_grad_two], axis=1)
    small = sum([shift(small, step) for step in range(1, tp)], small)
    small = jnp.concatenate([bias_grad, small], axis=1)
    travelling, ring_steps = partial[1 % tp], []
    once = square_once(parts) if square else ()
    needed = [[total_gate, total_out, small, *parts], [*once], []]
    for step in range(1, tp):
        travelling = add(
            shift(travelling, 1), partial[(step + 1) % tp], *(needed[step - 1] if step < 4 else [])
        )
        if step == 2:
            out_parts = jnp.swapaxes(
                tie(total_out, travelling).reshape(-1, tp, head_width), 0, 1
            )
            total_out = pick(out_parts, tensor_index).astype(F32)
            for ahead in range(1, tp):
                total_out = total_out + shift(pick(out_parts, (tensor_index + ahead) % tp), ahead).astype(F32)
            total_out = total_out.T
            total_up = tie(total_up, travelling).astype(F32)
            needed[2].extend([total_out, total_up])
        if step == 1:
            small = exchange(tie(small, travelling), "ctx", powers(0, nctx), nctx)
            needed[1].append(small)
        if step == 2:
            small = exchange(tie(small, travelling), "fsdp", powers(0, nfsdp), nfsdp)
            needed[2].append(small)
    grad_inputs = travelling
    if square:
        totals = square_twice(*once)
        total_down, total_qkv = totals[:, :inner].T, totals[:, inner:]
    else:
        total_qkv = scatter(blame(all_low, all_grad), 0).astype(F32)

    total_qkv = (
        total_qkv
        .reshape(-1, nctx, 3, piece)
        .transpose(0, 2, 1, 3)
        .reshape(-1, 3, head_width)
    )


    bias_total, small = small[:, : 3 * head_width], small[:, 3 * head_width :]
    bias_total = bias_total.reshape(nctx, 3, piece).transpose(1, 0, 2).reshape(3, head_width)
    small = small.reshape(4, depth)
    return (
        layer_out,
        grad_inputs,
        small[0],
        small[1],
        total_qkv,
        bias_total,
        total_out,
        small[2],
        small[3],
        total_gate,
        total_up,
        total_down,
    )


def solution(mesh):
    data = ("fsdp", "ctx")
    by_rows = P(data, "tp")
    by_columns = P("tp", data)
    qkv = P(data, None, "tp")
    return jax.shard_map(
        functools.partial(shards, mesh.shape["fsdp"], mesh.shape["ctx"], mesh.shape["tp"]),
        mesh=mesh,
        in_specs=(
            by_rows,
            by_rows,
            P(),
            P(),
            qkv,
            P(None, "tp"),
            by_columns,
            P(),
            P(),
            by_rows,
            by_rows,
            by_columns,
            P("fsdp", None),
            P("fsdp", None),
        ),
        out_specs=(
            by_rows,
            by_rows,
            P(),
            P(),
            qkv,
            P(None, "tp"),
            by_columns,
            P(),
            P(),
            by_rows,
            by_rows,
            by_columns,
        ),
        check_vma=False,
    )
```

profile of v0, /device:TPU:8, one launch (start us, length us, event | category | flops | bytes accessed | tf_op | source)
XLA Modules:
  0.0 785.8 jit_solution(590833821200510052)
XLA Ops:
  7.2 2.3 copy.131.refs_0_
  11.1 3.2 pack.1.refs_1_
  19.6 13.8 %collective-permute-done.refs_0_ = bf16[640,512]{1,0:T(8,128)(2,1)S(1)} collective-permute-done((bf16[640,512]{1,0:T(8,128)(2,1)S(1)}, bf16[640,512]{1,0:T(8,128)(2,1)S(1)}, u32[]{:S(2)}, u32[]{:S(2)}) %collective-permute-start) | collective-permute-done | bytes 655392 | tf_op jit(solution)/shard_map/ppermute | solution.py:1028
  35.8 11.6 %collective-permute-done.3.refs_0_ = bf16[640,512]{1,0:T(8,128)(2,1)S(1)} collective-permute-done((bf16[640,512]{1,0:T(8,128)(2,1)S(1)}, bf16[640,512]{1,0:T(8,128)(2,1)S(1)}, u32[]{:S(2)}, u32[]{:S(2)}) %collective-permute-start.3) | collective-permute-done | bytes 655392 | tf_op jit(solution)/shard_map/ppermute | solution.py:1028
  50.1 11.5 %collective-permute-done.1.refs_2_ = bf16[640,512]{1,0:T(8,128)(2,1)} collective-permute-done((bf16[640,512]{1,0:T(8,128)(2,1)}, bf16[640,512]{1,0:T(8,128)(2,1)}, u32[]{:S(2)}, u32[]{:S(2)}) %collective-permute-start.1) | collective-permute-done | bytes 655392 | tf_op jit(solution)/shard_map/ppermute | solution.py:1028
  63.2 12.4 %collective-permute-done.4.refs_6_ = bf16[640,512]{1,0:T(8,128)(2,1)S(1)} collective-permute-done((bf16[640,512]{1,0:T(8,128)(2,1)}, bf16[640,512]{1,0:T(8,128)(2,1)S(1)}, u32[]{:S(2)}, u32[]{:S(2)}) %collective-permute-start.4) | collective-permute-done | bytes 655392 | tf_op jit(solution)/shard_map/ppermute | solution.py:1028
  78.7 3.2 fusion.4
  81.8 7.7 collective-permute-done.2.refs_3_.refs_1_
  89.6 12.9 %collective-permute-done.5.refs_7_.refs_2_ = bf16[640,512]{1,0:T(8,128)(2,1)S(1)} collective-permute-done((bf16[640,512]{1,0:T(8,128)(2,1)S(1)}, bf16[640,512]{1,0:T(8,128)(2,1)S(1)}, u32[]{:S(2)}, u32[]{:S(2)}) %collective-permute-start.5) | collective-permute-done | bytes 655392 | tf_op jit(solution)/shard_map/ppermute | solution.py:1028
  103.3 21.5 %project.1 = (bf16[1024,2048]{1,0:T(8,128)(2,1)}, bf16[1024,2048]{1,0:T(8,128)(2,1)}, bf16[1024,1024]{1,0:T(8,128)(2,1)}, bf16[1024,384]{1,0:T(8,128)(2,1)}, bf1...) custom-call(s32[3]{0:T(128)} %pad_add_fusion.1.place, ...), custom_call_target="tpu_custom_call" | custom-call | flops 6000000000 | tf_op jit(solution)/shard_map/project/pallas_call | solution.py:225
  131.2 11.9 %collective-permute-done.10.refs_5_ = bf16[512,512]{1,0:T(8,128)(2,1)S(1)} collective-permute-done((bf16[512,512]{1,0:T(8,128)(2,1)S(1)}, bf16[512,512]{1,0:T(8,128)(2,1)S(1)}, u32[]{:S(2)}, u32[]{:S(2)}) %collective-permute-start.10) | collective-permute-done | bytes 524320 | tf_op jit(solution)/shard_map/ppermute | solution.py:1028
  144.4 9.9 %collective-permute-done.8.refs_1_ = bf16[512,512]{1,0:T(8,128)(2,1)S(1)} collective-permute-done((bf16[512,512]{1,0:T(8,128)(2,1)S(1)}, bf16[512,512]{1,0:T(8,128)(2,1)S(1)}, u32[]{:S(2)}, u32[]{:S(2)}) %collective-permute-start.8) | collective-permute-done | bytes 524320 | tf_op jit(solution)/shard_map/ppermute | solution.py:1028
  156.1 27.0 %collective-permute-done.7 = bf16[2,1024,384]{2,1,0:T(8,128)(2,1)} collective-permute-done((bf16[2,1024,384]{2,1,0:T(8,128)(2,1)}, bf16[2,1024,384]{2,1,0:T(8,128)(2,1)}, u32[]{:S(2)}, u32[]{:S(2)}) %collective-permute-start.7) | collective-permute-done | bytes 1572896 | tf_op jit(solution)/shard_map/ppermute | solution.py:1031
  183.1 2.9 slice_bitcast_fusion.2
  191.7 40.6 %attend.1 = (bf16[4096,128]{1,0:T(8,128)(2,1)}, bf16[4096,128]{1,0:T(8,128)(2,1)}, f32[2,4096]{1,0:T(2,128)}) custom-call(s32[1]{0:T(128)} %bitcast.1.place, s32[8]{0:T(128)} %fusion.27.lows, s32[8]{0:T(128)} %multiply_add_fusion.ends, s32[2,4096]{1,0:T(2,128)} %pad_add_fusion.bounds, bf16[1024,384]{1,0:T(8,128)(2,1)} %get-tuple-element.79.refs_0_, ...), custom_call_target="tpu_custom_call" | custom-call | flops 20000000000 | tf_op jit(solution)/shard_map/attend/pallas_call | solution.py:360
  233.4 4.2 all-to-all-start
  237.6 24.2 %all-to-all-done = bf16[16,256,128]{2,1,0:T(8,128)(2,1)S(1)} async-done(((bf16[16,256,128]{2,1,0:T(8,128)(2,1)}), bf16[16,256,128]{2,1,0:T(8,128)(2,1)S(1)}, u32[]{:S(2)}, u32[]{:S(2)}) %all-to-all-start) | async-done | bytes 1048608 | tf_op jit(solution)/shard_map/all_to_all | solution.py:1131
  262.8 9.5 %mix.1 = (bf16[256,2048]{1,0:T(8,128)(2,1)}, f32[256,2048]{1,0:T(8,128)}, bf16[256,2048]{1,0:T(8,128)(2,1)}) custom-call(s32[3]{0:T(128)} %pad_add_fusion.1.place, bf16[4,4,256,128]{3,2,1,0:T(8,128)(2,1)} %bitcast.127, bf16[4,2048,512]{2,1,0:T(8,128)(2,1)} %all-gather.8.cloned.1.call-done.weight.refs_7_, ...), custom_call_target="tpu_custom_call" | custom-call | flops 5000000000 | tf_op jit(solution)/shard_map/mix/pallas_call | solution.py:533
  272.9 6.0 join.1
  278.8 17.7 %feed.4 = (bf16[1024,2048]{1,0:T(8,128)(2,1)}, bf16[1024,1408]{1,0:T(8,128)(2,1)}, bf16[1024,1408]{1,0:T(8,128)(2,1)}, bf16[1024,1408]{1,0:T(8,128)(2,1)}, bf16[...) custom-call(s32[3]{0:T(128)} %pad_add_fusion.1.place, ...), custom_call_target="tpu_custom_call" | custom-call | flops 10000000000 | tf_op jit(solution)/shard_map/feed/pallas_call | solution.py:623
  300.1 17.7 %feed.5 = (bf16[1024,2048]{1,0:T(8,128)(2,1)}, bf16[1024,1408]{1,0:T(8,128)(2,1)}, bf16[1024,1408]{1,0:T(8,128)(2,1)}, bf16[1024,1408]{1,0:T(8,128)(2,1)}, bf16[...) custom-call(s32[3]{0:T(128)} %pad_add_fusion.1.place, ...), custom_call_target="tpu_custom_call", output_to_operand_aliasing={{0}: (5, {}), {1}: (6, {}), {2}: (7, {}), {3}: (8, {}), {4}... | custom-call | flops 10000000000 | tf_op jit(solution)/shard_map/feed/pallas_call | solution.py:623
  317.8 3.1 collective-permute-start.19
  320.9 3.1 collective-permute-start.18
  323.9 3.6 collective-permute-done.16.low
  328.5 17.7 %feed.6 = (bf16[1024,2048]{1,0:T(8,128)(2,1)}, bf16[1024,1408]{1,0:T(8,128)(2,1)}, bf16[1024,1408]{1,0:T(8,128)(2,1)}, bf16[1024,1408]{1,0:T(8,128)(2,1)}, bf16[...) custom-call(s32[3]{0:T(128)} %pad_add_fusion.1.place, ...), custom_call_target="tpu_custom_call", output_to_operand_aliasing={{0}: (5, {}), {1}: (6, {}), {2}: (7, {}), {3}: (8, {}), {4}... | custom-call | flops 10000000000 | tf_op jit(solution)/shard_map/feed/pallas_call | solution.py:623
  351.2 3.8 collective-permute-start.20
  354.9 17.5 %collective-permute-done.17.low = bf16[256,2048]{1,0:T(8,128)(2,1)S(1)} collective-permute-done((bf16[256,2048]{1,0:T(8,128)(2,1)S(1)}, bf16[256,2048]{1,0:T(8,128)(2,1)S(1)}, u32[]{:S(2)}, u32[]{:S(2)}) %collective-permute-start.17) | collective-permute-done | bytes 1048608 | tf_op jit(solution)/shard_map/ppermute | solution.py:1028
  373.4 17.8 %feed.7 = (bf16[1024,2048]{1,0:T(8,128)(2,1)}, bf16[1024,1408]{1,0:T(8,128)(2,1)}, bf16[1024,1408]{1,0:T(8,128)(2,1)}, bf16[1024,1408]{1,0:T(8,128)(2,1)}, bf16[...) custom-call(s32[3]{0:T(128)} %pad_add_fusion.1.place, ...), custom_call_target="tpu_custom_call", output_to_operand_aliasing={{0}: (5, {}), {1}: (6, {}), {2}: (7, {}), {3}: (8, {}), {4}... | custom-call | flops 10000000000 | tf_op jit(solution)/shard_map/feed/pallas_call | solution.py:623
  394.2 2.3 collective-permute-start.21
  396.5 10.7 %blame.4.refs_9_.refs_0_ = bf16[2048,1408]{1,0:T(8,128)(2,1)} custom-call(bf16[1024,2048]{1,0:T(8,128)(2,1)} %get-tuple-element.112.left, bf16[1024,1408]{1,0:T(8,128)(2,1)} %get-tuple-element.114.right, bf16[128,2048]{1,0:T(8,128)(2,1)} %copy-done.36, bf16[128,2048]{1,0:T(8,128)(2,1)} %copy-done.35), custom_call_target="tpu_custom_call" | custom-call | flops 6000000000 | tf_op jit(solution)/shard_map/blame/pallas_call | solution.py:726
  407.2 10.6 %blame.3.refs_8_.refs_0_ = bf16[2048,1408]{1,0:T(8,128)(2,1)} custom-call(bf16[1024,2048]{1,0:T(8,128)(2,1)} %get-tuple-element.112.left, bf16[1024,1408]{1,0:T(8,128)(2,1)} %get-tuple-element.113.right, bf16[128,2048]{1,0:T(8,128)(2,1)} %copy-done.36, bf16[128,2048]{1,0:T(8,128)(2,1)} %copy-done.35), custom_call_target="tpu_custom_call" | custom-call | flops 6000000000 | tf_op jit(solution)/shard_map/blame/pallas_call | solution.py:726
  418.8 11.7 %turn.1 = (bf16[4,4,256,128]{3,2,1,0:T(8,128)(2,1)}, f32[256,2048]{1,0:T(8,128)}, bf16[256,2048]{1,0:T(8,128)(2,1)}, f32[1,2048]{1,0:T(1,128)}, f32[1,2048]{1,0:T(1,128)}, /*index=5*/bf16[256,1024]{1,0:T(8,128)(2,1)}) custom-call(s32[3]{0:T(128)} %pad_add_fusion.1.place, bf16[128,2048]{1,0:T(8,128)(2,1)} %copy-done.34, bf16[128,2048]{1,0:T(8,128)(2,1)} %copy-done.33, ...), custom_call_target="tpu_custom_call" | custom-call | flops 6000000000 | tf_op jit(solution)/shard_map/turn/pallas_call | solution.py:798
  430.5 8.0 %all-to-all-start.1 = ((bf16[16,256,128]{2,1,0:T(8,128)(2,1)}), bf16[16,256,128]{2,1,0:T(8,128)(2,1)S(1)}, u32[]{:S(2)}, u32[]{:S(2)}) async-start(bf16[16,256,128]{2,1,0:T(8,128)(2,1)} %bitcast.33), calls=%async_computation.1 | async-start | bytes 2097152 | tf_op jit(solution)/shard_map/all_to_all | solution.py:1184
  438.5 6.7 blame.5.refs_6_
  445.2 8.9 %copy.117.refs_0_ = bf16[2048,2048]{1,0:T(8,128)(2,1)} copy(bf16[2048,2048]{1,0:T(8,128)(2,1)} %blame.5.refs_6_) | data formatting | bytes 16777216
  454.1 8.7 %all-to-all-done.1 = bf16[16,256,128]{2,1,0:T(8,128)(2,1)S(1)} async-done(((bf16[16,256,128]{2,1,0:T(8,128)(2,1)}), bf16[16,256,128]{2,1,0:T(8,128)(2,1)S(1)}, u32[]{:S(2)}, u32[]{:S(2)}) %all-to-all-start.1) | async-done | bytes 1048608 | tf_op jit(solution)/shard_map/all_to_all | solution.py:1184
  465.5 2.7 dynamic-slice_bitcast_fusion
  469.2 58.5 %attend_back.1 = (bf16[1024,384]{1,0:T(8,128)(2,1)}, bf16[1024,384]{1,0:T(8,128)(2,1)}, bf16[2,1024,384]{2,1,0:T(8,128)(2,1)}) custom-call(s32[1]{0:T(128)} %bitcast.1.place, s32[8]{0:T(128)} %fusion.27.lows, s32[8]{0:T(128)} %multiply_add_fusion.ends, s32[2,4096]{1,0:T(2,128)} %pad_add_fusion.bounds, f32[2,4096]{1,0:T(2,128)} %get-tuple-element.119.logs, ...), custom_call_target="tpu_custom_call" | custom-call | flops 24999999488 | tf_op jit(solution)/shard_map/attend_back/pallas_call | solution.py:476
  530.3 2.7 collective-permute-start.25
  533.7 13.2 %blame_halves.2 = (bf16[2,128,2944]{2,1,0:T(8,128)(2,1)}, bf16[2,128,2944]{2,1,0:T(8,128)(2,1)}, bf16[2,128,2944]{2,1,0:T(8,128)(2,1)}, bf16[2,128,2944]{2,1,0:T(8,128)(2,1)}) custom-call(s32[4]{0:T(128)} %pad_add_fusion.2.place, bf16[4,1024,512]{2,1,0:T(8,128)(2,1)} %get-tuple-element.86.cot.refs_5_.left_here, ...), custom_call_target="tpu_custom_call" | custom-call | flops 6000000000 | tf_op jit(solution)/shard_map/blame_halves/pallas_call | solution.py:698
  546.9 8.7 %collective-permute-done.25.left = bf16[1024,512]{1,0:T(8,128)(2,1)S(1)} collective-permute-done((bf16[1024,512]{1,0:T(8,128)(2,1)S(1)}, bf16[1024,512]{1,0:T(8,128)(2,1)S(1)}, u32[]{:S(2)}, u32[]{:S(2)}) %collective-permute-start.25) | collective-permute-done | bytes 1048608 | tf_op jit(solution)/shard_map/ppermute | solution.py:1028
  556.6 2.5 ring_add.4.refs_1_
  559.1 2.5 collective-permute-start.28
  561.6 20.4 %collective-permute-done.30 = bf16[2,1024,384]{2,1,0:T(8,128)(2,1)S(1)} collective-permute-done((bf16[2,1024,384]{2,1,0:T(8,128)(2,1)}, bf16[2,1024,384]{2,1,0:T(8,128)(2,1)S(1)}, u32[]{:S(2)}, u32[]{:S(2)}) %collective-permute-start.30) | collective-permute-done | bytes 1572896 | tf_op jit(solution)/shard_map/ppermute | solution.py:1031
  584.9 2.5 fusion.refs_11_
  588.5 19.7 %finish.1 = (bf16[1024,512]{1,0:T(8,128)(2,1)}, bf16[1024,512]{1,0:T(8,128)(2,1)}, bf16[1024,512]{1,0:T(8,128)(2,1)}, bf16[1024,512]{1,0:T(8,128)(2,1)}, bf16[10...) custom-call(s32[3]{0:T(128)} %pad_add_fusion.1.place, ...), custom_call_target="tpu_custom_call" | custom-call | flops 7000000000 | tf_op jit(solution)/shard_map/finish/pallas_call | solution.py:910
  610.4 4.5 collective-permute-start.35
  614.9 2.0 collective-permute-start.33
  618.6 14.4 %blame_halves.3 = (bf16[2,128,2944]{2,1,0:T(8,128)(2,1)}, bf16[2,128,2944]{2,1,0:T(8,128)(2,1)}, bf16[2,128,2944]{2,1,0:T(8,128)(2,1)}, bf16[2,128,2944]{2,1,0:T(8,128)(2,1)}) custom-call(s32[4]{0:T(128)} %pad_add_fusion.2.place, ...), custom_call_target="tpu_custom_call", output_to_operand_aliasing={{0}: (5, {}), {1}: (6, {}), {2}: (7, {}), {3}: (8, {})} | custom-call | flops 6000000000 | tf_op jit(solution)/shard_map/blame_halves/pallas_call | solution.py:698
  635.7 2.3 convert_element_type.157.refs_0_
  638.0 52.0 %collective-permute-done.40 = bf16[2,128,2944]{2,1,0:T(8,128)(2,1)S(1)} collective-permute-done((bf16[2,128,2944]{2,1,0:T(8,128)(2,1)}, bf16[2,128,2944]{2,1,0:T(8,128)(2,1)S(1)}, u32[]{:S(2)}, u32[]{:S(2)}) %collective-permute-start.40) | collective-permute-done | bytes 1507360 | tf_op jit(solution)/shard_map/ppermute | solution.py:1031
  697.4 2.4 ring_add.5.refs_1_
  701.3 10.7 %collective-permute-done.49 = bf16[128,2944]{1,0:T(8,128)(2,1)} collective-permute-done((bf16[128,2944]{1,0:T(8,128)(2,1)}, bf16[128,2944]{1,0:T(8,128)(2,1)}, u32[]{:S(2)}, u32[]{:S(2)}) %collective-permute-start.49) | collective-permute-done | bytes 753696 | tf_op jit(solution)/shard_map/ppermute | solution.py:1051
  712.0 2.4 convert_add_fusion.2
  718.1 2.1 collective-permute-done.42
  720.9 3.1 collective-permute-done.38.left
  724.0 2.4 ring_add.6.refs_1_
  728.2 2.9 copy.92
  739.3 2.3 convert_element_type.169.refs_1_
  745.0 2.0 collective-permute-start.46
  748.3 19.9 %collective-permute-done.44 = bf16[256,512]{0,1:T(8,128)(2,1)S(1)} collective-permute-done((bf16[256,512]{0,1:T(8,128)(2,1)S(1)}, bf16[256,512]{0,1:T(8,128)(2,1)S(1)}, u32[]{:S(2)}, u32[]{:S(2)}) %collective-permute-start.44) | collective-permute-done | bytes 262176 | tf_op jit(solution)/shard_map/ppermute | solution.py:1028
  768.2 2.8 collective-permute-done.45
  771.0 4.4 collective-permute-done.46
  776.3 2.4 ring_add.7
  (278 shorter events, 96.7 us)
Async XLA Ops:
  7.2 95.3 %all-gather.4.cloned.1.call-start = ((), (), s32[]{:S(2)}) async-start(), calls=%async_computation.5 | async-start | bytes 7077888 | tf_op jit(solution)/shard_map/all_gather | solution.py:1070
  11.1 180.7 %all-gather.6.cloned.1.call-start = ((), (), s32[]{:S(2)}) async-start(), calls=%async_computation.6 | async-start | bytes 19464192 | tf_op jit(solution)/shard_map/all_gather | solution.py:1072
  14.3 223.3 %all-gather.8.cloned.1.call-start = ((), (), s32[]{:S(2)}) async-start(), calls=%async_computation.7 | async-start | bytes 9437184 | tf_op jit(solution)/shard_map/all_gather | solution.py:1111
  15.7 17.7 %collective-permute-start = (bf16[640,512]{1,0:T(8,128)(2,1)S(1)}, bf16[640,512]{1,0:T(8,128)(2,1)S(1)}, u32[]{:S(2)}, u32[]{:S(2)}) collective-permute-start(bf16[640,512]{1,0:T(8,128)(2,1)S(1)} %pad_maximum_fusion.1.refs_0_), channel_id=1, source_target_pairs={{0,1},{1,2},{2,3},{3,0},{4,5},{5,6},{6,7},{7,4},{8,9},{9,10},{10,1... | collective-permute-start | bytes 1966088 | tf_op jit(solution)/shard_map/ppermute | solution.py:1028
  17.4 30.0 %collective-permute-start.3 = (bf16[640,512]{1,0:T(8,128)(2,1)S(1)}, bf16[640,512]{1,0:T(8,128)(2,1)S(1)}, u32[]{:S(2)}, u32[]{:S(2)}) collective-permute-start(bf16[640,512]{1,0:T(8,128)(2,1)S(1)} %pad_maximum_fusion.2.refs_4_), channel_id=1, source_target_pairs={{0,1},{1,2},{2,3},{3,0},{4,5},{5,6},{6,7},{7,4},{8,9},{9,10},{10,1... | collective-permute-start | bytes 1966088 | tf_op jit(solution)/shard_map/ppermute | solution.py:1028
  34.3 43.5 %copy-start.39 = (f32[3,512]{1,0:T(4,128)S(1)}, f32[3,512]{1,0:T(4,128)}, u32[]{:S(2)}) copy-start(f32[3,512]{1,0:T(4,128)} %param.19) | copy-start | bytes 18436
  34.3 27.3 %collective-permute-start.1 = (bf16[640,512]{1,0:T(8,128)(2,1)}, bf16[640,512]{1,0:T(8,128)(2,1)}, u32[]{:S(2)}, u32[]{:S(2)}) collective-permute-start(bf16[640,512]{1,0:T(8,128)(2,1)} %tie.15.refs_1_), channel_id=1, source_target_pairs={{0,1},{1,2},{2,3},{3,0},{4,5},{5,6},{6,7},{7,4},{8,9},{9,10},{10,1... | collective-permute-start | bytes 1966088 | tf_op jit(solution)/shard_map/ppermute | solution.py:1028
  48.3 27.2 %collective-permute-start.4 = (bf16[640,512]{1,0:T(8,128)(2,1)}, bf16[640,512]{1,0:T(8,128)(2,1)S(1)}, u32[]{:S(2)}, u32[]{:S(2)}) collective-permute-start(bf16[640,512]{1,0:T(8,128)(2,1)} %tie.16.refs_5_), channel_id=1, source_target_pairs={{0,1},{1,2},{2,3},{3,0},{4,5},{5,6},{6,7},{7,4},{8,9},{9,10},{10,1... | collective-permute-start | bytes 1966088 | tf_op jit(solution)/shard_map/ppermute | solution.py:1028
  61.6 28.0 %collective-permute-start.2 = (bf16[640,512]{1,0:T(8,128)(2,1)}, bf16[640,512]{1,0:T(8,128)(2,1)S(1)}, u32[]{:S(2)}, u32[]{:S(2)}) collective-permute-start(bf16[640,512]{1,0:T(8,128)(2,1)} %collective-permute-done.1.refs_2_), channel_id=1, source_target_pairs={{0,1},{1,2},{2,3},{3,0},{4,5},{5,6},{6,7},{7,4},{8,9},{9,10},{10,1... | collective-permute-start | bytes 1966088 | tf_op jit(solution)/shard_map/ppermute | solution.py:1028
  75.5 26.9 %collective-permute-start.5 = (bf16[640,512]{1,0:T(8,128)(2,1)S(1)}, bf16[640,512]{1,0:T(8,128)(2,1)S(1)}, u32[]{:S(2)}, u32[]{:S(2)}) collective-permute-start(bf16[640,512]{1,0:T(8,128)(2,1)S(1)} %collective-permute-done.4.refs_6_), channel_id=1, source_target_pairs={{0,1},{1,2},{2,3},{3,0},{4,5},{5,6},{6,7},{7,4},{8,9},{9,10},{10,1... | collective-permute-start | bytes 1966088 | tf_op jit(solution)/shard_map/ppermute | solution.py:1028
  124.9 58.2 %collective-permute-start.7 = (bf16[2,1024,384]{2,1,0:T(8,128)(2,1)}, bf16[2,1024,384]{2,1,0:T(8,128)(2,1)}, u32[]{:S(2)}, u32[]{:S(2)}) collective-permute-start(bf16[2,1024,384]{2,1,0:T(8,128)(2,1)} %get-tuple-element.81), channel_id=1, source_target_pairs={{0,8},{4,12},{8,0},{12,4},{1,9},{5,13},{9,1},{13,5},{2,10},{6,14},... | collective-permute-start | bytes 4718600 | tf_op jit(solution)/shard_map/ppermute | solution.py:1031
  127.8 59.2 %copy-start.12 = (bf16[512,512]{1,0:T(8,128)(2,1)}, bf16[512,512]{1,0:T(8,128)(2,1)S(1)}, u32[]{:S(2)}) copy-start(bf16[512,512]{1,0:T(8,128)(2,1)S(1)} %get-tuple-element.211.refs_4_) | copy-start | bytes 1572868
  127.8 59.2 %copy-start.13 = (bf16[512,512]{1,0:T(8,128)(2,1)}, bf16[512,512]{1,0:T(8,128)(2,1)S(1)}, u32[]{:S(2)}) copy-start(bf16[512,512]{1,0:T(8,128)(2,1)S(1)} %get-tuple-element.212.refs_0_) | copy-start | bytes 1572868
  127.8 15.3 %collective-permute-start.10 = (bf16[512,512]{1,0:T(8,128)(2,1)S(1)}, bf16[512,512]{1,0:T(8,128)(2,1)S(1)}, u32[]{:S(2)}, u32[]{:S(2)}) collective-permute-start(bf16[512,512]{1,0:T(8,128)(2,1)S(1)} %get-tuple-element.211.refs_4_), channel_id=1, source_target_pairs={{0,1},{1,2},{2,3},{3,0},{4,5},{5,6},{6,7},{7,4},{8,9},{9,10},{10,1... | collective-permute-start | bytes 1572872 | tf_op jit(solution)/shard_map/ppermute | solution.py:1028
  129.5 24.8 %collective-permute-start.8 = (bf16[512,512]{1,0:T(8,128)(2,1)S(1)}, bf16[512,512]{1,0:T(8,128)(2,1)S(1)}, u32[]{:S(2)}, u32[]{:S(2)}) collective-permute-start(bf16[512,512]{1,0:T(8,128)(2,1)S(1)} %get-tuple-element.212.refs_0_), channel_id=1, source_target_pairs={{0,1},{1,2},{2,3},{3,0},{4,5},{5,6},{6,7},{7,4},{8,9},{9,10},{10,1... | collective-permute-start | bytes 1572872 | tf_op jit(solution)/shard_map/ppermute | solution.py:1028
  143.1 43.9 %copy-start.31 = (bf16[512,512]{1,0:T(8,128)(2,1)}, bf16[512,512]{1,0:T(8,128)(2,1)S(1)}, u32[]{:S(2)}) copy-start(bf16[512,512]{1,0:T(8,128)(2,1)S(1)} %collective-permute-done.10.refs_5_) | copy-start | bytes 1572868
  143.1 42.9 %collective-permute-start.11 = (bf16[512,512]{1,0:T(8,128)(2,1)S(1)}, bf16[512,512]{1,0:T(8,128)(2,1)S(1)}, u32[]{:S(2)}, u32[]{:S(2)}) collective-permute-start(bf16[512,512]{1,0:T(8,128)(2,1)S(1)} %collective-permute-done.10.refs_5_), channel_id=1, source_target_pairs={{0,1},{1,2},{2,3},{3,0},{4,5},{5,6},{6,7},{7,4},{8,9},{9,10},{10,1... | collective-permute-start | bytes 1572872 | tf_op jit(solution)/shard_map/ppermute | solution.py:1028
  154.3 32.7 %copy-start.32 = (bf16[512,512]{1,0:T(8,128)(2,1)}, bf16[512,512]{1,0:T(8,128)(2,1)S(1)}, u32[]{:S(2)}) copy-start(bf16[512,512]{1,0:T(8,128)(2,1)S(1)} %collective-permute-done.8.refs_1_) | copy-start | bytes 1572868
  154.3 31.7 %collective-permute-start.9 = (bf16[512,512]{1,0:T(8,128)(2,1)S(1)}, bf16[512,512]{1,0:T(8,128)(2,1)S(1)}, u32[]{:S(2)}, u32[]{:S(2)}) collective-permute-start(bf16[512,512]{1,0:T(8,128)(2,1)S(1)} %collective-permute-done.8.refs_1_), channel_id=1, source_target_pairs={{0,1},{1,2},{2,3},{3,0},{4,5},{5,6},{6,7},{7,4},{8,9},{9,10},{10,1... | collective-permute-start | bytes 1572872 | tf_op jit(solution)/shard_map/ppermute | solution.py:1028
  156.1 35.6 %collective-permute-start.6 = (bf16[1024,384]{1,0:T(8,128)(2,1)}, bf16[1024,384]{1,0:T(8,128)(2,1)}, u32[]{:S(2)}, u32[]{:S(2)}) collective-permute-start(bf16[1024,384]{1,0:T(8,128)(2,1)} %get-tuple-element.80), channel_id=1, source_target_pairs={{0,4},{4,0},{8,12},{12,8},{1,5},{5,1},{9,13},{13,9},{2,6},{6,2},{1... | collective-permute-start | bytes 2359304 | tf_op jit(solution)/shard_map/ppermute | solution.py:1031
  187.0 4.8 collective-permute-start.12
  188.8 43.6 %collective-permute-start.13 = (bf16[512,512]{1,0:T(8,128)(2,1)}, bf16[512,512]{1,0:T(8,128)(2,1)S(1)}, u32[]{:S(2)}, u32[]{:S(2)}) collective-permute-start(bf16[512,512]{1,0:T(8,128)(2,1)} %copy-done.11), channel_id=1, source_target_pairs={{0,1},{1,2},{2,3},{3,0},{4,5},{5,6},{6,7},{7,4},{8,9},{9,10},{10,1... | collective-permute-start | bytes 1572872 | tf_op jit(solution)/shard_map/ppermute | solution.py:1028
  190.2 42.1 %collective-permute-start.14 = (bf16[512,512]{1,0:T(8,128)(2,1)}, bf16[512,512]{1,0:T(8,128)(2,1)S(1)}, u32[]{:S(2)}, u32[]{:S(2)}) collective-permute-start(bf16[512,512]{1,0:T(8,128)(2,1)} %copy-done.10), channel_id=1, source_target_pairs={{0,1},{1,2},{2,3},{3,0},{4,5},{5,6},{6,7},{7,4},{8,9},{9,10},{10,1... | collective-permute-start | bytes 1572872 | tf_op jit(solution)/shard_map/ppermute | solution.py:1028
  233.4 28.4 %all-to-all-start = ((bf16[16,256,128]{2,1,0:T(8,128)(2,1)}), bf16[16,256,128]{2,1,0:T(8,128)(2,1)S(1)}, u32[]{:S(2)}, u32[]{:S(2)}) async-start(bf16[16,256,128]{2,1,0:T(8,128)(2,1)} %bitcast.122), calls=%async_computation | async-start | bytes 2097152 | tf_op jit(solution)/shard_map/all_to_all | solution.py:1131
  237.5 398.2 %reduce-scatter.4.cloned.1.call-start = ((), (), s32[]{:S(2)}) async-start(), calls=%async_computation.8 | async-start | bytes 6488064 | tf_op jit(solution)/shard_map/reduce_scatter | solution.py:1048
  272.3 26.0 %collective-permute-start.15 = (bf16[256,2048]{1,0:T(8,128)(2,1)}, bf16[256,2048]{1,0:T(8,128)(2,1)S(1)}, u32[]{:S(2)}, u32[]{:S(2)}) collective-permute-start(bf16[256,2048]{1,0:T(8,128)(2,1)} %get-tuple-element.85.low), channel_id=1, source_target_pairs={{0,1},{1,2},{2,3},{3,0},{4,5},{5,6},{6,7},{7,4},{8,9},{9,10},{10,1... | collective-permute-start | bytes 3145736 | tf_op jit(solution)/shard_map/ppermute | solution.py:1028
  299.3 28.2 %collective-permute-start.16 = (bf16[256,2048]{1,0:T(8,128)(2,1)}, bf16[256,2048]{1,0:T(8,128)(2,1)S(1)}, u32[]{:S(2)}, u32[]{:S(2)}) collective-permute-start(bf16[256,2048]{1,0:T(8,128)(2,1)} %tie.20.low), channel_id=1, source_target_pairs={{0,1},{1,2},{2,3},{3,0},{4,5},{5,6},{6,7},{7,4},{8,9},{9,10},{10,1... | collective-permute-start | bytes 3145736 | tf_op jit(solution)/shard_map/ppermute | solution.py:1028
  317.8 28.4 %collective-permute-start.19 = (bf16[128,2048]{1,0:T(8,128)(2,1)}, bf16[128,2048]{1,0:T(8,128)(2,1)S(1)}, u32[]{:S(2)}, u32[]{:S(2)}) collective-permute-start(bf16[128,2048]{1,0:T(8,128)(2,1)} %get-tuple-element.106), channel_id=1, source_target_pairs={{0,1},{1,2},{2,3},{3,0},{4,5},{5,6},{6,7},{7,4},{8,9},{9,10},{10,1... | collective-permute-start | bytes 1572872 | tf_op jit(solution)/shard_map/ppermute | solution.py:1028
  320.9 29.1 %collective-permute-start.18 = (bf16[128,2048]{1,0:T(8,128)(2,1)}, bf16[128,2048]{1,0:T(8,128)(2,1)S(1)}, u32[]{:S(2)}, u32[]{:S(2)}) collective-permute-start(bf16[128,2048]{1,0:T(8,128)(2,1)} %get-tuple-element.104), channel_id=1, source_target_pairs={{0,1},{1,2},{2,3},{3,0},{4,5},{5,6},{6,7},{7,4},{8,9},{9,10},{10,1... | collective-permute-start | bytes 1572872 | tf_op jit(solution)/shard_map/ppermute | solution.py:1028
  327.5 44.9 %collective-permute-start.17 = (bf16[256,2048]{1,0:T(8,128)(2,1)S(1)}, bf16[256,2048]{1,0:T(8,128)(2,1)S(1)}, u32[]{:S(2)}, u32[]{:S(2)}) collective-permute-start(bf16[256,2048]{1,0:T(8,128)(2,1)S(1)} %collective-permute-done.16.low), channel_id=1, source_target_pairs={{0,1},{1,2},{2,3},{3,0},{4,5},{5,6},{6,7},{7,4},{8,9},{9,10},{10,1... | collective-permute-start | bytes 3145736 | tf_op jit(solution)/shard_map/ppermute | solution.py:1028
  347.4 43.8 %collective-permute-start.22 = (bf16[128,2048]{1,0:T(8,128)(2,1)S(1)}, bf16[128,2048]{1,0:T(8,128)(2,1)S(1)}, u32[]{:S(2)}, u32[]{:S(2)}) collective-permute-start(bf16[128,2048]{1,0:T(8,128)(2,1)S(1)} %add_convert_fusion.4.refs_6_), channel_id=1, source_target_pairs={{0,1},{1,2},{2,3},{3,0},{4,5},{5,6},{6,7},{7,4},{8,9},{9,10},{10,1... | collective-permute-start | bytes 1572872 | tf_op jit(solution)/shard_map/ppermute | solution.py:1028
  351.2 41.9 %collective-permute-start.20 = (bf16[128,2048]{1,0:T(8,128)(2,1)S(1)}, bf16[128,2048]{1,0:T(8,128)(2,1)S(1)}, u32[]{:S(2)}, u32[]{:S(2)}) collective-permute-start(bf16[128,2048]{1,0:T(8,128)(2,1)S(1)} %add_convert_fusion.5.refs_5_), channel_id=1, source_target_pairs={{0,1},{1,2},{2,3},{3,0},{4,5},{5,6},{6,7},{7,4},{8,9},{9,10},{10,1... | collective-permute-start | bytes 1572872 | tf_op jit(solution)/shard_map/ppermute | solution.py:1028
  392.4 25.4 %collective-permute-start.23 = (bf16[128,2048]{1,0:T(8,128)(2,1)S(1)}, bf16[128,2048]{1,0:T(8,128)(2,1)S(1)}, u32[]{:S(2)}, u32[]{:S(2)}) collective-permute-start(bf16[128,2048]{1,0:T(8,128)(2,1)S(1)} %add_convert_fusion.2.refs_1_), channel_id=1, source_target_pairs={{0,1},{1,2},{2,3},{3,0},{4,5},{5,6},{6,7},{7,4},{8,9},{9,10},{10,1... | collective-permute-start | bytes 1572872 | tf_op jit(solution)/shard_map/ppermute | solution.py:1028
  394.2 23.6 %collective-permute-start.21 = (bf16[128,2048]{1,0:T(8,128)(2,1)S(1)}, bf16[128,2048]{1,0:T(8,128)(2,1)S(1)}, u32[]{:S(2)}, u32[]{:S(2)}) collective-permute-start(bf16[128,2048]{1,0:T(8,128)(2,1)S(1)} %add_convert_fusion.3.refs_0_), channel_id=1, source_target_pairs={{0,1},{1,2},{2,3},{3,0},{4,5},{5,6},{6,7},{7,4},{8,9},{9,10},{10,1... | collective-permute-start | bytes 1572872 | tf_op jit(solution)/shard_map/ppermute | solution.py:1028
  430.5 32.3 %all-to-all-start.1 = ((bf16[16,256,128]{2,1,0:T(8,128)(2,1)}), bf16[16,256,128]{2,1,0:T(8,128)(2,1)S(1)}, u32[]{:S(2)}, u32[]{:S(2)}) async-start(bf16[16,256,128]{2,1,0:T(8,128)(2,1)} %bitcast.33), calls=%async_computation.1 | async-start | bytes 2097152 | tf_op jit(solution)/shard_map/all_to_all | solution.py:1184
  438.5 258.9 %reduce-scatter.6.cloned.1.call-start = ((), (), s32[]{:S(2)}) async-start(), calls=%async_computation.9 | async-start | bytes 9437184 | tf_op jit(solution)/shard_map/reduce_scatter | solution.py:1048
  463.7 275.5 %reduce-scatter.8.cloned.1.call-start = ((), (), s32[]{:S(2)}) async-start(), calls=%async_computation.10 | async-start | bytes 6488064 | tf_op jit(solution)/shard_map/reduce_scatter | solution.py:1048
  463.8 69.9 %collective-permute-start.26 = (bf16[1024,1024]{1,0:T(8,128)(2,1)}, bf16[1024,1024]{1,0:T(8,128)(2,1)}, u32[]{:S(2)}, u32[]{:S(2)}) collective-permute-start(bf16[1024,1024]{1,0:T(8,128)(2,1)} %get-tuple-element.116), channel_id=1, source_target_pairs={{0,4},{4,0},{8,12},{12,8},{1,5},{5,1},{9,13},{13,9},{2,6},{6,2},{1... | collective-permute-start | bytes 6291464 | tf_op jit(solution)/shard_map/ppermute | solution.py:1031
  465.5 68.2 %collective-permute-start.27 = (bf16[1024,1408]{1,0:T(8,128)(2,1)S(1)}, bf16[1024,1408]{1,0:T(8,128)(2,1)}, u32[]{:S(2)}, u32[]{:S(2)}) collective-permute-start(bf16[1024,1408]{1,0:T(8,128)(2,1)S(1)} %copy-done), channel_id=1, source_target_pairs={{0,4},{4,0},{8,12},{12,8},{1,5},{5,1},{9,13},{13,9},{2,6},{6,2},{1... | collective-permute-start | bytes 8650760 | tf_op jit(solution)/shard_map/ppermute | solution.py:1031
  468.2 60.6 %collective-permute-start.24 = (bf16[1024,512]{1,0:T(8,128)(2,1)S(1)}, bf16[1024,512]{1,0:T(8,128)(2,1)S(1)}, u32[]{:S(2)}, u32[]{:S(2)}) collective-permute-start(bf16[1024,512]{1,0:T(8,128)(2,1)S(1)} %get-tuple-element.203), channel_id=1, source_target_pairs={{0,1},{1,2},{2,3},{3,0},{4,5},{5,6},{6,7},{7,4},{8,9},{9,10},{10,1... | collective-permute-start | bytes 3145736 | tf_op jit(solution)/shard_map/ppermute | solution.py:1028
  527.7 54.3 %collective-permute-start.30 = (bf16[2,1024,384]{2,1,0:T(8,128)(2,1)}, bf16[2,1024,384]{2,1,0:T(8,128)(2,1)S(1)}, u32[]{:S(2)}, u32[]{:S(2)}) collective-permute-start(bf16[2,1024,384]{2,1,0:T(8,128)(2,1)} %get-tuple-element.125), channel_id=1, source_target_pairs={{0,8},{4,12},{8,0},{12,4},{1,9},{5,13},{9,1},{13,5},{2,10},{6,14},... | collective-permute-start | bytes 4718600 | tf_op jit(solution)/shard_map/ppermute | solution.py:1031
  530.3 25.4 %collective-permute-start.25 = (bf16[1024,512]{1,0:T(8,128)(2,1)S(1)}, bf16[1024,512]{1,0:T(8,128)(2,1)S(1)}, u32[]{:S(2)}, u32[]{:S(2)}) collective-permute-start(bf16[1024,512]{1,0:T(8,128)(2,1)S(1)} %fusion.1), channel_id=1, source_target_pairs={{0,1},{1,2},{2,3},{3,0},{4,5},{5,6},{6,7},{7,4},{8,9},{9,10},{10,1... | collective-permute-start | bytes 3145736 | tf_op jit(solution)/shard_map/ppermute | solution.py:1028
  533.0 54.3 %collective-permute-start.32 = (bf16[1024,1024]{1,0:T(8,128)(2,1)}, bf16[1024,1024]{1,0:T(8,128)(2,1)}, u32[]{:S(2)}, u32[]{:S(2)}) collective-permute-start(bf16[1024,1024]{1,0:T(8,128)(2,1)} %get-tuple-element.127), channel_id=1, source_target_pairs={{0,4},{4,0},{8,12},{12,8},{1,5},{5,1},{9,13},{13,9},{2,6},{6,2},{1... | collective-permute-start | bytes 6291464 | tf_op jit(solution)/shard_map/ppermute | solution.py:1031
  559.1 25.7 %collective-permute-start.28 = (bf16[1024,512]{1,0:T(8,128)(2,1)}, bf16[1024,512]{1,0:T(8,128)(2,1)S(1)}, u32[]{:S(2)}, u32[]{:S(2)}) collective-permute-start(bf16[1024,512]{1,0:T(8,128)(2,1)} %ring_add.4.refs_1_), channel_id=1, source_target_pairs={{0,1},{1,2},{2,3},{3,0},{4,5},{5,6},{6,7},{7,4},{8,9},{9,10},{10,1... | collective-permute-start | bytes 3145736 | tf_op jit(solution)/shard_map/ppermute | solution.py:1028
  561.6 25.8 %collective-permute-start.29 = (bf16[1024,384]{1,0:T(8,128)(2,1)S(1)}, bf16[1024,384]{1,0:T(8,128)(2,1)S(1)}, u32[]{:S(2)}, u32[]{:S(2)}) collective-permute-start(bf16[1024,384]{1,0:T(8,128)(2,1)S(1)} %copy-done.48), channel_id=1, source_target_pairs={{0,4},{4,0},{8,12},{12,8},{1,5},{5,1},{9,13},{13,9},{2,6},{6,2},{1... | collective-permute-start | bytes 2359304 | tf_op jit(solution)/shard_map/ppermute | solution.py:1031
  583.3 4.1 collective-permute-start.31
  608.2 8.7 %collective-permute-start.37 = (bf16[1024,1536]{1,0:T(8,128)(2,1)}, bf16[1024,1536]{1,0:T(8,128)(2,1)S(1)}, u32[]{:S(2)}, u32[]{:S(2)}) collective-permute-start(bf16[1024,1536]{1,0:T(8,128)(2,1)} %get-tuple-element.136.right_here), channel_id=1, source_target_pairs={{0,4},{4,0},{8,12},{12,8},{1,5},{5,1},{9,13},{13,9},{2,6},{6,2},{1... | collective-permute-start | bytes 9437192 | tf_op jit(solution)/shard_map/ppermute | solution.py:1031
  609.1 25.8 %collective-permute-start.34 = (f32[1,8192]{1,0:T(1,128)S(1)}, f32[1,8192]{1,0:T(1,128)S(1)}, u32[]{:S(2)}, u32[]{:S(2)}) collective-permute-start(f32[1,8192]{1,0:T(1,128)S(1)} %constant_dynamic-update-slice_fusion), channel_id=1, source_target_pairs={{0,1},{1,2},{2,3},{3,0},{4,5},{5,6},{6,7},{7,4},{8,9},{9,10},{10,1... | collective-permute-start | bytes 98312 | tf_op jit(solution)/shard_map/ppermute | solution.py:1028
  610.4 24.5 %collective-permute-start.35 = (f32[1,8192]{1,0:T(1,128)S(1)}, f32[1,8192]{1,0:T(1,128)S(1)}, u32[]{:S(2)}, u32[]{:S(2)}) collective-permute-start(f32[1,8192]{1,0:T(1,128)S(1)} %constant_dynamic-update-slice_fusion), channel_id=1, source_target_pairs={{0,2},{1,3},{2,0},{3,1},{4,6},{5,7},{6,4},{7,5},{8,10},{9,11},{10,... | collective-permute-start | bytes 98312 | tf_op jit(solution)/shard_map/ppermute | solution.py:1028
  614.9 20.0 %collective-permute-start.36 = (f32[1,8192]{1,0:T(1,128)S(1)}, f32[1,8192]{1,0:T(1,128)S(1)}, u32[]{:S(2)}, u32[]{:S(2)}) collective-permute-start(f32[1,8192]{1,0:T(1,128)S(1)} %constant_dynamic-update-slice_fusion), channel_id=1, source_target_pairs={{0,3},{1,0},{2,1},{3,2},{4,7},{5,4},{6,5},{7,6},{8,11},{9,8},{10,9... | collective-permute-start | bytes 98312 | tf_op jit(solution)/shard_map/ppermute | solution.py:1028
  614.9 82.5 %collective-permute-start.33 = (bf16[1024,512]{1,0:T(8,128)(2,1)}, bf16[1024,512]{1,0:T(8,128)(2,1)}, u32[]{:S(2)}, u32[]{:S(2)}) collective-permute-start(bf16[1024,512]{1,0:T(8,128)(2,1)} %get-tuple-element.128), channel_id=1, source_target_pairs={{0,1},{1,2},{2,3},{3,0},{4,5},{5,6},{6,7},{7,4},{8,9},{9,10},{10,1... | collective-permute-start | bytes 3145736 | tf_op jit(solution)/shard_map/ppermute | solution.py:1028
  633.0 58.2 %copy-start.6 = (bf16[2,128,2944]{2,1,0:T(8,128)(2,1)S(1)}, bf16[2,128,2944]{2,1,0:T(8,128)(2,1)}, u32[]{:S(2)}) copy-start(bf16[2,128,2944]{2,1,0:T(8,128)(2,1)} %get-tuple-element.142.refs_5_) | copy-start | bytes 4521988
  633.0 57.0 %collective-permute-start.40 = (bf16[2,128,2944]{2,1,0:T(8,128)(2,1)}, bf16[2,128,2944]{2,1,0:T(8,128)(2,1)S(1)}, u32[]{:S(2)}, u32[]{:S(2)}) collective-permute-start(bf16[2,128,2944]{2,1,0:T(8,128)(2,1)} %get-tuple-element.143.refs_6_), channel_id=1, source_target_pairs={{0,8},{4,12},{8,0},{12,4},{1,9},{5,13},{9,1},{13,5},{2,10},{6,14},... | collective-permute-start | bytes 4521992 | tf_op jit(solution)/shard_map/ppermute | solution.py:1031
  635.0 59.0 %collective-permute-start.39 = (bf16[2,128,2944]{2,1,0:T(8,128)(2,1)}, bf16[2,128,2944]{2,1,0:T(8,128)(2,1)}, u32[]{:S(2)}, u32[]{:S(2)}) collective-permute-start(bf16[2,128,2944]{2,1,0:T(8,128)(2,1)} %get-tuple-element.141.refs_4_), channel_id=1, source_target_pairs={{0,16},{16,0},{1,17},{17,1},{2,18},{18,2},{3,19},{19,3},{4,20},{20... | collective-permute-start | bytes 4521992 | tf_op jit(solution)/shard_map/ppermute | solution.py:1051
  694.0 18.0 %collective-permute-start.49 = (bf16[128,2944]{1,0:T(8,128)(2,1)}, bf16[128,2944]{1,0:T(8,128)(2,1)}, u32[]{:S(2)}, u32[]{:S(2)}) collective-permute-start(bf16[128,2944]{1,0:T(8,128)(2,1)} %slice_bitcast_fusion.4), channel_id=1, source_target_pairs={{0,16},{16,0},{1,17},{17,1},{2,18},{18,2},{3,19},{19,3},{4,20},{20... | collective-permute-start | bytes 2261000 | tf_op jit(solution)/shard_map/ppermute | solution.py:1051
  696.8 18.0 %collective-permute-start.48 = (bf16[128,2944]{1,0:T(8,128)(2,1)}, bf16[128,2944]{1,0:T(8,128)(2,1)}, u32[]{:S(2)}, u32[]{:S(2)}) collective-permute-start(bf16[128,2944]{1,0:T(8,128)(2,1)} %slice_bitcast_fusion.6), channel_id=1, source_target_pairs={{0,8},{4,12},{8,0},{12,4},{1,9},{5,13},{9,1},{13,5},{2,10},{6,14},... | collective-permute-start | bytes 2261000 | tf_op jit(solution)/shard_map/ppermute | solution.py:1031
  699.9 24.1 %collective-permute-start.38 = (bf16[1024,512]{1,0:T(8,128)(2,1)}, bf16[1024,512]{1,0:T(8,128)(2,1)}, u32[]{:S(2)}, u32[]{:S(2)}) collective-permute-start(bf16[1024,512]{1,0:T(8,128)(2,1)} %ring_add.5.refs_1_), channel_id=1, source_target_pairs={{0,1},{1,2},{2,3},{3,0},{4,5},{5,6},{6,7},{7,4},{8,9},{9,10},{10,1... | collective-permute-start | bytes 3145736 | tf_op jit(solution)/shard_map/ppermute | solution.py:1028
  714.4 1.7 collective-permute-start.41
  716.2 4.0 collective-permute-start.42
  726.4 49.9 %collective-permute-start.43 = (bf16[1024,512]{1,0:T(8,128)(2,1)}, bf16[1024,512]{1,0:T(8,128)(2,1)}, u32[]{:S(2)}, u32[]{:S(2)}) collective-permute-start(bf16[1024,512]{1,0:T(8,128)(2,1)} %ring_add.6.refs_1_), channel_id=1, source_target_pairs={{0,1},{1,2},{2,3},{3,0},{4,5},{5,6},{6,7},{7,4},{8,9},{9,10},{10,1... | collective-permute-start | bytes 3145736 | tf_op jit(solution)/shard_map/ppermute | solution.py:1028
  735.9 11.1 %collective-permute-start.47 = (f32[1,9728]{1,0:T(1,128)}, f32[1,9728]{1,0:T(1,128)S(1)}, u32[]{:S(2)}, u32[]{:S(2)}) collective-permute-start(f32[1,9728]{1,0:T(1,128)} %tie.29), channel_id=1, source_target_pairs={{0,16},{16,0},{1,17},{17,1},{2,18},{18,2},{3,19},{19,3},{4,20},{20... | collective-permute-start | bytes 116744 | tf_op jit(solution)/shard_map/ppermute | solution.py:1240
  741.6 26.6 %collective-permute-start.44 = (bf16[256,512]{0,1:T(8,128)(2,1)S(1)}, bf16[256,512]{0,1:T(8,128)(2,1)S(1)}, u32[]{:S(2)}, u32[]{:S(2)}) collective-permute-start(bf16[256,512]{0,1:T(8,128)(2,1)S(1)} %get-tuple-element.208), channel_id=1, source_target_pairs={{0,1},{1,2},{2,3},{3,0},{4,5},{5,6},{6,7},{7,4},{8,9},{9,10},{10,1... | collective-permute-start | bytes 786440 | tf_op jit(solution)/shard_map/ppermute | solution.py:1028
  743.2 27.8 %collective-permute-start.45 = (bf16[256,512]{0,1:T(8,128)(2,1)S(1)}, bf16[256,512]{0,1:T(8,128)(2,1)S(1)}, u32[]{:S(2)}, u32[]{:S(2)}) collective-permute-start(bf16[256,512]{0,1:T(8,128)(2,1)S(1)} %get-tuple-element.210), channel_id=1, source_target_pairs={{0,2},{1,3},{2,0},{3,1},{4,6},{5,7},{6,4},{7,5},{8,10},{9,11},{10,... | collective-permute-start | bytes 786440 | tf_op jit(solution)/shard_map/ppermute | solution.py:1028
  745.0 30.4 %collective-permute-start.46 = (bf16[256,512]{0,1:T(8,128)(2,1)S(1)}, bf16[256,512]{0,1:T(8,128)(2,1)S(1)}, u32[]{:S(2)}, u32[]{:S(2)}) collective-permute-start(bf16[256,512]{0,1:T(8,128)(2,1)S(1)} %get-tuple-element.209), channel_id=1, source_target_pairs={{0,3},{1,0},{2,1},{3,2},{4,7},{5,4},{6,5},{7,6},{8,11},{9,8},{10,9... | collective-permute-start | bytes 786440 | tf_op jit(solution)/shard_map/ppermute | solution.py:1028
  (46 other events, 280.5 us)
Sparse Core Ops, SparseCore 0:
  11.2 46.6 all-gather.3
  59.8 113.7 all-gather.5
  176.1 54.3 all-gather.7
  430.6 61.7 reduce-scatter.3
  496.1 95.9 reduce-scatter.5
  608.5 82.5 reduce-scatter.7
where the time goes:
time: 791 us; the launch traced here: 786 us
  Pallas kernels  307 us (39%)
  waiting for transfers between devices  302 us (38%)
  starting transfers between devices  77.3 us (10%)
  local copies, waits for them, and re-layouts  52.8 us (7%)
  other arithmetic  31.7 us (4%)
  between operations  15.1 us (2%)
    ppermute x33, waiting for transfers between devices, shift(): return lax.ppermute(value, 'tp', [(i, (i + step) % tp) for i in range(tp)])  156 us
    ppermute x12, waiting for transfers between devices, swap(): return lax.ppermute(value, 'ctx', [(i, i ^ step) for i in range(nctx)])  99.8 us
    pallas_call x4, Pallas kernels, feed(): pl.pallas_call(functools.partial(feed_kernel, tuple(cuts), parts, tp, ste...  71 us
    pallas_call x1, Pallas kernels, attend_back(): pl.pallas_call(functools.partial(attend_back_kernel, nctx, heads, len(pie...  58.5 us
    ppermute x33, starting transfers between devices, shift(): return lax.ppermute(value, 'tp', [(i, (i + step) % tp) for i in range(tp)])  56.9 us
    pallas_call x1, Pallas kernels, attend(): pl.pallas_call(functools.partial(attend_kernel, nctx, heads, len(pieces),...  40.6 us
    unnamed x113, local copies, waits for them, and re-layouts  34.6 us
    pallas_call x3, Pallas kernels, blame(): pl.pallas_call(kernel, grid=(steps,), in_specs=in_specs + anywhere(len(ne...  27.9 us
  transfers between devices with their start and end apart: 58, of which 27 were waited for; matrix products, arithmetic and copies ran while one was open for 8% of the time, Pallas kernels for 36%

commit v1 on v0

--- a/solution.py
+++ b/solution.py
@@ -1050,9 +1050,10 @@
     def cross(value):
         return lax.ppermute(value, "fsdp", [(i, i ^ 1) for i in range(nfsdp)])
 
-    def square_once(parts):
+    def square_once(parts, last):
         near, far, low, high = parts
-        return total(near, cross(far)), total(low, swap(high, 2))
+        far, high = cross(far), swap(high, 2)
+        return total(tie(near, last), far), total(tie(low, last), high)
 
     def square_twice(first, second):
         first = first[0].astype(F32) + swap(first[1], 2).astype(F32)
@@ -1247,8 +1248,7 @@
     small = sum([shift(small, step) for step in range(1, tp)], small)
     small = jnp.concatenate([bias_grad, small], axis=1)
     travelling, ring_steps = partial[1 % tp], []
-    once = square_once(parts) if square else ()
-    needed = [[total_gate, total_out, small, *parts], [*once], []]
+    needed = [[total_gate, total_out, small, *parts], [], []]
     for step in range(1, tp):
         travelling = add(
             shift(travelling, 1), partial[(step + 1) % tp], *(needed[step - 1] if step < 4 else [])
@@ -1264,6 +1264,8 @@
             total_up = tie(total_up, travelling).astype(F32)
             needed[2].extend([total_out, total_up])
         if step == 1:
+            once = square_once(parts, travelling) if square else ()
+            needed[1].extend(once)
             small = exchange(tie(small, travelling), "ctx", powers(0, nctx), nctx)
             needed[1].append(small)
         if step == 2:

time: 791 us -> 793 us (level); the launches traced: 786 us -> 777 us
  Pallas kernels: 307 us -> 293 us
  waiting for transfers between devices: 302 us -> 311 us
    ppermute x33, waiting for transfers between devices: 156 us -> 169 us  [shift(): return lax.ppermute(value, 'tp', [(i, (i + step) % tp) for i in range(tp)])]
    pallas_call x1, Pallas kernels: 58.5 us -> 50.1 us  [attend_back(): pl.pallas_call(functools.partial(attend_back_kernel, nctx, heads, len(pie...]
    unnamed x113 -> x125, local copies, waits for them, and re-layouts: 34.6 us -> 33.7 us
  transfers between devices with their start and end apart: 58 -> 58, of which waited for: 27 -> 26; matrix products, arithmetic and copies ran while one was open for 8% -> 7% of each run, Pallas kernels for 36% -> 35%
where the time goes in v1:
time: 793 us; the launch traced here: 777 us
  waiting for transfers between devices  311 us (39%)
  Pallas kernels  293 us (37%)
  starting transfers between devices  81.5 us (10%)
  local copies, waits for them, and re-layouts  49.1 us (6%)
  other arithmetic  27.3 us (3%)
  between operations  15.2 us (2%)
    ppermute x33, waiting for transfers between devices, shift(): return lax.ppermute(value, 'tp', [(i, (i + step) % tp) for i in range(tp)])  169 us
    ppermute x12, waiting for transfers between devices, swap(): return lax.ppermute(value, 'ctx', [(i, i ^ step) for i in range(nctx)])  102 us
    pallas_call x4, Pallas kernels, feed(): pl.pallas_call(functools.partial(feed_kernel, tuple(cuts), parts, tp, ste...  70.8 us
    ppermute x33, starting transfers between devices, shift(): return lax.ppermute(value, 'tp', [(i, (i + step) % tp) for i in range(tp)])  58.7 us
    pallas_call x1, Pallas kernels, attend_back(): pl.pallas_call(functools.partial(attend_back_kernel, nctx, heads, len(pie...  50.1 us
    pallas_call x1, Pallas kernels, attend(): pl.pallas_call(functools.partial(attend_kernel, nctx, heads, len(pieces),...  34.8 us
    unnamed x125, local copies, waits for them, and re-layouts  33.7 us
    pallas_call x3, Pallas kernels, blame(): pl.pallas_call(kernel, grid=(steps,), in_specs=in_specs + anywhere(len(ne...  28.2 us
  transfers between devices with their start and end apart: 58, of which 26 were waited for; matrix products, arithmetic and copies ran while one was open for 7% of the time, Pallas kernels for 35%

profile of v1, /device:TPU:8, one launch (start us, length us, event | category | flops | bytes accessed | tf_op | source)
XLA Modules:
  0.0 777.0 jit_solution(1808787466840007897)
XLA Ops:
  7.2 2.3 copy.135.refs_0_
  11.1 3.1 pack.1.refs_1_
  19.6 13.8 %collective-permute-done.refs_0_ = bf16[640,512]{1,0:T(8,128)(2,1)S(1)} collective-permute-done((bf16[640,512]{1,0:T(8,128)(2,1)S(1)}, bf16[640,512]{1,0:T(8,128)(2,1)S(1)}, u32[]{:S(2)}, u32[]{:S(2)}) %collective-permute-start) | collective-permute-done | bytes 655392 | tf_op jit(solution)/shard_map/ppermute | solution.py:1028
  35.9 11.6 %collective-permute-done.3.refs_0_ = bf16[640,512]{1,0:T(8,128)(2,1)S(1)} collective-permute-done((bf16[640,512]{1,0:T(8,128)(2,1)S(1)}, bf16[640,512]{1,0:T(8,128)(2,1)S(1)}, u32[]{:S(2)}, u32[]{:S(2)}) %collective-permute-start.3) | collective-permute-done | bytes 655392 | tf_op jit(solution)/shard_map/ppermute | solution.py:1028
  50.1 11.5 %collective-permute-done.1.refs_2_ = bf16[640,512]{1,0:T(8,128)(2,1)} collective-permute-done((bf16[640,512]{1,0:T(8,128)(2,1)}, bf16[640,512]{1,0:T(8,128)(2,1)}, u32[]{:S(2)}, u32[]{:S(2)}) %collective-permute-start.1) | collective-permute-done | bytes 655392 | tf_op jit(solution)/shard_map/ppermute | solution.py:1028
  63.2 12.4 %collective-permute-done.4.refs_6_ = bf16[640,512]{1,0:T(8,128)(2,1)S(1)} collective-permute-done((bf16[640,512]{1,0:T(8,128)(2,1)}, bf16[640,512]{1,0:T(8,128)(2,1)S(1)}, u32[]{:S(2)}, u32[]{:S(2)}) %collective-permute-start.4) | collective-permute-done | bytes 655392 | tf_op jit(solution)/shard_map/ppermute | solution.py:1028
  78.6 3.2 fusion.4
  81.8 7.8 %collective-permute-done.2.refs_3_.refs_1_ = bf16[640,512]{1,0:T(8,128)(2,1)S(1)} collective-permute-done((bf16[640,512]{1,0:T(8,128)(2,1)}, bf16[640,512]{1,0:T(8,128)(2,1)S(1)}, u32[]{:S(2)}, u32[]{:S(2)}) %collective-permute-start.2) | collective-permute-done | bytes 655392 | tf_op jit(solution)/shard_map/ppermute | solution.py:1028
  89.6 12.9 %collective-permute-done.5.refs_7_.refs_2_ = bf16[640,512]{1,0:T(8,128)(2,1)S(1)} collective-permute-done((bf16[640,512]{1,0:T(8,128)(2,1)S(1)}, bf16[640,512]{1,0:T(8,128)(2,1)S(1)}, u32[]{:S(2)}, u32[]{:S(2)}) %collective-permute-start.5) | collective-permute-done | bytes 655392 | tf_op jit(solution)/shard_map/ppermute | solution.py:1028
  103.3 21.5 %project.1 = (bf16[1024,2048]{1,0:T(8,128)(2,1)}, bf16[1024,2048]{1,0:T(8,128)(2,1)}, bf16[1024,1024]{1,0:T(8,128)(2,1)}, bf16[1024,384]{1,0:T(8,128)(2,1)}, bf1...) custom-call(s32[3]{0:T(128)} %pad_add_fusion.1.place, ...), custom_call_target="tpu_custom_call" | custom-call | flops 6000000000 | tf_op jit(solution)/shard_map/project/pallas_call | solution.py:225
  131.2 11.9 %collective-permute-done.10.refs_5_ = bf16[512,512]{1,0:T(8,128)(2,1)S(1)} collective-permute-done((bf16[512,512]{1,0:T(8,128)(2,1)S(1)}, bf16[512,512]{1,0:T(8,128)(2,1)S(1)}, u32[]{:S(2)}, u32[]{:S(2)}) %collective-permute-start.10) | collective-permute-done | bytes 524320 | tf_op jit(solution)/shard_map/ppermute | solution.py:1028
  144.4 9.9 %collective-permute-done.8.refs_1_ = bf16[512,512]{1,0:T(8,128)(2,1)S(1)} collective-permute-done((bf16[512,512]{1,0:T(8,128)(2,1)S(1)}, bf16[512,512]{1,0:T(8,128)(2,1)S(1)}, u32[]{:S(2)}, u32[]{:S(2)}) %collective-permute-start.8) | collective-permute-done | bytes 524320 | tf_op jit(solution)/shard_map/ppermute | solution.py:1028
  156.1 27.0 %collective-permute-done.7 = bf16[2,1024,384]{2,1,0:T(8,128)(2,1)} collective-permute-done((bf16[2,1024,384]{2,1,0:T(8,128)(2,1)}, bf16[2,1024,384]{2,1,0:T(8,128)(2,1)}, u32[]{:S(2)}, u32[]{:S(2)}) %collective-permute-start.7) | collective-permute-done | bytes 1572896 | tf_op jit(solution)/shard_map/ppermute | solution.py:1031
  183.1 2.9 slice_bitcast_fusion.2
  192.6 34.8 %attend.1 = (bf16[4096,128]{1,0:T(8,128)(2,1)}, bf16[4096,128]{1,0:T(8,128)(2,1)}, f32[2,4096]{1,0:T(2,128)}) custom-call(s32[1]{0:T(128)} %bitcast.1.place, s32[8]{0:T(128)} %fusion.27.lows, s32[8]{0:T(128)} %multiply_add_fusion.ends, s32[2,4096]{1,0:T(2,128)} %pad_add_fusion.bounds, bf16[1024,384]{1,0:T(8,128)(2,1)} %get-tuple-element.79.refs_0_, ...), custom_call_target="tpu_custom_call" | custom-call | flops 20000000000 | tf_op jit(solution)/shard_map/attend/pallas_call | solution.py:360
  228.4 4.2 all-to-all-start
  232.6 24.2 %all-to-all-done = bf16[16,256,128]{2,1,0:T(8,128)(2,1)S(1)} async-done(((bf16[16,256,128]{2,1,0:T(8,128)(2,1)}), bf16[16,256,128]{2,1,0:T(8,128)(2,1)S(1)}, u32[]{:S(2)}, u32[]{:S(2)}) %all-to-all-start) | async-done | bytes 1048608 | tf_op jit(solution)/shard_map/all_to_all | solution.py:1132
  257.7 9.5 %mix.1 = (bf16[256,2048]{1,0:T(8,128)(2,1)}, f32[256,2048]{1,0:T(8,128)}, bf16[256,2048]{1,0:T(8,128)(2,1)}) custom-call(s32[3]{0:T(128)} %pad_add_fusion.1.place, bf16[4,4,256,128]{3,2,1,0:T(8,128)(2,1)} %bitcast.127, bf16[4,2048,512]{2,1,0:T(8,128)(2,1)} %all-gather.8.cloned.1.call-done.weight.refs_7_, ...), custom_call_target="tpu_custom_call" | custom-call | flops 5000000000 | tf_op jit(solution)/shard_map/mix/pallas_call | solution.py:533
  267.8 6.0 join.1
  273.8 17.7 %feed.4 = (bf16[1024,2048]{1,0:T(8,128)(2,1)}, bf16[1024,1408]{1,0:T(8,128)(2,1)}, bf16[1024,1408]{1,0:T(8,128)(2,1)}, bf16[1024,1408]{1,0:T(8,128)(2,1)}, bf16[...) custom-call(s32[3]{0:T(128)} %pad_add_fusion.1.place, ...), custom_call_target="tpu_custom_call" | custom-call | flops 10000000000 | tf_op jit(solution)/shard_map/feed/pallas_call | solution.py:623
  295.1 17.7 %feed.5 = (bf16[1024,2048]{1,0:T(8,128)(2,1)}, bf16[1024,1408]{1,0:T(8,128)(2,1)}, bf16[1024,1408]{1,0:T(8,128)(2,1)}, bf16[1024,1408]{1,0:T(8,128)(2,1)}, bf16[...) custom-call(s32[3]{0:T(128)} %pad_add_fusion.1.place, ...), custom_call_target="tpu_custom_call", output_to_operand_aliasing={{0}: (5, {}), {1}: (6, {}), {2}: (7, {}), {3}: (8, {}), {4}... | custom-call | flops 10000000000 | tf_op jit(solution)/shard_map/feed/pallas_call | solution.py:623
  312.8 3.0 collective-permute-start.19
  315.8 3.1 collective-permute-start.18
  318.9 3.6 collective-permute-done.16.low
  323.5 17.7 %feed.6 = (bf16[1024,2048]{1,0:T(8,128)(2,1)}, bf16[1024,1408]{1,0:T(8,128)(2,1)}, bf16[1024,1408]{1,0:T(8,128)(2,1)}, bf16[1024,1408]{1,0:T(8,128)(2,1)}, bf16[...) custom-call(s32[3]{0:T(128)} %pad_add_fusion.1.place, ...), custom_call_target="tpu_custom_call", output_to_operand_aliasing={{0}: (5, {}), {1}: (6, {}), {2}: (7, {}), {3}: (8, {}), {4}... | custom-call | flops 10000000000 | tf_op jit(solution)/shard_map/feed/pallas_call | solution.py:623
  345.1 3.9 collective-permute-start.20
  349.0 18.5 %collective-permute-done.17.low = bf16[256,2048]{1,0:T(8,128)(2,1)S(1)} collective-permute-done((bf16[256,2048]{1,0:T(8,128)(2,1)S(1)}, bf16[256,2048]{1,0:T(8,128)(2,1)S(1)}, u32[]{:S(2)}, u32[]{:S(2)}) %collective-permute-start.17) | collective-permute-done | bytes 1048608 | tf_op jit(solution)/shard_map/ppermute | solution.py:1028
  368.4 17.7 %feed.7 = (bf16[1024,2048]{1,0:T(8,128)(2,1)}, bf16[1024,1408]{1,0:T(8,128)(2,1)}, bf16[1024,1408]{1,0:T(8,128)(2,1)}, bf16[1024,1408]{1,0:T(8,128)(2,1)}, bf16[...) custom-call(s32[3]{0:T(128)} %pad_add_fusion.1.place, ...), custom_call_target="tpu_custom_call", output_to_operand_aliasing={{0}: (5, {}), {1}: (6, {}), {2}: (7, {}), {3}: (8, {}), {4}... | custom-call | flops 10000000000 | tf_op jit(solution)/shard_map/feed/pallas_call | solution.py:623
  388.1 2.4 collective-permute-start.21
  390.5 10.7 %blame.4.refs_9_.refs_0_ = bf16[2048,1408]{1,0:T(8,128)(2,1)} custom-call(bf16[1024,2048]{1,0:T(8,128)(2,1)} %get-tuple-element.112.left, bf16[1024,1408]{1,0:T(8,128)(2,1)} %get-tuple-element.114.right, bf16[128,2048]{1,0:T(8,128)(2,1)} %copy-done.41, bf16[128,2048]{1,0:T(8,128)(2,1)} %copy-done.40), custom_call_target="tpu_custom_call" | custom-call | flops 6000000000 | tf_op jit(solution)/shard_map/blame/pallas_call | solution.py:726
  401.2 10.6 %blame.3.refs_8_.refs_0_ = bf16[2048,1408]{1,0:T(8,128)(2,1)} custom-call(bf16[1024,2048]{1,0:T(8,128)(2,1)} %get-tuple-element.112.left, bf16[1024,1408]{1,0:T(8,128)(2,1)} %get-tuple-element.113.right, bf16[128,2048]{1,0:T(8,128)(2,1)} %copy-done.41, bf16[128,2048]{1,0:T(8,128)(2,1)} %copy-done.40), custom_call_target="tpu_custom_call" | custom-call | flops 6000000000 | tf_op jit(solution)/shard_map/blame/pallas_call | solution.py:726
  412.8 11.7 %turn.1 = (bf16[4,4,256,128]{3,2,1,0:T(8,128)(2,1)}, f32[256,2048]{1,0:T(8,128)}, bf16[256,2048]{1,0:T(8,128)(2,1)}, f32[1,2048]{1,0:T(1,128)}, f32[1,2048]{1,0:T(1,128)}, /*index=5*/bf16[256,1024]{1,0:T(8,128)(2,1)}) custom-call(s32[3]{0:T(128)} %pad_add_fusion.1.place, bf16[128,2048]{1,0:T(8,128)(2,1)} %copy-done.39, bf16[128,2048]{1,0:T(8,128)(2,1)} %copy-done.36, ...), custom_call_target="tpu_custom_call" | custom-call | flops 6000000000 | tf_op jit(solution)/shard_map/turn/pallas_call | solution.py:798
  424.5 8.0 %all-to-all-start.1 = ((bf16[16,256,128]{2,1,0:T(8,128)(2,1)}), bf16[16,256,128]{2,1,0:T(8,128)(2,1)S(1)}, u32[]{:S(2)}, u32[]{:S(2)}) async-start(bf16[16,256,128]{2,1,0:T(8,128)(2,1)} %bitcast.33), calls=%async_computation.1 | async-start | bytes 2097152 | tf_op jit(solution)/shard_map/all_to_all | solution.py:1185
  432.5 6.9 blame.5.refs_6_
  439.5 8.9 %copy.119.refs_0_ = bf16[2048,2048]{1,0:T(8,128)(2,1)} copy(bf16[2048,2048]{1,0:T(8,128)(2,1)} %blame.5.refs_6_) | data formatting | bytes 16777216
  448.4 8.3 %all-to-all-done.1 = bf16[16,256,128]{2,1,0:T(8,128)(2,1)S(1)} async-done(((bf16[16,256,128]{2,1,0:T(8,128)(2,1)}), bf16[16,256,128]{2,1,0:T(8,128)(2,1)S(1)}, u32[]{:S(2)}, u32[]{:S(2)}) %all-to-all-start.1) | async-done | bytes 1048608 | tf_op jit(solution)/shard_map/all_to_all | solution.py:1185
  459.5 2.7 dynamic-slice_bitcast_fusion
  463.1 50.1 %attend_back.1 = (bf16[1024,384]{1,0:T(8,128)(2,1)}, bf16[1024,384]{1,0:T(8,128)(2,1)}, bf16[2,1024,384]{2,1,0:T(8,128)(2,1)}) custom-call(s32[1]{0:T(128)} %bitcast.1.place, s32[8]{0:T(128)} %fusion.27.lows, s32[8]{0:T(128)} %multiply_add_fusion.ends, s32[2,4096]{1,0:T(2,128)} %pad_add_fusion.bounds, f32[2,4096]{1,0:T(2,128)} %get-tuple-element.119.logs, ...), custom_call_target="tpu_custom_call" | custom-call | flops 24999999488 | tf_op jit(solution)/shard_map/attend_back/pallas_call | solution.py:476
  515.9 2.7 collective-permute-start.25
  519.2 13.2 %blame_halves.2 = (bf16[2,128,2944]{2,1,0:T(8,128)(2,1)}, bf16[2,128,2944]{2,1,0:T(8,128)(2,1)}, bf16[2,128,2944]{2,1,0:T(8,128)(2,1)}, bf16[2,128,2944]{2,1,0:T(8,128)(2,1)}) custom-call(s32[4]{0:T(128)} %pad_add_fusion.2.place, bf16[4,1024,512]{2,1,0:T(8,128)(2,1)} %get-tuple-element.86.cot.refs_5_.left_here, ...), custom_call_target="tpu_custom_call" | custom-call | flops 6000000000 | tf_op jit(solution)/shard_map/blame_halves/pallas_call | solution.py:698
  532.4 8.7 %collective-permute-done.25.left = bf16[1024,512]{1,0:T(8,128)(2,1)S(1)} collective-permute-done((bf16[1024,512]{1,0:T(8,128)(2,1)S(1)}, bf16[1024,512]{1,0:T(8,128)(2,1)S(1)}, u32[]{:S(2)}, u32[]{:S(2)}) %collective-permute-start.25) | collective-permute-done | bytes 1048608 | tf_op jit(solution)/shard_map/ppermute | solution.py:1028
  542.1 2.7 ring_add.4.refs_1_
  544.8 2.3 collective-permute-start.28
  547.1 25.1 %collective-permute-done.30 = bf16[2,1024,384]{2,1,0:T(8,128)(2,1)S(1)} collective-permute-done((bf16[2,1024,384]{2,1,0:T(8,128)(2,1)}, bf16[2,1024,384]{2,1,0:T(8,128)(2,1)S(1)}, u32[]{:S(2)}, u32[]{:S(2)}) %collective-permute-start.30) | collective-permute-done | bytes 1572896 | tf_op jit(solution)/shard_map/ppermute | solution.py:1031
  573.5 2.5 fusion.refs_11_
  577.2 19.7 %finish.1 = (bf16[1024,512]{1,0:T(8,128)(2,1)}, bf16[1024,512]{1,0:T(8,128)(2,1)}, bf16[1024,512]{1,0:T(8,128)(2,1)}, bf16[1024,512]{1,0:T(8,128)(2,1)}, bf16[10...) custom-call(s32[3]{0:T(128)} %pad_add_fusion.1.place, ...), custom_call_target="tpu_custom_call" | custom-call | flops 7000000000 | tf_op jit(solution)/shard_map/finish/pallas_call | solution.py:910
  598.3 3.6 collective-permute-start.34
  601.9 3.3 collective-permute-start.35
  607.2 14.1 %blame_halves.3 = (bf16[2,128,2944]{2,1,0:T(8,128)(2,1)}, bf16[2,128,2944]{2,1,0:T(8,128)(2,1)}, bf16[2,128,2944]{2,1,0:T(8,128)(2,1)}, bf16[2,128,2944]{2,1,0:T(8,128)(2,1)}) custom-call(s32[4]{0:T(128)} %pad_add_fusion.2.place, ...), custom_call_target="tpu_custom_call", output_to_operand_aliasing={{0}: (5, {}), {1}: (6, {}), {2}: (7, {}), {3}: (8, {})} | custom-call | flops 6000000000 | tf_op jit(solution)/shard_map/blame_halves/pallas_call | solution.py:698
  624.3 2.3 convert_element_type.157.refs_0_
  626.6 5.1 collective-permute-done.33.left
  632.8 2.4 ring_add.5.refs_1_
  635.2 41.3 %collective-permute-done.40 = bf16[2,128,2944]{2,1,0:T(8,128)(2,1)} collective-permute-done((bf16[2,128,2944]{2,1,0:T(8,128)(2,1)}, bf16[2,128,2944]{2,1,0:T(8,128)(2,1)}, u32[]{:S(2)}, u32[]{:S(2)}) %collective-permute-start.40) | collective-permute-done | bytes 1507360 | tf_op jit(solution)/shard_map/ppermute | solution.py:1031
  688.0 8.0 %collective-permute-done.49 = bf16[128,2944]{1,0:T(8,128)(2,1)S(1)} collective-permute-done((bf16[128,2944]{1,0:T(8,128)(2,1)}, bf16[128,2944]{1,0:T(8,128)(2,1)S(1)}, u32[]{:S(2)}, u32[]{:S(2)}) %collective-permute-start.49) | collective-permute-done | bytes 753696 | tf_op jit(solution)/shard_map/ppermute | solution.py:1051
  696.1 8.1 %collective-permute-done.48 = bf16[128,2944]{1,0:T(8,128)(2,1)} collective-permute-done((bf16[128,2944]{1,0:T(8,128)(2,1)}, bf16[128,2944]{1,0:T(8,128)(2,1)}, u32[]{:S(2)}, u32[]{:S(2)}) %collective-permute-start.48) | collective-permute-done | bytes 753696 | tf_op jit(solution)/shard_map/ppermute | solution.py:1031
  706.7 5.6 collective-permute-done.38.left
  713.2 2.4 ring_add.6.refs_1_
  723.1 2.3 convert_element_type.169.refs_1_
  725.4 2.1 collective-permute-start.44
  727.6 3.8 collective-permute-start.45
  733.7 15.5 %collective-permute-done.44 = bf16[256,512]{0,1:T(8,128)(2,1)S(1)} collective-permute-done((bf16[256,512]{0,1:T(8,128)(2,1)S(1)}, bf16[256,512]{0,1:T(8,128)(2,1)S(1)}, u32[]{:S(2)}, u32[]{:S(2)}) %collective-permute-start.44) | collective-permute-done | bytes 262176 | tf_op jit(solution)/shard_map/ppermute | solution.py:1028
  749.2 11.6 %collective-permute-done.45 = bf16[256,512]{0,1:T(8,128)(2,1)S(1)} collective-permute-done((bf16[256,512]{0,1:T(8,128)(2,1)S(1)}, bf16[256,512]{0,1:T(8,128)(2,1)S(1)}, u32[]{:S(2)}, u32[]{:S(2)}) %collective-permute-start.45) | collective-permute-done | bytes 262176 | tf_op jit(solution)/shard_map/ppermute | solution.py:1028
  760.9 5.7 collective-permute-done.46
  767.5 2.4 ring_add.7
  (292 shorter events, 91.7 us)
Async XLA Ops:
  7.2 95.3 %all-gather.4.cloned.1.call-start = ((), (), s32[]{:S(2)}) async-start(), calls=%async_computation.5 | async-start | bytes 7077888 | tf_op jit(solution)/shard_map/all_gather | solution.py:1071
  11.1 180.6 %all-gather.6.cloned.1.call-start = ((), (), s32[]{:S(2)}) async-start(), calls=%async_computation.6 | async-start | bytes 19464192 | tf_op jit(solution)/shard_map/all_gather | solution.py:1073
  14.3 218.3 %all-gather.8.cloned.1.call-start = ((), (), s32[]{:S(2)}) async-start(), calls=%async_computation.7 | async-start | bytes 9437184 | tf_op jit(solution)/shard_map/all_gather | solution.py:1112
  15.7 17.7 %collective-permute-start = (bf16[640,512]{1,0:T(8,128)(2,1)S(1)}, bf16[640,512]{1,0:T(8,128)(2,1)S(1)}, u32[]{:S(2)}, u32[]{:S(2)}) collective-permute-start(bf16[640,512]{1,0:T(8,128)(2,1)S(1)} %pad_maximum_fusion.1.refs_0_), channel_id=1, source_target_pairs={{0,1},{1,2},{2,3},{3,0},{4,5},{5,6},{6,7},{7,4},{8,9},{9,10},{10,1... | collective-permute-start | bytes 1966088 | tf_op jit(solution)/shard_map/ppermute | solution.py:1028
  17.4 30.0 %collective-permute-start.3 = (bf16[640,512]{1,0:T(8,128)(2,1)S(1)}, bf16[640,512]{1,0:T(8,128)(2,1)S(1)}, u32[]{:S(2)}, u32[]{:S(2)}) collective-permute-start(bf16[640,512]{1,0:T(8,128)(2,1)S(1)} %pad_maximum_fusion.2.refs_4_), channel_id=1, source_target_pairs={{0,1},{1,2},{2,3},{3,0},{4,5},{5,6},{6,7},{7,4},{8,9},{9,10},{10,1... | collective-permute-start | bytes 1966088 | tf_op jit(solution)/shard_map/ppermute | solution.py:1028
  34.3 43.5 %copy-start.44 = (f32[3,512]{1,0:T(4,128)S(1)}, f32[3,512]{1,0:T(4,128)}, u32[]{:S(2)}) copy-start(f32[3,512]{1,0:T(4,128)} %param.19) | copy-start | bytes 18436
  34.3 27.3 %collective-permute-start.1 = (bf16[640,512]{1,0:T(8,128)(2,1)}, bf16[640,512]{1,0:T(8,128)(2,1)}, u32[]{:S(2)}, u32[]{:S(2)}) collective-permute-start(bf16[640,512]{1,0:T(8,128)(2,1)} %tie.17.refs_1_), channel_id=1, source_target_pairs={{0,1},{1,2},{2,3},{3,0},{4,5},{5,6},{6,7},{7,4},{8,9},{9,10},{10,1... | collective-permute-start | bytes 1966088 | tf_op jit(solution)/shard_map/ppermute | solution.py:1028
  48.3 27.2 %collective-permute-start.4 = (bf16[640,512]{1,0:T(8,128)(2,1)}, bf16[640,512]{1,0:T(8,128)(2,1)S(1)}, u32[]{:S(2)}, u32[]{:S(2)}) collective-permute-start(bf16[640,512]{1,0:T(8,128)(2,1)} %tie.18.refs_5_), channel_id=1, source_target_pairs={{0,1},{1,2},{2,3},{3,0},{4,5},{5,6},{6,7},{7,4},{8,9},{9,10},{10,1... | collective-permute-start | bytes 1966088 | tf_op jit(solution)/shard_map/ppermute | solution.py:1028
  61.6 28.0 %collective-permute-start.2 = (bf16[640,512]{1,0:T(8,128)(2,1)}, bf16[640,512]{1,0:T(8,128)(2,1)S(1)}, u32[]{:S(2)}, u32[]{:S(2)}) collective-permute-start(bf16[640,512]{1,0:T(8,128)(2,1)} %collective-permute-done.1.refs_2_), channel_id=1, source_target_pairs={{0,1},{1,2},{2,3},{3,0},{4,5},{5,6},{6,7},{7,4},{8,9},{9,10},{10,1... | collective-permute-start | bytes 1966088 | tf_op jit(solution)/shard_map/ppermute | solution.py:1028
  75.6 26.9 %collective-permute-start.5 = (bf16[640,512]{1,0:T(8,128)(2,1)S(1)}, bf16[640,512]{1,0:T(8,128)(2,1)S(1)}, u32[]{:S(2)}, u32[]{:S(2)}) collective-permute-start(bf16[640,512]{1,0:T(8,128)(2,1)S(1)} %collective-permute-done.4.refs_6_), channel_id=1, source_target_pairs={{0,1},{1,2},{2,3},{3,0},{4,5},{5,6},{6,7},{7,4},{8,9},{9,10},{10,1... | collective-permute-start | bytes 1966088 | tf_op jit(solution)/shard_map/ppermute | solution.py:1028
  124.9 58.2 %collective-permute-start.7 = (bf16[2,1024,384]{2,1,0:T(8,128)(2,1)}, bf16[2,1024,384]{2,1,0:T(8,128)(2,1)}, u32[]{:S(2)}, u32[]{:S(2)}) collective-permute-start(bf16[2,1024,384]{2,1,0:T(8,128)(2,1)} %get-tuple-element.81), channel_id=1, source_target_pairs={{0,8},{4,12},{8,0},{12,4},{1,9},{5,13},{9,1},{13,5},{2,10},{6,14},... | collective-permute-start | bytes 4718600 | tf_op jit(solution)/shard_map/ppermute | solution.py:1031
  127.8 58.2 %copy-start.14 = (bf16[512,512]{1,0:T(8,128)(2,1)}, bf16[512,512]{1,0:T(8,128)(2,1)S(1)}, u32[]{:S(2)}) copy-start(bf16[512,512]{1,0:T(8,128)(2,1)S(1)} %get-tuple-element.211.refs_4_) | copy-start | bytes 1572868
  127.8 58.2 %copy-start.15 = (bf16[512,512]{1,0:T(8,128)(2,1)}, bf16[512,512]{1,0:T(8,128)(2,1)S(1)}, u32[]{:S(2)}) copy-start(bf16[512,512]{1,0:T(8,128)(2,1)S(1)} %get-tuple-element.212.refs_0_) | copy-start | bytes 1572868
  127.8 15.3 %collective-permute-start.10 = (bf16[512,512]{1,0:T(8,128)(2,1)S(1)}, bf16[512,512]{1,0:T(8,128)(2,1)S(1)}, u32[]{:S(2)}, u32[]{:S(2)}) collective-permute-start(bf16[512,512]{1,0:T(8,128)(2,1)S(1)} %get-tuple-element.211.refs_4_), channel_id=1, source_target_pairs={{0,1},{1,2},{2,3},{3,0},{4,5},{5,6},{6,7},{7,4},{8,9},{9,10},{10,1... | collective-permute-start | bytes 1572872 | tf_op jit(solution)/shard_map/ppermute | solution.py:1028
  129.5 24.8 %collective-permute-start.8 = (bf16[512,512]{1,0:T(8,128)(2,1)S(1)}, bf16[512,512]{1,0:T(8,128)(2,1)S(1)}, u32[]{:S(2)}, u32[]{:S(2)}) collective-permute-start(bf16[512,512]{1,0:T(8,128)(2,1)S(1)} %get-tuple-element.212.refs_0_), channel_id=1, source_target_pairs={{0,1},{1,2},{2,3},{3,0},{4,5},{5,6},{6,7},{7,4},{8,9},{9,10},{10,1... | collective-permute-start | bytes 1572872 | tf_op jit(solution)/shard_map/ppermute | solution.py:1028
  143.1 42.9 %copy-start.34 = (bf16[512,512]{1,0:T(8,128)(2,1)}, bf16[512,512]{1,0:T(8,128)(2,1)S(1)}, u32[]{:S(2)}) copy-start(bf16[512,512]{1,0:T(8,128)(2,1)S(1)} %collective-permute-done.10.refs_5_) | copy-start | bytes 1572868
  143.1 43.0 %collective-permute-start.11 = (bf16[512,512]{1,0:T(8,128)(2,1)S(1)}, bf16[512,512]{1,0:T(8,128)(2,1)S(1)}, u32[]{:S(2)}, u32[]{:S(2)}) collective-permute-start(bf16[512,512]{1,0:T(8,128)(2,1)S(1)} %collective-permute-done.10.refs_5_), channel_id=1, source_target_pairs={{0,1},{1,2},{2,3},{3,0},{4,5},{5,6},{6,7},{7,4},{8,9},{9,10},{10,1... | collective-permute-start | bytes 1572872 | tf_op jit(solution)/shard_map/ppermute | solution.py:1028
  154.3 31.7 %collective-permute-start.9 = (bf16[512,512]{1,0:T(8,128)(2,1)S(1)}, bf16[512,512]{1,0:T(8,128)(2,1)S(1)}, u32[]{:S(2)}, u32[]{:S(2)}) collective-permute-start(bf16[512,512]{1,0:T(8,128)(2,1)S(1)} %collective-permute-done.8.refs_1_), channel_id=1, source_target_pairs={{0,1},{1,2},{2,3},{3,0},{4,5},{5,6},{6,7},{7,4},{8,9},{9,10},{10,1... | collective-permute-start | bytes 1572872 | tf_op jit(solution)/shard_map/ppermute | solution.py:1028
  156.1 35.5 %collective-permute-start.6 = (bf16[1024,384]{1,0:T(8,128)(2,1)}, bf16[1024,384]{1,0:T(8,128)(2,1)}, u32[]{:S(2)}, u32[]{:S(2)}) collective-permute-start(bf16[1024,384]{1,0:T(8,128)(2,1)} %get-tuple-element.80), channel_id=1, source_target_pairs={{0,4},{4,0},{8,12},{12,8},{1,5},{5,1},{9,13},{13,9},{2,6},{6,2},{1... | collective-permute-start | bytes 2359304 | tf_op jit(solution)/shard_map/ppermute | solution.py:1031
  187.0 4.7 collective-permute-start.12
  188.7 38.7 %collective-permute-start.13 = (bf16[512,512]{1,0:T(8,128)(2,1)}, bf16[512,512]{1,0:T(8,128)(2,1)S(1)}, u32[]{:S(2)}, u32[]{:S(2)}) collective-permute-start(bf16[512,512]{1,0:T(8,128)(2,1)} %copy-done.13), channel_id=1, source_target_pairs={{0,1},{1,2},{2,3},{3,0},{4,5},{5,6},{6,7},{7,4},{8,9},{9,10},{10,1... | collective-permute-start | bytes 1572872 | tf_op jit(solution)/shard_map/ppermute | solution.py:1028
  190.2 37.2 %collective-permute-start.14 = (bf16[512,512]{1,0:T(8,128)(2,1)}, bf16[512,512]{1,0:T(8,128)(2,1)S(1)}, u32[]{:S(2)}, u32[]{:S(2)}) collective-permute-start(bf16[512,512]{1,0:T(8,128)(2,1)} %copy-done.12), channel_id=1, source_target_pairs={{0,1},{1,2},{2,3},{3,0},{4,5},{5,6},{6,7},{7,4},{8,9},{9,10},{10,1... | collective-permute-start | bytes 1572872 | tf_op jit(solution)/shard_map/ppermute | solution.py:1028
  228.4 28.4 %all-to-all-start = ((bf16[16,256,128]{2,1,0:T(8,128)(2,1)}), bf16[16,256,128]{2,1,0:T(8,128)(2,1)S(1)}, u32[]{:S(2)}, u32[]{:S(2)}) async-start(bf16[16,256,128]{2,1,0:T(8,128)(2,1)} %bitcast.122), calls=%async_computation | async-start | bytes 2097152 | tf_op jit(solution)/shard_map/all_to_all | solution.py:1132
  232.5 391.8 %reduce-scatter.4.cloned.1.call-start = ((), (), s32[]{:S(2)}) async-start(), calls=%async_computation.8 | async-start | bytes 6488064 | tf_op jit(solution)/shard_map/reduce_scatter | solution.py:1048
  267.3 26.0 %collective-permute-start.15 = (bf16[256,2048]{1,0:T(8,128)(2,1)}, bf16[256,2048]{1,0:T(8,128)(2,1)S(1)}, u32[]{:S(2)}, u32[]{:S(2)}) collective-permute-start(bf16[256,2048]{1,0:T(8,128)(2,1)} %get-tuple-element.85.low), channel_id=1, source_target_pairs={{0,1},{1,2},{2,3},{3,0},{4,5},{5,6},{6,7},{7,4},{8,9},{9,10},{10,1... | collective-permute-start | bytes 3145736 | tf_op jit(solution)/shard_map/ppermute | solution.py:1028
  294.3 28.2 %collective-permute-start.16 = (bf16[256,2048]{1,0:T(8,128)(2,1)}, bf16[256,2048]{1,0:T(8,128)(2,1)S(1)}, u32[]{:S(2)}, u32[]{:S(2)}) collective-permute-start(bf16[256,2048]{1,0:T(8,128)(2,1)} %tie.22.low), channel_id=1, source_target_pairs={{0,1},{1,2},{2,3},{3,0},{4,5},{5,6},{6,7},{7,4},{8,9},{9,10},{10,1... | collective-permute-start | bytes 3145736 | tf_op jit(solution)/shard_map/ppermute | solution.py:1028
  312.8 28.4 %collective-permute-start.19 = (bf16[128,2048]{1,0:T(8,128)(2,1)}, bf16[128,2048]{1,0:T(8,128)(2,1)S(1)}, u32[]{:S(2)}, u32[]{:S(2)}) collective-permute-start(bf16[128,2048]{1,0:T(8,128)(2,1)} %get-tuple-element.106), channel_id=1, source_target_pairs={{0,1},{1,2},{2,3},{3,0},{4,5},{5,6},{6,7},{7,4},{8,9},{9,10},{10,1... | collective-permute-start | bytes 1572872 | tf_op jit(solution)/shard_map/ppermute | solution.py:1028
  315.8 29.2 %collective-permute-start.18 = (bf16[128,2048]{1,0:T(8,128)(2,1)}, bf16[128,2048]{1,0:T(8,128)(2,1)S(1)}, u32[]{:S(2)}, u32[]{:S(2)}) collective-permute-start(bf16[128,2048]{1,0:T(8,128)(2,1)} %get-tuple-element.104), channel_id=1, source_target_pairs={{0,1},{1,2},{2,3},{3,0},{4,5},{5,6},{6,7},{7,4},{8,9},{9,10},{10,1... | collective-permute-start | bytes 1572872 | tf_op jit(solution)/shard_map/ppermute | solution.py:1028
  322.5 44.9 %collective-permute-start.17 = (bf16[256,2048]{1,0:T(8,128)(2,1)S(1)}, bf16[256,2048]{1,0:T(8,128)(2,1)S(1)}, u32[]{:S(2)}, u32[]{:S(2)}) collective-permute-start(bf16[256,2048]{1,0:T(8,128)(2,1)S(1)} %collective-permute-done.16.low), channel_id=1, source_target_pairs={{0,1},{1,2},{2,3},{3,0},{4,5},{5,6},{6,7},{7,4},{8,9},{9,10},{10,1... | collective-permute-start | bytes 3145736 | tf_op jit(solution)/shard_map/ppermute | solution.py:1028
  342.4 43.7 %collective-permute-start.22 = (bf16[128,2048]{1,0:T(8,128)(2,1)S(1)}, bf16[128,2048]{1,0:T(8,128)(2,1)S(1)}, u32[]{:S(2)}, u32[]{:S(2)}) collective-permute-start(bf16[128,2048]{1,0:T(8,128)(2,1)S(1)} %add_convert_fusion.4.refs_6_), channel_id=1, source_target_pairs={{0,1},{1,2},{2,3},{3,0},{4,5},{5,6},{6,7},{7,4},{8,9},{9,10},{10,1... | collective-permute-start | bytes 1572872 | tf_op jit(solution)/shard_map/ppermute | solution.py:1028
  345.1 42.8 %collective-permute-start.20 = (bf16[128,2048]{1,0:T(8,128)(2,1)S(1)}, bf16[128,2048]{1,0:T(8,128)(2,1)S(1)}, u32[]{:S(2)}, u32[]{:S(2)}) collective-permute-start(bf16[128,2048]{1,0:T(8,128)(2,1)S(1)} %add_convert_fusion.5.refs_5_), channel_id=1, source_target_pairs={{0,1},{1,2},{2,3},{3,0},{4,5},{5,6},{6,7},{7,4},{8,9},{9,10},{10,1... | collective-permute-start | bytes 1572872 | tf_op jit(solution)/shard_map/ppermute | solution.py:1028
  387.4 24.4 %collective-permute-start.23 = (bf16[128,2048]{1,0:T(8,128)(2,1)S(1)}, bf16[128,2048]{1,0:T(8,128)(2,1)S(1)}, u32[]{:S(2)}, u32[]{:S(2)}) collective-permute-start(bf16[128,2048]{1,0:T(8,128)(2,1)S(1)} %add_convert_fusion.2.refs_1_), channel_id=1, source_target_pairs={{0,1},{1,2},{2,3},{3,0},{4,5},{5,6},{6,7},{7,4},{8,9},{9,10},{10,1... | collective-permute-start | bytes 1572872 | tf_op jit(solution)/shard_map/ppermute | solution.py:1028
  388.1 23.7 %collective-permute-start.21 = (bf16[128,2048]{1,0:T(8,128)(2,1)S(1)}, bf16[128,2048]{1,0:T(8,128)(2,1)S(1)}, u32[]{:S(2)}, u32[]{:S(2)}) collective-permute-start(bf16[128,2048]{1,0:T(8,128)(2,1)S(1)} %add_convert_fusion.3.refs_0_), channel_id=1, source_target_pairs={{0,1},{1,2},{2,3},{3,0},{4,5},{5,6},{6,7},{7,4},{8,9},{9,10},{10,1... | collective-permute-start | bytes 1572872 | tf_op jit(solution)/shard_map/ppermute | solution.py:1028
  424.5 32.2 %all-to-all-start.1 = ((bf16[16,256,128]{2,1,0:T(8,128)(2,1)}), bf16[16,256,128]{2,1,0:T(8,128)(2,1)S(1)}, u32[]{:S(2)}, u32[]{:S(2)}) async-start(bf16[16,256,128]{2,1,0:T(8,128)(2,1)} %bitcast.33), calls=%async_computation.1 | async-start | bytes 2097152 | tf_op jit(solution)/shard_map/all_to_all | solution.py:1185
  432.5 199.3 %reduce-scatter.6.cloned.1.call-start = ((), (), s32[]{:S(2)}) async-start(), calls=%async_computation.9 | async-start | bytes 9437184 | tf_op jit(solution)/shard_map/reduce_scatter | solution.py:1048
  457.7 265.4 %reduce-scatter.8.cloned.1.call-start = ((), (), s32[]{:S(2)}) async-start(), calls=%async_computation.10 | async-start | bytes 6488064 | tf_op jit(solution)/shard_map/reduce_scatter | solution.py:1048
  457.8 61.4 %collective-permute-start.26 = (bf16[1024,1024]{1,0:T(8,128)(2,1)}, bf16[1024,1024]{1,0:T(8,128)(2,1)}, u32[]{:S(2)}, u32[]{:S(2)}) collective-permute-start(bf16[1024,1024]{1,0:T(8,128)(2,1)} %get-tuple-element.116), channel_id=1, source_target_pairs={{0,4},{4,0},{8,12},{12,8},{1,5},{5,1},{9,13},{13,9},{2,6},{6,2},{1... | collective-permute-start | bytes 6291464 | tf_op jit(solution)/shard_map/ppermute | solution.py:1031
  459.5 59.7 %collective-permute-start.27 = (bf16[1024,1408]{1,0:T(8,128)(2,1)S(1)}, bf16[1024,1408]{1,0:T(8,128)(2,1)}, u32[]{:S(2)}, u32[]{:S(2)}) collective-permute-start(bf16[1024,1408]{1,0:T(8,128)(2,1)S(1)} %copy-done), channel_id=1, source_target_pairs={{0,4},{4,0},{8,12},{12,8},{1,5},{5,1},{9,13},{13,9},{2,6},{6,2},{1... | collective-permute-start | bytes 8650760 | tf_op jit(solution)/shard_map/ppermute | solution.py:1031
  462.2 52.2 %collective-permute-start.24 = (bf16[1024,512]{1,0:T(8,128)(2,1)S(1)}, bf16[1024,512]{1,0:T(8,128)(2,1)S(1)}, u32[]{:S(2)}, u32[]{:S(2)}) collective-permute-start(bf16[1024,512]{1,0:T(8,128)(2,1)S(1)} %get-tuple-element.203), channel_id=1, source_target_pairs={{0,1},{1,2},{2,3},{3,0},{4,5},{5,6},{6,7},{7,4},{8,9},{9,10},{10,1... | collective-permute-start | bytes 3145736 | tf_op jit(solution)/shard_map/ppermute | solution.py:1028
  513.2 59.0 %collective-permute-start.30 = (bf16[2,1024,384]{2,1,0:T(8,128)(2,1)}, bf16[2,1024,384]{2,1,0:T(8,128)(2,1)S(1)}, u32[]{:S(2)}, u32[]{:S(2)}) collective-permute-start(bf16[2,1024,384]{2,1,0:T(8,128)(2,1)} %get-tuple-element.125), channel_id=1, source_target_pairs={{0,8},{4,12},{8,0},{12,4},{1,9},{5,13},{9,1},{13,5},{2,10},{6,14},... | collective-permute-start | bytes 4718600 | tf_op jit(solution)/shard_map/ppermute | solution.py:1031
  515.9 25.2 %collective-permute-start.25 = (bf16[1024,512]{1,0:T(8,128)(2,1)S(1)}, bf16[1024,512]{1,0:T(8,128)(2,1)S(1)}, u32[]{:S(2)}, u32[]{:S(2)}) collective-permute-start(bf16[1024,512]{1,0:T(8,128)(2,1)S(1)} %fusion.1), channel_id=1, source_target_pairs={{0,1},{1,2},{2,3},{3,0},{4,5},{5,6},{6,7},{7,4},{8,9},{9,10},{10,1... | collective-permute-start | bytes 3145736 | tf_op jit(solution)/shard_map/ppermute | solution.py:1028
  518.6 57.4 %collective-permute-start.32 = (bf16[1024,1024]{1,0:T(8,128)(2,1)}, bf16[1024,1024]{1,0:T(8,128)(2,1)}, u32[]{:S(2)}, u32[]{:S(2)}) collective-permute-start(bf16[1024,1024]{1,0:T(8,128)(2,1)} %get-tuple-element.127), channel_id=1, source_target_pairs={{0,4},{4,0},{8,12},{12,8},{1,5},{5,1},{9,13},{13,9},{2,6},{6,2},{1... | collective-permute-start | bytes 6291464 | tf_op jit(solution)/shard_map/ppermute | solution.py:1031
  544.8 28.7 %collective-permute-start.28 = (bf16[1024,512]{1,0:T(8,128)(2,1)}, bf16[1024,512]{1,0:T(8,128)(2,1)S(1)}, u32[]{:S(2)}, u32[]{:S(2)}) collective-permute-start(bf16[1024,512]{1,0:T(8,128)(2,1)} %ring_add.4.refs_1_), channel_id=1, source_target_pairs={{0,1},{1,2},{2,3},{3,0},{4,5},{5,6},{6,7},{7,4},{8,9},{9,10},{10,1... | collective-permute-start | bytes 3145736 | tf_op jit(solution)/shard_map/ppermute | solution.py:1028
  547.1 28.9 %collective-permute-start.29 = (bf16[1024,384]{1,0:T(8,128)(2,1)S(1)}, bf16[1024,384]{1,0:T(8,128)(2,1)S(1)}, u32[]{:S(2)}, u32[]{:S(2)}) collective-permute-start(bf16[1024,384]{1,0:T(8,128)(2,1)S(1)} %copy-done.54), channel_id=1, source_target_pairs={{0,4},{4,0},{8,12},{12,8},{1,5},{5,1},{9,13},{13,9},{2,6},{6,2},{1... | collective-permute-start | bytes 2359304 | tf_op jit(solution)/shard_map/ppermute | solution.py:1031
  573.5 2.5 collective-permute-start.31
  596.9 10.3 %collective-permute-start.37 = (bf16[1024,1536]{1,0:T(8,128)(2,1)}, bf16[1024,1536]{1,0:T(8,128)(2,1)}, u32[]{:S(2)}, u32[]{:S(2)}) collective-permute-start(bf16[1024,1536]{1,0:T(8,128)(2,1)} %get-tuple-element.136.right_here), channel_id=1, source_target_pairs={{0,4},{4,0},{8,12},{12,8},{1,5},{5,1},{9,13},{13,9},{2,6},{6,2},{1... | collective-permute-start | bytes 9437192 | tf_op jit(solution)/shard_map/ppermute | solution.py:1031
  598.3 23.8 %collective-permute-start.34 = (f32[1,8192]{1,0:T(1,128)S(1)}, f32[1,8192]{1,0:T(1,128)S(1)}, u32[]{:S(2)}, u32[]{:S(2)}) collective-permute-start(f32[1,8192]{1,0:T(1,128)S(1)} %constant_dynamic-update-slice_fusion), channel_id=1, source_target_pairs={{0,1},{1,2},{2,3},{3,0},{4,5},{5,6},{6,7},{7,4},{8,9},{9,10},{10,1... | collective-permute-start | bytes 98312 | tf_op jit(solution)/shard_map/ppermute | solution.py:1028
  601.9 20.2 %collective-permute-start.35 = (f32[1,8192]{1,0:T(1,128)S(1)}, f32[1,8192]{1,0:T(1,128)S(1)}, u32[]{:S(2)}, u32[]{:S(2)}) collective-permute-start(f32[1,8192]{1,0:T(1,128)S(1)} %constant_dynamic-update-slice_fusion), channel_id=1, source_target_pairs={{0,2},{1,3},{2,0},{3,1},{4,6},{5,7},{6,4},{7,5},{8,10},{9,11},{10,... | collective-permute-start | bytes 98312 | tf_op jit(solution)/shard_map/ppermute | solution.py:1028
  605.2 17.0 %collective-permute-start.36 = (f32[1,8192]{1,0:T(1,128)S(1)}, f32[1,8192]{1,0:T(1,128)S(1)}, u32[]{:S(2)}, u32[]{:S(2)}) collective-permute-start(f32[1,8192]{1,0:T(1,128)S(1)} %constant_dynamic-update-slice_fusion), channel_id=1, source_target_pairs={{0,3},{1,0},{2,1},{3,2},{4,7},{5,4},{6,5},{7,6},{8,11},{9,8},{10,9... | collective-permute-start | bytes 98312 | tf_op jit(solution)/shard_map/ppermute | solution.py:1028
  607.1 24.7 %collective-permute-start.33 = (bf16[1024,512]{1,0:T(8,128)(2,1)S(1)}, bf16[1024,512]{1,0:T(8,128)(2,1)S(1)}, u32[]{:S(2)}, u32[]{:S(2)}) collective-permute-start(bf16[1024,512]{1,0:T(8,128)(2,1)S(1)} %copy-done.52), channel_id=1, source_target_pairs={{0,1},{1,2},{2,3},{3,0},{4,5},{5,6},{6,7},{7,4},{8,9},{9,10},{10,1... | collective-permute-start | bytes 3145736 | tf_op jit(solution)/shard_map/ppermute | solution.py:1028
  621.3 55.2 %collective-permute-start.40 = (bf16[2,128,2944]{2,1,0:T(8,128)(2,1)}, bf16[2,128,2944]{2,1,0:T(8,128)(2,1)}, u32[]{:S(2)}, u32[]{:S(2)}) collective-permute-start(bf16[2,128,2944]{2,1,0:T(8,128)(2,1)} %get-tuple-element.143.refs_6_), channel_id=1, source_target_pairs={{0,8},{4,12},{8,0},{12,4},{1,9},{5,13},{9,1},{13,5},{2,10},{6,14},... | collective-permute-start | bytes 4521992 | tf_op jit(solution)/shard_map/ppermute | solution.py:1031
  622.8 57.9 %collective-permute-start.39 = (bf16[2,128,2944]{2,1,0:T(8,128)(2,1)}, bf16[2,128,2944]{2,1,0:T(8,128)(2,1)}, u32[]{:S(2)}, u32[]{:S(2)}) collective-permute-start(bf16[2,128,2944]{2,1,0:T(8,128)(2,1)} %get-tuple-element.141.refs_4_), channel_id=1, source_target_pairs={{0,16},{16,0},{1,17},{17,1},{2,18},{18,2},{3,19},{19,3},{4,20},{20... | collective-permute-start | bytes 4521992 | tf_op jit(solution)/shard_map/ppermute | solution.py:1051
  635.2 41.4 %copy-start.7 = (bf16[2,128,2944]{2,1,0:T(8,128)(2,1)S(1)}, bf16[2,128,2944]{2,1,0:T(8,128)(2,1)}, u32[]{:S(2)}) copy-start(bf16[2,128,2944]{2,1,0:T(8,128)(2,1)} %tie.28) | copy-start | bytes 4521988
  635.2 45.6 %copy-start.33 = (f32[1,9728]{1,0:T(1,128)S(1)}, f32[1,9728]{1,0:T(1,128)}, u32[]{:S(2)}) copy-start(f32[1,9728]{1,0:T(1,128)} %tie.29) | copy-start | bytes 116740
  679.2 16.8 %collective-permute-start.49 = (bf16[128,2944]{1,0:T(8,128)(2,1)}, bf16[128,2944]{1,0:T(8,128)(2,1)S(1)}, u32[]{:S(2)}, u32[]{:S(2)}) collective-permute-start(bf16[128,2944]{1,0:T(8,128)(2,1)} %slice_bitcast_fusion.4), channel_id=1, source_target_pairs={{0,16},{16,0},{1,17},{17,1},{2,18},{18,2},{3,19},{19,3},{4,20},{20... | collective-permute-start | bytes 2261000 | tf_op jit(solution)/shard_map/ppermute | solution.py:1051
  680.8 1.8 collective-permute-start.41
  682.6 4.7 collective-permute-start.42
  684.8 19.4 %collective-permute-start.48 = (bf16[128,2944]{1,0:T(8,128)(2,1)}, bf16[128,2944]{1,0:T(8,128)(2,1)}, u32[]{:S(2)}, u32[]{:S(2)}) collective-permute-start(bf16[128,2944]{1,0:T(8,128)(2,1)} %slice_bitcast_fusion.6), channel_id=1, source_target_pairs={{0,8},{4,12},{8,0},{12,4},{1,9},{5,13},{9,1},{13,5},{2,10},{6,14},... | collective-permute-start | bytes 2261000 | tf_op jit(solution)/shard_map/ppermute | solution.py:1031
  685.8 26.4 %collective-permute-start.38 = (bf16[1024,512]{1,0:T(8,128)(2,1)S(1)}, bf16[1024,512]{1,0:T(8,128)(2,1)S(1)}, u32[]{:S(2)}, u32[]{:S(2)}) collective-permute-start(bf16[1024,512]{1,0:T(8,128)(2,1)S(1)} %copy-done.3), channel_id=1, source_target_pairs={{0,1},{1,2},{2,3},{3,0},{4,5},{5,6},{6,7},{7,4},{8,9},{9,10},{10,1... | collective-permute-start | bytes 3145736 | tf_op jit(solution)/shard_map/ppermute | solution.py:1028
  715.6 51.9 %collective-permute-start.43 = (bf16[1024,512]{1,0:T(8,128)(2,1)}, bf16[1024,512]{1,0:T(8,128)(2,1)}, u32[]{:S(2)}, u32[]{:S(2)}) collective-permute-start(bf16[1024,512]{1,0:T(8,128)(2,1)} %ring_add.6.refs_1_), channel_id=1, source_target_pairs={{0,1},{1,2},{2,3},{3,0},{4,5},{5,6},{6,7},{7,4},{8,9},{9,10},{10,1... | collective-permute-start | bytes 3145736 | tf_op jit(solution)/shard_map/ppermute | solution.py:1028
  720.7 11.7 %collective-permute-start.47 = (f32[1,9728]{1,0:T(1,128)}, f32[1,9728]{1,0:T(1,128)S(1)}, u32[]{:S(2)}, u32[]{:S(2)}) collective-permute-start(f32[1,9728]{1,0:T(1,128)} %tie.33), channel_id=1, source_target_pairs={{0,16},{16,0},{1,17},{17,1},{2,18},{18,2},{3,19},{19,3},{4,20},{20... | collective-permute-start | bytes 116744 | tf_op jit(solution)/shard_map/ppermute | solution.py:1241
  725.4 23.8 %collective-permute-start.44 = (bf16[256,512]{0,1:T(8,128)(2,1)S(1)}, bf16[256,512]{0,1:T(8,128)(2,1)S(1)}, u32[]{:S(2)}, u32[]{:S(2)}) collective-permute-start(bf16[256,512]{0,1:T(8,128)(2,1)S(1)} %get-tuple-element.208), channel_id=1, source_target_pairs={{0,1},{1,2},{2,3},{3,0},{4,5},{5,6},{6,7},{7,4},{8,9},{9,10},{10,1... | collective-permute-start | bytes 786440 | tf_op jit(solution)/shard_map/ppermute | solution.py:1028
  727.6 33.3 %collective-permute-start.45 = (bf16[256,512]{0,1:T(8,128)(2,1)S(1)}, bf16[256,512]{0,1:T(8,128)(2,1)S(1)}, u32[]{:S(2)}, u32[]{:S(2)}) collective-permute-start(bf16[256,512]{0,1:T(8,128)(2,1)S(1)} %get-tuple-element.210), channel_id=1, source_target_pairs={{0,2},{1,3},{2,0},{3,1},{4,6},{5,7},{6,4},{7,5},{8,10},{9,11},{10,... | collective-permute-start | bytes 786440 | tf_op jit(solution)/shard_map/ppermute | solution.py:1028
  731.3 35.2 %collective-permute-start.46 = (bf16[256,512]{0,1:T(8,128)(2,1)S(1)}, bf16[256,512]{0,1:T(8,128)(2,1)S(1)}, u32[]{:S(2)}, u32[]{:S(2)}) collective-permute-start(bf16[256,512]{0,1:T(8,128)(2,1)S(1)} %get-tuple-element.209), channel_id=1, source_target_pairs={{0,3},{1,0},{2,1},{3,2},{4,7},{5,4},{6,5},{7,6},{8,11},{9,8},{10,9... | collective-permute-start | bytes 786440 | tf_op jit(solution)/shard_map/ppermute | solution.py:1028
  (52 other events, 318.8 us)
Sparse Core Ops, SparseCore 0:
  11.2 46.6 all-gather.3
  59.8 113.7 all-gather.5
  176.1 54.3 all-gather.7
  424.6 63.2 reduce-scatter.3
  491.6 93.6 reduce-scatter.5
  597.7 84.5 reduce-scatter.7

commit v2 on v0

--- a/solution.py
+++ b/solution.py
@@ -1190,9 +1190,9 @@
     ).reshape(nctx * block_rows, piece)
 
     total_gate = scatter(tie(half_gate, mixed_low), 0).astype(F32)
+    total_up = scatter(tie(half_up, mixed_low), 0).astype(F32)
     half_out = blame(mixed_low, returned)
     total_out = scatter(tie(half_out, grad_heads), 0)
-    total_up = scatter(tie(half_up, grad_heads), 0)
 
     feedforward = tie(feedforward, grad_heads)
     inner = hidden.shape[1]
@@ -1248,12 +1248,12 @@
     small = jnp.concatenate([bias_grad, small], axis=1)
     travelling, ring_steps = partial[1 % tp], []
     once = square_once(parts) if square else ()
-    needed = [[total_gate, total_out, small, *parts], [*once], []]
+    needed = [[total_gate, total_up, small, *parts], [*once], []]
     for step in range(1, tp):
         travelling = add(
             shift(travelling, 1), partial[(step + 1) % tp], *(needed[step - 1] if step < 4 else [])
         )
-        if step == 2:
+        if step == 1:
             out_parts = jnp.swapaxes(
                 tie(total_out, travelling).reshape(-1, tp, head_width), 0, 1
             )
@@ -1261,14 +1261,12 @@
             for ahead in range(1, tp):
                 total_out = total_out + shift(pick(out_parts, (tensor_index + ahead) % tp), ahead).astype(F32)
             total_out = total_out.T
-            total_up = tie(total_up, travelling).astype(F32)
-            needed[2].extend([total_out, total_up])
-        if step == 1:
-            small = exchange(tie(small, travelling), "ctx", powers(0, nctx), nctx)
-            needed[1].append(small)
-        if step == 2:
-            small = exchange(tie(small, travelling), "fsdp", powers(0, nfsdp), nfsdp)
-            needed[2].append(small)
+            needed[2].append(total_out)
+        if step < 3:
+            bits = powers(0, min(nctx, 2)) if step == 1 else powers(1, nctx)
+            small = exchange(tie(small, travelling), "ctx", bits, nctx)
+            needed[step].append(small)
+    small = exchange(tie(small, travelling), "fsdp", powers(0, nfsdp), nfsdp)
     grad_inputs = travelling
     if square:
         totals = square_twice(*once)

time: 791 us -> 764 us (0.966)
  Pallas kernels: 307 us -> 293 us
  waiting for transfers between devices: 302 us -> 290 us
  local copies, waits for them, and re-layouts: 52.8 us -> 42.2 us
    unnamed x113 -> x110, local copies, waits for them, and re-layouts: 34.6 us -> 24.8 us
    ppermute x33, waiting for transfers between devices: 156 us -> 148 us  [shift(): return lax.ppermute(value, 'tp', [(i, (i + step) % tp) for i in range(tp)])]
    all_to_all x1, waiting for transfers between devices: 8.66 us -> 17 us  [shards(): lax.all_to_all(grad_heads.reshape(nctx * tp, part_rows, piece), ('ctx', '...]
    pallas_call x1, Pallas kernels: 58.5 us -> 50.1 us  [attend_back(): pl.pallas_call(functools.partial(attend_back_kernel, nctx, heads, len(pie...]
  transfers between devices with their start and end apart: 58 -> 58, of which waited for: 27 -> 27; matrix products, arithmetic and copies ran while one was open for 8% -> 7% of each run, Pallas kernels for 36% -> 36%
where the time goes in v2:
time: 764 us; the launch traced here: 754 us
  Pallas kernels  293 us (38%)
  waiting for transfers between devices  290 us (38%)
  starting transfers between devices  79.2 us (10%)
  local copies, waits for them, and re-layouts  42.2 us (6%)
  other arithmetic  34.6 us (5%)
  between operations  15 us (2%)
    ppermute x33, waiting for transfers between devices, shift(): return lax.ppermute(value, 'tp', [(i, (i + step) % tp) for i in range(tp)])  148 us
    ppermute x12, waiting for transfers between devices, swap(): return lax.ppermute(value, 'ctx', [(i, i ^ step) for i in range(nctx)])  93.9 us
    pallas_call x4, Pallas kernels, feed(): pl.pallas_call(functools.partial(feed_kernel, tuple(cuts), parts, tp, ste...  70.8 us
    ppermute x33, starting transfers between devices, shift(): return lax.ppermute(value, 'tp', [(i, (i + step) % tp) for i in range(tp)])  54.9 us
    pallas_call x1, Pallas kernels, attend_back(): pl.pallas_call(functools.partial(attend_back_kernel, nctx, heads, len(pie...  50.1 us
    pallas_call x1, Pallas kernels, attend(): pl.pallas_call(functools.partial(attend_kernel, nctx, heads, len(pieces),...  34.8 us
    pallas_call x3, Pallas kernels, blame(): pl.pallas_call(kernel, grid=(steps,), in_specs=in_specs + anywhere(len(ne...  28 us
    pallas_call x2, Pallas kernels, blame_halves(): pl.pallas_call(kernel, grid_spec=grid_spec, out_shape=[jax.ShapeDtypeStru...  27.5 us
  transfers between devices with their start and end apart: 58, of which 27 were waited for; matrix products, arithmetic and copies ran while one was open for 7% of the time, Pallas kernels for 36%

profile of v2, /device:TPU:8, one launch (start us, length us, event | category | flops | bytes accessed | tf_op | source)
XLA Modules:
  0.0 754.2 jit_solution(15795006852571710166)
XLA Ops:
  7.2 2.3 copy.131.refs_0_
  11.1 3.1 pack.1.refs_1_
  19.6 13.8 %collective-permute-done.refs_0_ = bf16[640,512]{1,0:T(8,128)(2,1)S(1)} collective-permute-done((bf16[640,512]{1,0:T(8,128)(2,1)S(1)}, bf16[640,512]{1,0:T(8,128)(2,1)S(1)}, u32[]{:S(2)}, u32[]{:S(2)}) %collective-permute-start) | collective-permute-done | bytes 655392 | tf_op jit(solution)/shard_map/ppermute | solution.py:1028
  35.8 11.6 %collective-permute-done.3.refs_0_ = bf16[640,512]{1,0:T(8,128)(2,1)S(1)} collective-permute-done((bf16[640,512]{1,0:T(8,128)(2,1)S(1)}, bf16[640,512]{1,0:T(8,128)(2,1)S(1)}, u32[]{:S(2)}, u32[]{:S(2)}) %collective-permute-start.3) | collective-permute-done | bytes 655392 | tf_op jit(solution)/shard_map/ppermute | solution.py:1028
  50.1 11.5 %collective-permute-done.1.refs_2_ = bf16[640,512]{1,0:T(8,128)(2,1)} collective-permute-done((bf16[640,512]{1,0:T(8,128)(2,1)}, bf16[640,512]{1,0:T(8,128)(2,1)}, u32[]{:S(2)}, u32[]{:S(2)}) %collective-permute-start.1) | collective-permute-done | bytes 655392 | tf_op jit(solution)/shard_map/ppermute | solution.py:1028
  63.2 12.4 %collective-permute-done.4.refs_6_ = bf16[640,512]{1,0:T(8,128)(2,1)S(1)} collective-permute-done((bf16[640,512]{1,0:T(8,128)(2,1)}, bf16[640,512]{1,0:T(8,128)(2,1)S(1)}, u32[]{:S(2)}, u32[]{:S(2)}) %collective-permute-start.4) | collective-permute-done | bytes 655392 | tf_op jit(solution)/shard_map/ppermute | solution.py:1028
  78.7 3.2 fusion.4
  81.9 7.7 %collective-permute-done.2.refs_3_.refs_1_ = bf16[640,512]{1,0:T(8,128)(2,1)S(1)} collective-permute-done((bf16[640,512]{1,0:T(8,128)(2,1)}, bf16[640,512]{1,0:T(8,128)(2,1)S(1)}, u32[]{:S(2)}, u32[]{:S(2)}) %collective-permute-start.2) | collective-permute-done | bytes 655392 | tf_op jit(solution)/shard_map/ppermute | solution.py:1028
  89.6 12.9 %collective-permute-done.5.refs_7_.refs_2_ = bf16[640,512]{1,0:T(8,128)(2,1)S(1)} collective-permute-done((bf16[640,512]{1,0:T(8,128)(2,1)S(1)}, bf16[640,512]{1,0:T(8,128)(2,1)S(1)}, u32[]{:S(2)}, u32[]{:S(2)}) %collective-permute-start.5) | collective-permute-done | bytes 655392 | tf_op jit(solution)/shard_map/ppermute | solution.py:1028
  103.3 21.5 %project.1 = (bf16[1024,2048]{1,0:T(8,128)(2,1)}, bf16[1024,2048]{1,0:T(8,128)(2,1)}, bf16[1024,1024]{1,0:T(8,128)(2,1)}, bf16[1024,384]{1,0:T(8,128)(2,1)}, bf1...) custom-call(s32[3]{0:T(128)} %pad_add_fusion.1.place, ...), custom_call_target="tpu_custom_call" | custom-call | flops 6000000000 | tf_op jit(solution)/shard_map/project/pallas_call | solution.py:225
  131.2 11.9 %collective-permute-done.10.refs_5_ = bf16[512,512]{1,0:T(8,128)(2,1)S(1)} collective-permute-done((bf16[512,512]{1,0:T(8,128)(2,1)S(1)}, bf16[512,512]{1,0:T(8,128)(2,1)S(1)}, u32[]{:S(2)}, u32[]{:S(2)}) %collective-permute-start.10) | collective-permute-done | bytes 524320 | tf_op jit(solution)/shard_map/ppermute | solution.py:1028
  144.4 9.9 %collective-permute-done.8.refs_1_ = bf16[512,512]{1,0:T(8,128)(2,1)S(1)} collective-permute-done((bf16[512,512]{1,0:T(8,128)(2,1)S(1)}, bf16[512,512]{1,0:T(8,128)(2,1)S(1)}, u32[]{:S(2)}, u32[]{:S(2)}) %collective-permute-start.8) | collective-permute-done | bytes 524320 | tf_op jit(solution)/shard_map/ppermute | solution.py:1028
  156.1 27.0 %collective-permute-done.7 = bf16[2,1024,384]{2,1,0:T(8,128)(2,1)} collective-permute-done((bf16[2,1024,384]{2,1,0:T(8,128)(2,1)}, bf16[2,1024,384]{2,1,0:T(8,128)(2,1)}, u32[]{:S(2)}, u32[]{:S(2)}) %collective-permute-start.7) | collective-permute-done | bytes 1572896 | tf_op jit(solution)/shard_map/ppermute | solution.py:1031
  183.1 2.9 slice_bitcast_fusion.2
  191.8 34.8 %attend.1 = (bf16[4096,128]{1,0:T(8,128)(2,1)}, bf16[4096,128]{1,0:T(8,128)(2,1)}, f32[2,4096]{1,0:T(2,128)}) custom-call(s32[1]{0:T(128)} %bitcast.1.place, s32[8]{0:T(128)} %fusion.27.lows, s32[8]{0:T(128)} %multiply_add_fusion.ends, s32[2,4096]{1,0:T(2,128)} %pad_add_fusion.bounds, bf16[1024,384]{1,0:T(8,128)(2,1)} %get-tuple-element.79.refs_0_, ...), custom_call_target="tpu_custom_call" | custom-call | flops 20000000000 | tf_op jit(solution)/shard_map/attend/pallas_call | solution.py:360
  227.6 4.2 all-to-all-start
  231.8 24.2 %all-to-all-done = bf16[16,256,128]{2,1,0:T(8,128)(2,1)S(1)} async-done(((bf16[16,256,128]{2,1,0:T(8,128)(2,1)}), bf16[16,256,128]{2,1,0:T(8,128)(2,1)S(1)}, u32[]{:S(2)}, u32[]{:S(2)}) %all-to-all-start) | async-done | bytes 1048608 | tf_op jit(solution)/shard_map/all_to_all | solution.py:1131
  256.9 9.5 %mix.1 = (bf16[256,2048]{1,0:T(8,128)(2,1)}, f32[256,2048]{1,0:T(8,128)}, bf16[256,2048]{1,0:T(8,128)(2,1)}) custom-call(s32[3]{0:T(128)} %pad_add_fusion.1.place, bf16[4,4,256,128]{3,2,1,0:T(8,128)(2,1)} %bitcast.124, bf16[4,2048,512]{2,1,0:T(8,128)(2,1)} %all-gather.8.cloned.1.call-done.weight.refs_7_, ...), custom_call_target="tpu_custom_call" | custom-call | flops 5000000000 | tf_op jit(solution)/shard_map/mix/pallas_call | solution.py:533
  267.1 6.0 join.1
  273.1 17.7 %feed.4 = (bf16[1024,2048]{1,0:T(8,128)(2,1)}, bf16[1024,1408]{1,0:T(8,128)(2,1)}, bf16[1024,1408]{1,0:T(8,128)(2,1)}, bf16[1024,1408]{1,0:T(8,128)(2,1)}, bf16[...) custom-call(s32[3]{0:T(128)} %pad_add_fusion.1.place, ...), custom_call_target="tpu_custom_call" | custom-call | flops 10000000000 | tf_op jit(solution)/shard_map/feed/pallas_call | solution.py:623
  294.3 17.7 %feed.5 = (bf16[1024,2048]{1,0:T(8,128)(2,1)}, bf16[1024,1408]{1,0:T(8,128)(2,1)}, bf16[1024,1408]{1,0:T(8,128)(2,1)}, bf16[1024,1408]{1,0:T(8,128)(2,1)}, bf16[...) custom-call(s32[3]{0:T(128)} %pad_add_fusion.1.place, ...), custom_call_target="tpu_custom_call", output_to_operand_aliasing={{0}: (5, {}), {1}: (6, {}), {2}: (7, {}), {3}: (8, {}), {4}... | custom-call | flops 10000000000 | tf_op jit(solution)/shard_map/feed/pallas_call | solution.py:623
  312.0 3.0 collective-permute-start.19
  315.0 3.0 collective-permute-start.18
  318.1 3.6 collective-permute-done.16.low
  322.7 17.7 %feed.6 = (bf16[1024,2048]{1,0:T(8,128)(2,1)}, bf16[1024,1408]{1,0:T(8,128)(2,1)}, bf16[1024,1408]{1,0:T(8,128)(2,1)}, bf16[1024,1408]{1,0:T(8,128)(2,1)}, bf16[...) custom-call(s32[3]{0:T(128)} %pad_add_fusion.1.place, ...), custom_call_target="tpu_custom_call", output_to_operand_aliasing={{0}: (5, {}), {1}: (6, {}), {2}: (7, {}), {3}: (8, {}), {4}... | custom-call | flops 10000000000 | tf_op jit(solution)/shard_map/feed/pallas_call | solution.py:623
  345.4 3.6 collective-permute-start.20
  349.0 17.7 %collective-permute-done.17.low = bf16[256,2048]{1,0:T(8,128)(2,1)S(1)} collective-permute-done((bf16[256,2048]{1,0:T(8,128)(2,1)S(1)}, bf16[256,2048]{1,0:T(8,128)(2,1)S(1)}, u32[]{:S(2)}, u32[]{:S(2)}) %collective-permute-start.17) | collective-permute-done | bytes 1048608 | tf_op jit(solution)/shard_map/ppermute | solution.py:1028
  367.6 17.8 %feed.7 = (bf16[1024,2048]{1,0:T(8,128)(2,1)}, bf16[1024,1408]{1,0:T(8,128)(2,1)}, bf16[1024,1408]{1,0:T(8,128)(2,1)}, bf16[1024,1408]{1,0:T(8,128)(2,1)}, bf16[...) custom-call(s32[3]{0:T(128)} %pad_add_fusion.1.place, ...), custom_call_target="tpu_custom_call", output_to_operand_aliasing={{0}: (5, {}), {1}: (6, {}), {2}: (7, {}), {3}: (8, {}), {4}... | custom-call | flops 10000000000 | tf_op jit(solution)/shard_map/feed/pallas_call | solution.py:623
  388.6 2.1 collective-permute-start.21
  390.7 10.7 %blame.4.refs_9_.refs_0_ = bf16[2048,1408]{1,0:T(8,128)(2,1)} custom-call(bf16[1024,2048]{1,0:T(8,128)(2,1)} %get-tuple-element.112.left, bf16[1024,1408]{1,0:T(8,128)(2,1)} %get-tuple-element.114.right, bf16[128,2048]{1,0:T(8,128)(2,1)} %copy-done.38, bf16[128,2048]{1,0:T(8,128)(2,1)} %copy-done.37), custom_call_target="tpu_custom_call" | custom-call | flops 6000000000 | tf_op jit(solution)/shard_map/blame/pallas_call | solution.py:726
  401.4 10.6 %blame.3.refs_8_.refs_0_ = bf16[2048,1408]{1,0:T(8,128)(2,1)} custom-call(bf16[1024,2048]{1,0:T(8,128)(2,1)} %get-tuple-element.112.left, bf16[1024,1408]{1,0:T(8,128)(2,1)} %get-tuple-element.113.right, bf16[128,2048]{1,0:T(8,128)(2,1)} %copy-done.38, bf16[128,2048]{1,0:T(8,128)(2,1)} %copy-done.37), custom_call_target="tpu_custom_call" | custom-call | flops 6000000000 | tf_op jit(solution)/shard_map/blame/pallas_call | solution.py:726
  413.0 11.7 %turn.1 = (bf16[4,4,256,128]{3,2,1,0:T(8,128)(2,1)}, f32[256,2048]{1,0:T(8,128)}, bf16[256,2048]{1,0:T(8,128)(2,1)}, f32[1,2048]{1,0:T(1,128)}, f32[1,2048]{1,0:T(1,128)}, /*index=5*/bf16[256,1024]{1,0:T(8,128)(2,1)}) custom-call(s32[3]{0:T(128)} %pad_add_fusion.1.place, bf16[128,2048]{1,0:T(8,128)(2,1)} %copy-done.36, bf16[128,2048]{1,0:T(8,128)(2,1)} %copy-done.35, ...), custom_call_target="tpu_custom_call" | custom-call | flops 6000000000 | tf_op jit(solution)/shard_map/turn/pallas_call | solution.py:798
  425.3 8.2 %all-to-all-start.1 = ((bf16[16,256,128]{2,1,0:T(8,128)(2,1)}), bf16[16,256,128]{2,1,0:T(8,128)(2,1)}, u32[]{:S(2)}, u32[]{:S(2)}) async-start(bf16[16,256,128]{2,1,0:T(8,128)(2,1)} %bitcast.123), calls=%async_computation.1 | async-start | bytes 2097152 | tf_op jit(solution)/shard_map/all_to_all | solution.py:1184
  434.1 6.7 blame.5.refs_6_.refs_0_
  440.8 17.0 %all-to-all-done.1 = bf16[16,256,128]{2,1,0:T(8,128)(2,1)} async-done(((bf16[16,256,128]{2,1,0:T(8,128)(2,1)}), bf16[16,256,128]{2,1,0:T(8,128)(2,1)}, u32[]{:S(2)}, u32[]{:S(2)}) %all-to-all-start.1) | async-done | bytes 1048608 | tf_op jit(solution)/shard_map/all_to_all | solution.py:1184
  457.8 2.6 dynamic-slice_bitcast_fusion
  461.0 50.1 %attend_back.1 = (bf16[1024,384]{1,0:T(8,128)(2,1)}, bf16[1024,384]{1,0:T(8,128)(2,1)}, bf16[2,1024,384]{2,1,0:T(8,128)(2,1)}) custom-call(s32[1]{0:T(128)} %bitcast.1.place, s32[8]{0:T(128)} %fusion.27.lows, s32[8]{0:T(128)} %multiply_add_fusion.ends, s32[2,4096]{1,0:T(2,128)} %pad_add_fusion.bounds, f32[2,4096]{1,0:T(2,128)} %get-tuple-element.119.logs, ...), custom_call_target="tpu_custom_call" | custom-call | flops 24999999488 | tf_op jit(solution)/shard_map/attend_back/pallas_call | solution.py:476
  514.1 2.5 collective-permute-start.25
  517.3 14.1 %blame_halves.2 = (bf16[2,128,2944]{2,1,0:T(8,128)(2,1)}, bf16[2,128,2944]{2,1,0:T(8,128)(2,1)}, bf16[2,128,2944]{2,1,0:T(8,128)(2,1)}, bf16[2,128,2944]{2,1,0:T(8,128)(2,1)}) custom-call(s32[4]{0:T(128)} %pad_add_fusion.2.place, bf16[4,1024,512]{2,1,0:T(8,128)(2,1)} %get-tuple-element.86.cot.refs_5_.left_here, ...), custom_call_target="tpu_custom_call" | custom-call | flops 6000000000 | tf_op jit(solution)/shard_map/blame_halves/pallas_call | solution.py:698
  531.4 7.5 collective-permute-done.25.left
  539.8 2.5 ring_add.4.refs_1_
  542.3 2.5 collective-permute-start.28
  544.8 21.7 %collective-permute-done.30 = bf16[2,1024,384]{2,1,0:T(8,128)(2,1)S(1)} collective-permute-done((bf16[2,1024,384]{2,1,0:T(8,128)(2,1)}, bf16[2,1024,384]{2,1,0:T(8,128)(2,1)S(1)}, u32[]{:S(2)}, u32[]{:S(2)}) %collective-permute-start.30) | collective-permute-done | bytes 1572896 | tf_op jit(solution)/shard_map/ppermute | solution.py:1031
  568.5 2.5 fusion.refs_11_
  572.1 19.8 %finish.1 = (bf16[1024,512]{1,0:T(8,128)(2,1)}, bf16[1024,512]{1,0:T(8,128)(2,1)}, bf16[1024,512]{1,0:T(8,128)(2,1)}, bf16[1024,512]{1,0:T(8,128)(2,1)}, bf16[10...) custom-call(s32[3]{0:T(128)} %pad_add_fusion.1.place, ...), custom_call_target="tpu_custom_call" | custom-call | flops 7000000000 | tf_op jit(solution)/shard_map/finish/pallas_call | solution.py:910
  593.4 3.1 collective-permute-start.34
  596.5 3.1 collective-permute-start.35
  599.6 1.9 collective-permute-start.36
  603.3 13.4 %blame_halves.3 = (bf16[2,128,2944]{2,1,0:T(8,128)(2,1)}, bf16[2,128,2944]{2,1,0:T(8,128)(2,1)}, bf16[2,128,2944]{2,1,0:T(8,128)(2,1)}, bf16[2,128,2944]{2,1,0:T(8,128)(2,1)}) custom-call(s32[4]{0:T(128)} %pad_add_fusion.2.place, ...), custom_call_target="tpu_custom_call", output_to_operand_aliasing={{0}: (5, {}), {1}: (6, {}), {2}: (7, {}), {3}: (8, {})} | custom-call | flops 6000000000 | tf_op jit(solution)/shard_map/blame_halves/pallas_call | solution.py:698
  618.8 2.3 convert_element_type.158.refs_1_
  621.2 2.3 convert_element_type.157.refs_0_
  623.5 2.8 collective-permute-done.33.left
  627.3 2.6 ring_add.5.refs_1_
  634.1 37.7 %collective-permute-done.40 = bf16[2,128,2944]{2,1,0:T(8,128)(2,1)} collective-permute-done((bf16[2,128,2944]{2,1,0:T(8,128)(2,1)}, bf16[2,128,2944]{2,1,0:T(8,128)(2,1)}, u32[]{:S(2)}, u32[]{:S(2)}) %collective-permute-start.40) | collective-permute-done | bytes 1507360 | tf_op jit(solution)/shard_map/ppermute | solution.py:1031
  679.0 2.5 ring_add.6.refs_1_
  687.1 6.1 collective-permute-done.49
  694.5 7.5 collective-permute-done.48
  703.4 2.3 copy.88
  708.0 3.4 collective-permute-start.44
  712.6 13.4 %collective-permute-done.43 = bf16[256,512]{0,1:T(8,128)(2,1)S(1)} collective-permute-done((bf16[256,512]{0,1:T(8,128)(2,1)S(1)}, bf16[256,512]{0,1:T(8,128)(2,1)S(1)}, u32[]{:S(2)}, u32[]{:S(2)}) %collective-permute-start.43) | collective-permute-done | bytes 262176 | tf_op jit(solution)/shard_map/ppermute | solution.py:1028
  726.0 4.0 collective-permute-done.44
  730.0 3.5 collective-permute-done.45
  735.4 2.4 ring_add.7.refs_1_
  740.7 3.0 copy.92
  (275 shorter events, 96.8 us)
Async XLA Ops:
  7.2 95.3 %all-gather.4.cloned.1.call-start = ((), (), s32[]{:S(2)}) async-start(), calls=%async_computation.5 | async-start | bytes 7077888 | tf_op jit(solution)/shard_map/all_gather | solution.py:1070
  11.1 180.7 %all-gather.6.cloned.1.call-start = ((), (), s32[]{:S(2)}) async-start(), calls=%async_computation.6 | async-start | bytes 19464192 | tf_op jit(solution)/shard_map/all_gather | solution.py:1072
  14.3 217.5 %all-gather.8.cloned.1.call-start = ((), (), s32[]{:S(2)}) async-start(), calls=%async_computation.7 | async-start | bytes 9437184 | tf_op jit(solution)/shard_map/all_gather | solution.py:1111
  15.7 17.7 %collective-permute-start = (bf16[640,512]{1,0:T(8,128)(2,1)S(1)}, bf16[640,512]{1,0:T(8,128)(2,1)S(1)}, u32[]{:S(2)}, u32[]{:S(2)}) collective-permute-start(bf16[640,512]{1,0:T(8,128)(2,1)S(1)} %pad_maximum_fusion.1.refs_0_), channel_id=1, source_target_pairs={{0,1},{1,2},{2,3},{3,0},{4,5},{5,6},{6,7},{7,4},{8,9},{9,10},{10,1... | collective-permute-start | bytes 1966088 | tf_op jit(solution)/shard_map/ppermute | solution.py:1028
  17.4 30.0 %collective-permute-start.3 = (bf16[640,512]{1,0:T(8,128)(2,1)S(1)}, bf16[640,512]{1,0:T(8,128)(2,1)S(1)}, u32[]{:S(2)}, u32[]{:S(2)}) collective-permute-start(bf16[640,512]{1,0:T(8,128)(2,1)S(1)} %pad_maximum_fusion.2.refs_4_), channel_id=1, source_target_pairs={{0,1},{1,2},{2,3},{3,0},{4,5},{5,6},{6,7},{7,4},{8,9},{9,10},{10,1... | collective-permute-start | bytes 1966088 | tf_op jit(solution)/shard_map/ppermute | solution.py:1028
  34.2 43.5 %copy-start.40 = (f32[3,512]{1,0:T(4,128)S(1)}, f32[3,512]{1,0:T(4,128)}, u32[]{:S(2)}) copy-start(f32[3,512]{1,0:T(4,128)} %param.19) | copy-start | bytes 18436
  34.2 27.3 %collective-permute-start.1 = (bf16[640,512]{1,0:T(8,128)(2,1)}, bf16[640,512]{1,0:T(8,128)(2,1)}, u32[]{:S(2)}, u32[]{:S(2)}) collective-permute-start(bf16[640,512]{1,0:T(8,128)(2,1)} %tie.15.refs_1_), channel_id=1, source_target_pairs={{0,1},{1,2},{2,3},{3,0},{4,5},{5,6},{6,7},{7,4},{8,9},{9,10},{10,1... | collective-permute-start | bytes 1966088 | tf_op jit(solution)/shard_map/ppermute | solution.py:1028
  48.3 27.2 %collective-permute-start.4 = (bf16[640,512]{1,0:T(8,128)(2,1)}, bf16[640,512]{1,0:T(8,128)(2,1)S(1)}, u32[]{:S(2)}, u32[]{:S(2)}) collective-permute-start(bf16[640,512]{1,0:T(8,128)(2,1)} %tie.16.refs_5_), channel_id=1, source_target_pairs={{0,1},{1,2},{2,3},{3,0},{4,5},{5,6},{6,7},{7,4},{8,9},{9,10},{10,1... | collective-permute-start | bytes 1966088 | tf_op jit(solution)/shard_map/ppermute | solution.py:1028
  61.6 28.0 %collective-permute-start.2 = (bf16[640,512]{1,0:T(8,128)(2,1)}, bf16[640,512]{1,0:T(8,128)(2,1)S(1)}, u32[]{:S(2)}, u32[]{:S(2)}) collective-permute-start(bf16[640,512]{1,0:T(8,128)(2,1)} %collective-permute-done.1.refs_2_), channel_id=1, source_target_pairs={{0,1},{1,2},{2,3},{3,0},{4,5},{5,6},{6,7},{7,4},{8,9},{9,10},{10,1... | collective-permute-start | bytes 1966088 | tf_op jit(solution)/shard_map/ppermute | solution.py:1028
  75.5 26.9 %collective-permute-start.5 = (bf16[640,512]{1,0:T(8,128)(2,1)S(1)}, bf16[640,512]{1,0:T(8,128)(2,1)S(1)}, u32[]{:S(2)}, u32[]{:S(2)}) collective-permute-start(bf16[640,512]{1,0:T(8,128)(2,1)S(1)} %collective-permute-done.4.refs_6_), channel_id=1, source_target_pairs={{0,1},{1,2},{2,3},{3,0},{4,5},{5,6},{6,7},{7,4},{8,9},{9,10},{10,1... | collective-permute-start | bytes 1966088 | tf_op jit(solution)/shard_map/ppermute | solution.py:1028
  124.9 58.2 %collective-permute-start.7 = (bf16[2,1024,384]{2,1,0:T(8,128)(2,1)}, bf16[2,1024,384]{2,1,0:T(8,128)(2,1)}, u32[]{:S(2)}, u32[]{:S(2)}) collective-permute-start(bf16[2,1024,384]{2,1,0:T(8,128)(2,1)} %get-tuple-element.81), channel_id=1, source_target_pairs={{0,8},{4,12},{8,0},{12,4},{1,9},{5,13},{9,1},{13,5},{2,10},{6,14},... | collective-permute-start | bytes 4718600 | tf_op jit(solution)/shard_map/ppermute | solution.py:1031
  127.7 59.3 %copy-start.13 = (bf16[512,512]{1,0:T(8,128)(2,1)}, bf16[512,512]{1,0:T(8,128)(2,1)S(1)}, u32[]{:S(2)}) copy-start(bf16[512,512]{1,0:T(8,128)(2,1)S(1)} %get-tuple-element.211.refs_4_) | copy-start | bytes 1572868
  127.7 59.3 %copy-start.14 = (bf16[512,512]{1,0:T(8,128)(2,1)}, bf16[512,512]{1,0:T(8,128)(2,1)S(1)}, u32[]{:S(2)}) copy-start(bf16[512,512]{1,0:T(8,128)(2,1)S(1)} %get-tuple-element.212.refs_0_) | copy-start | bytes 1572868
  127.8 15.3 %collective-permute-start.10 = (bf16[512,512]{1,0:T(8,128)(2,1)S(1)}, bf16[512,512]{1,0:T(8,128)(2,1)S(1)}, u32[]{:S(2)}, u32[]{:S(2)}) collective-permute-start(bf16[512,512]{1,0:T(8,128)(2,1)S(1)} %get-tuple-element.211.refs_4_), channel_id=1, source_target_pairs={{0,1},{1,2},{2,3},{3,0},{4,5},{5,6},{6,7},{7,4},{8,9},{9,10},{10,1... | collective-permute-start | bytes 1572872 | tf_op jit(solution)/shard_map/ppermute | solution.py:1028
  129.5 24.8 %collective-permute-start.8 = (bf16[512,512]{1,0:T(8,128)(2,1)S(1)}, bf16[512,512]{1,0:T(8,128)(2,1)S(1)}, u32[]{:S(2)}, u32[]{:S(2)}) collective-permute-start(bf16[512,512]{1,0:T(8,128)(2,1)S(1)} %get-tuple-element.212.refs_0_), channel_id=1, source_target_pairs={{0,1},{1,2},{2,3},{3,0},{4,5},{5,6},{6,7},{7,4},{8,9},{9,10},{10,1... | collective-permute-start | bytes 1572872 | tf_op jit(solution)/shard_map/ppermute | solution.py:1028
  143.1 44.0 %copy-start.33 = (bf16[512,512]{1,0:T(8,128)(2,1)}, bf16[512,512]{1,0:T(8,128)(2,1)S(1)}, u32[]{:S(2)}) copy-start(bf16[512,512]{1,0:T(8,128)(2,1)S(1)} %collective-permute-done.10.refs_5_) | copy-start | bytes 1572868
  143.1 43.0 %collective-permute-start.11 = (bf16[512,512]{1,0:T(8,128)(2,1)S(1)}, bf16[512,512]{1,0:T(8,128)(2,1)S(1)}, u32[]{:S(2)}, u32[]{:S(2)}) collective-permute-start(bf16[512,512]{1,0:T(8,128)(2,1)S(1)} %collective-permute-done.10.refs_5_), channel_id=1, source_target_pairs={{0,1},{1,2},{2,3},{3,0},{4,5},{5,6},{6,7},{7,4},{8,9},{9,10},{10,1... | collective-permute-start | bytes 1572872 | tf_op jit(solution)/shard_map/ppermute | solution.py:1028
  154.3 31.8 %collective-permute-start.9 = (bf16[512,512]{1,0:T(8,128)(2,1)S(1)}, bf16[512,512]{1,0:T(8,128)(2,1)S(1)}, u32[]{:S(2)}, u32[]{:S(2)}) collective-permute-start(bf16[512,512]{1,0:T(8,128)(2,1)S(1)} %collective-permute-done.8.refs_1_), channel_id=1, source_target_pairs={{0,1},{1,2},{2,3},{3,0},{4,5},{5,6},{6,7},{7,4},{8,9},{9,10},{10,1... | collective-permute-start | bytes 1572872 | tf_op jit(solution)/shard_map/ppermute | solution.py:1028
  156.1 35.7 %collective-permute-start.6 = (bf16[1024,384]{1,0:T(8,128)(2,1)}, bf16[1024,384]{1,0:T(8,128)(2,1)}, u32[]{:S(2)}, u32[]{:S(2)}) collective-permute-start(bf16[1024,384]{1,0:T(8,128)(2,1)} %get-tuple-element.80), channel_id=1, source_target_pairs={{0,4},{4,0},{8,12},{12,8},{1,5},{5,1},{9,13},{13,9},{2,6},{6,2},{1... | collective-permute-start | bytes 2359304 | tf_op jit(solution)/shard_map/ppermute | solution.py:1031
  187.0 4.8 collective-permute-start.12
  188.8 37.8 %collective-permute-start.13 = (bf16[512,512]{1,0:T(8,128)(2,1)}, bf16[512,512]{1,0:T(8,128)(2,1)S(1)}, u32[]{:S(2)}, u32[]{:S(2)}) collective-permute-start(bf16[512,512]{1,0:T(8,128)(2,1)} %copy-done.12), channel_id=1, source_target_pairs={{0,1},{1,2},{2,3},{3,0},{4,5},{5,6},{6,7},{7,4},{8,9},{9,10},{10,1... | collective-permute-start | bytes 1572872 | tf_op jit(solution)/shard_map/ppermute | solution.py:1028
  190.3 36.3 %collective-permute-start.14 = (bf16[512,512]{1,0:T(8,128)(2,1)}, bf16[512,512]{1,0:T(8,128)(2,1)S(1)}, u32[]{:S(2)}, u32[]{:S(2)}) collective-permute-start(bf16[512,512]{1,0:T(8,128)(2,1)} %copy-done.11), channel_id=1, source_target_pairs={{0,1},{1,2},{2,3},{3,0},{4,5},{5,6},{6,7},{7,4},{8,9},{9,10},{10,1... | collective-permute-start | bytes 1572872 | tf_op jit(solution)/shard_map/ppermute | solution.py:1028
  227.6 28.4 %all-to-all-start = ((bf16[16,256,128]{2,1,0:T(8,128)(2,1)}), bf16[16,256,128]{2,1,0:T(8,128)(2,1)S(1)}, u32[]{:S(2)}, u32[]{:S(2)}) async-start(bf16[16,256,128]{2,1,0:T(8,128)(2,1)} %bitcast.118), calls=%async_computation | async-start | bytes 2097152 | tf_op jit(solution)/shard_map/all_to_all | solution.py:1131
  231.7 387.1 %reduce-scatter.6.cloned.1.call-start = ((), (), s32[]{:S(2)}) async-start(), calls=%async_computation.9 | async-start | bytes 6488064 | tf_op jit(solution)/shard_map/reduce_scatter | solution.py:1048
  266.5 26.0 %collective-permute-start.15 = (bf16[256,2048]{1,0:T(8,128)(2,1)}, bf16[256,2048]{1,0:T(8,128)(2,1)S(1)}, u32[]{:S(2)}, u32[]{:S(2)}) collective-permute-start(bf16[256,2048]{1,0:T(8,128)(2,1)} %get-tuple-element.85.low), channel_id=1, source_target_pairs={{0,1},{1,2},{2,3},{3,0},{4,5},{5,6},{6,7},{7,4},{8,9},{9,10},{10,1... | collective-permute-start | bytes 3145736 | tf_op jit(solution)/shard_map/ppermute | solution.py:1028
  293.5 28.2 %collective-permute-start.16 = (bf16[256,2048]{1,0:T(8,128)(2,1)}, bf16[256,2048]{1,0:T(8,128)(2,1)S(1)}, u32[]{:S(2)}, u32[]{:S(2)}) collective-permute-start(bf16[256,2048]{1,0:T(8,128)(2,1)} %tie.20.low), channel_id=1, source_target_pairs={{0,1},{1,2},{2,3},{3,0},{4,5},{5,6},{6,7},{7,4},{8,9},{9,10},{10,1... | collective-permute-start | bytes 3145736 | tf_op jit(solution)/shard_map/ppermute | solution.py:1028
  312.0 28.4 %collective-permute-start.19 = (bf16[128,2048]{1,0:T(8,128)(2,1)}, bf16[128,2048]{1,0:T(8,128)(2,1)S(1)}, u32[]{:S(2)}, u32[]{:S(2)}) collective-permute-start(bf16[128,2048]{1,0:T(8,128)(2,1)} %get-tuple-element.106), channel_id=1, source_target_pairs={{0,1},{1,2},{2,3},{3,0},{4,5},{5,6},{6,7},{7,4},{8,9},{9,10},{10,1... | collective-permute-start | bytes 1572872 | tf_op jit(solution)/shard_map/ppermute | solution.py:1028
  315.0 29.1 %collective-permute-start.18 = (bf16[128,2048]{1,0:T(8,128)(2,1)}, bf16[128,2048]{1,0:T(8,128)(2,1)S(1)}, u32[]{:S(2)}, u32[]{:S(2)}) collective-permute-start(bf16[128,2048]{1,0:T(8,128)(2,1)} %get-tuple-element.104), channel_id=1, source_target_pairs={{0,1},{1,2},{2,3},{3,0},{4,5},{5,6},{6,7},{7,4},{8,9},{9,10},{10,1... | collective-permute-start | bytes 1572872 | tf_op jit(solution)/shard_map/ppermute | solution.py:1028
  321.7 44.9 %collective-permute-start.17 = (bf16[256,2048]{1,0:T(8,128)(2,1)S(1)}, bf16[256,2048]{1,0:T(8,128)(2,1)S(1)}, u32[]{:S(2)}, u32[]{:S(2)}) collective-permute-start(bf16[256,2048]{1,0:T(8,128)(2,1)S(1)} %collective-permute-done.16.low), channel_id=1, source_target_pairs={{0,1},{1,2},{2,3},{3,0},{4,5},{5,6},{6,7},{7,4},{8,9},{9,10},{10,1... | collective-permute-start | bytes 3145736 | tf_op jit(solution)/shard_map/ppermute | solution.py:1028
  341.5 43.8 %collective-permute-start.22 = (bf16[128,2048]{1,0:T(8,128)(2,1)S(1)}, bf16[128,2048]{1,0:T(8,128)(2,1)S(1)}, u32[]{:S(2)}, u32[]{:S(2)}) collective-permute-start(bf16[128,2048]{1,0:T(8,128)(2,1)S(1)} %add_convert_fusion.4.refs_6_), channel_id=1, source_target_pairs={{0,1},{1,2},{2,3},{3,0},{4,5},{5,6},{6,7},{7,4},{8,9},{9,10},{10,1... | collective-permute-start | bytes 1572872 | tf_op jit(solution)/shard_map/ppermute | solution.py:1028
  345.4 42.0 %collective-permute-start.20 = (bf16[128,2048]{1,0:T(8,128)(2,1)S(1)}, bf16[128,2048]{1,0:T(8,128)(2,1)S(1)}, u32[]{:S(2)}, u32[]{:S(2)}) collective-permute-start(bf16[128,2048]{1,0:T(8,128)(2,1)S(1)} %add_convert_fusion.5.refs_5_), channel_id=1, source_target_pairs={{0,1},{1,2},{2,3},{3,0},{4,5},{5,6},{6,7},{7,4},{8,9},{9,10},{10,1... | collective-permute-start | bytes 1572872 | tf_op jit(solution)/shard_map/ppermute | solution.py:1028
  386.6 25.4 %collective-permute-start.23 = (bf16[128,2048]{1,0:T(8,128)(2,1)S(1)}, bf16[128,2048]{1,0:T(8,128)(2,1)S(1)}, u32[]{:S(2)}, u32[]{:S(2)}) collective-permute-start(bf16[128,2048]{1,0:T(8,128)(2,1)S(1)} %add_convert_fusion.2.refs_1_), channel_id=1, source_target_pairs={{0,1},{1,2},{2,3},{3,0},{4,5},{5,6},{6,7},{7,4},{8,9},{9,10},{10,1... | collective-permute-start | bytes 1572872 | tf_op jit(solution)/shard_map/ppermute | solution.py:1028
  388.6 23.4 %collective-permute-start.21 = (bf16[128,2048]{1,0:T(8,128)(2,1)S(1)}, bf16[128,2048]{1,0:T(8,128)(2,1)S(1)}, u32[]{:S(2)}, u32[]{:S(2)}) collective-permute-start(bf16[128,2048]{1,0:T(8,128)(2,1)S(1)} %add_convert_fusion.3.refs_0_), channel_id=1, source_target_pairs={{0,1},{1,2},{2,3},{3,0},{4,5},{5,6},{6,7},{7,4},{8,9},{9,10},{10,1... | collective-permute-start | bytes 1572872 | tf_op jit(solution)/shard_map/ppermute | solution.py:1028
  424.7 196.5 %reduce-scatter.4.cloned.1.call-start = ((), (), s32[]{:S(2)}) async-start(), calls=%async_computation.8 | async-start | bytes 6488064 | tf_op jit(solution)/shard_map/reduce_scatter | solution.py:1048
  425.3 32.5 %all-to-all-start.1 = ((bf16[16,256,128]{2,1,0:T(8,128)(2,1)}), bf16[16,256,128]{2,1,0:T(8,128)(2,1)}, u32[]{:S(2)}, u32[]{:S(2)}) async-start(bf16[16,256,128]{2,1,0:T(8,128)(2,1)} %bitcast.123), calls=%async_computation.1 | async-start | bytes 2097152 | tf_op jit(solution)/shard_map/all_to_all | solution.py:1184
  433.4 269.9 %reduce-scatter.8.cloned.1.call-start = ((), (), s32[]{:S(2)}) async-start(), calls=%async_computation.10 | async-start | bytes 9437184 | tf_op jit(solution)/shard_map/reduce_scatter | solution.py:1048
  433.5 83.8 %collective-permute-start.26 = (bf16[1024,1024]{1,0:T(8,128)(2,1)}, bf16[1024,1024]{1,0:T(8,128)(2,1)}, u32[]{:S(2)}, u32[]{:S(2)}) collective-permute-start(bf16[1024,1024]{1,0:T(8,128)(2,1)} %get-tuple-element.116), channel_id=1, source_target_pairs={{0,4},{4,0},{8,12},{12,8},{1,5},{5,1},{9,13},{13,9},{2,6},{6,2},{1... | collective-permute-start | bytes 6291464 | tf_op jit(solution)/shard_map/ppermute | solution.py:1031
  433.7 83.6 %collective-permute-start.27 = (bf16[1024,1408]{1,0:T(8,128)(2,1)S(1)}, bf16[1024,1408]{1,0:T(8,128)(2,1)}, u32[]{:S(2)}, u32[]{:S(2)}) collective-permute-start(bf16[1024,1408]{1,0:T(8,128)(2,1)S(1)} %copy-done), channel_id=1, source_target_pairs={{0,4},{4,0},{8,12},{12,8},{1,5},{5,1},{9,13},{13,9},{2,6},{6,2},{1... | collective-permute-start | bytes 8650760 | tf_op jit(solution)/shard_map/ppermute | solution.py:1031
  460.4 52.1 %collective-permute-start.24 = (bf16[1024,512]{1,0:T(8,128)(2,1)S(1)}, bf16[1024,512]{1,0:T(8,128)(2,1)S(1)}, u32[]{:S(2)}, u32[]{:S(2)}) collective-permute-start(bf16[1024,512]{1,0:T(8,128)(2,1)S(1)} %get-tuple-element.203), channel_id=1, source_target_pairs={{0,1},{1,2},{2,3},{3,0},{4,5},{5,6},{6,7},{7,4},{8,9},{9,10},{10,1... | collective-permute-start | bytes 3145736 | tf_op jit(solution)/shard_map/ppermute | solution.py:1028
  511.1 55.4 %collective-permute-start.30 = (bf16[2,1024,384]{2,1,0:T(8,128)(2,1)}, bf16[2,1024,384]{2,1,0:T(8,128)(2,1)S(1)}, u32[]{:S(2)}, u32[]{:S(2)}) collective-permute-start(bf16[2,1024,384]{2,1,0:T(8,128)(2,1)} %get-tuple-element.125), channel_id=1, source_target_pairs={{0,8},{4,12},{8,0},{12,4},{1,9},{5,13},{9,1},{13,5},{2,10},{6,14},... | collective-permute-start | bytes 4718600 | tf_op jit(solution)/shard_map/ppermute | solution.py:1031
  514.1 24.8 %collective-permute-start.25 = (bf16[1024,512]{1,0:T(8,128)(2,1)S(1)}, bf16[1024,512]{1,0:T(8,128)(2,1)S(1)}, u32[]{:S(2)}, u32[]{:S(2)}) collective-permute-start(bf16[1024,512]{1,0:T(8,128)(2,1)S(1)} %fusion.1), channel_id=1, source_target_pairs={{0,1},{1,2},{2,3},{3,0},{4,5},{5,6},{6,7},{7,4},{8,9},{9,10},{10,1... | collective-permute-start | bytes 3145736 | tf_op jit(solution)/shard_map/ppermute | solution.py:1028
  516.6 54.3 %collective-permute-start.32 = (bf16[1024,1024]{1,0:T(8,128)(2,1)}, bf16[1024,1024]{1,0:T(8,128)(2,1)}, u32[]{:S(2)}, u32[]{:S(2)}) collective-permute-start(bf16[1024,1024]{1,0:T(8,128)(2,1)} %get-tuple-element.127), channel_id=1, source_target_pairs={{0,4},{4,0},{8,12},{12,8},{1,5},{5,1},{9,13},{13,9},{2,6},{6,2},{1... | collective-permute-start | bytes 6291464 | tf_op jit(solution)/shard_map/ppermute | solution.py:1031
  542.3 26.2 %collective-permute-start.28 = (bf16[1024,512]{1,0:T(8,128)(2,1)}, bf16[1024,512]{1,0:T(8,128)(2,1)S(1)}, u32[]{:S(2)}, u32[]{:S(2)}) collective-permute-start(bf16[1024,512]{1,0:T(8,128)(2,1)} %ring_add.4.refs_1_), channel_id=1, source_target_pairs={{0,1},{1,2},{2,3},{3,0},{4,5},{5,6},{6,7},{7,4},{8,9},{9,10},{10,1... | collective-permute-start | bytes 3145736 | tf_op jit(solution)/shard_map/ppermute | solution.py:1028
  544.8 26.1 %collective-permute-start.29 = (bf16[1024,384]{1,0:T(8,128)(2,1)S(1)}, bf16[1024,384]{1,0:T(8,128)(2,1)S(1)}, u32[]{:S(2)}, u32[]{:S(2)}) collective-permute-start(bf16[1024,384]{1,0:T(8,128)(2,1)S(1)} %copy-done.47), channel_id=1, source_target_pairs={{0,4},{4,0},{8,12},{12,8},{1,5},{5,1},{9,13},{13,9},{2,6},{6,2},{1... | collective-permute-start | bytes 2359304 | tf_op jit(solution)/shard_map/ppermute | solution.py:1031
  567.9 3.1 collective-permute-start.31
  591.9 9.8 %collective-permute-start.37 = (bf16[1024,1536]{1,0:T(8,128)(2,1)}, bf16[1024,1536]{1,0:T(8,128)(2,1)S(1)}, u32[]{:S(2)}, u32[]{:S(2)}) collective-permute-start(bf16[1024,1536]{1,0:T(8,128)(2,1)} %get-tuple-element.136.right_here), channel_id=1, source_target_pairs={{0,4},{4,0},{8,12},{12,8},{1,5},{5,1},{9,13},{13,9},{2,6},{6,2},{1... | collective-permute-start | bytes 9437192 | tf_op jit(solution)/shard_map/ppermute | solution.py:1031
  593.4 24.7 %collective-permute-start.34 = (f32[1,8192]{1,0:T(1,128)S(1)}, f32[1,8192]{1,0:T(1,128)S(1)}, u32[]{:S(2)}, u32[]{:S(2)}) collective-permute-start(f32[1,8192]{1,0:T(1,128)S(1)} %constant_dynamic-update-slice_fusion), channel_id=1, source_target_pairs={{0,1},{1,2},{2,3},{3,0},{4,5},{5,6},{6,7},{7,4},{8,9},{9,10},{10,1... | collective-permute-start | bytes 98312 | tf_op jit(solution)/shard_map/ppermute | solution.py:1028
  596.5 21.6 %collective-permute-start.35 = (f32[1,8192]{1,0:T(1,128)S(1)}, f32[1,8192]{1,0:T(1,128)S(1)}, u32[]{:S(2)}, u32[]{:S(2)}) collective-permute-start(f32[1,8192]{1,0:T(1,128)S(1)} %constant_dynamic-update-slice_fusion), channel_id=1, source_target_pairs={{0,2},{1,3},{2,0},{3,1},{4,6},{5,7},{6,4},{7,5},{8,10},{9,11},{10,... | collective-permute-start | bytes 98312 | tf_op jit(solution)/shard_map/ppermute | solution.py:1028
  599.6 18.5 %collective-permute-start.36 = (f32[1,8192]{1,0:T(1,128)S(1)}, f32[1,8192]{1,0:T(1,128)S(1)}, u32[]{:S(2)}, u32[]{:S(2)}) collective-permute-start(f32[1,8192]{1,0:T(1,128)S(1)} %constant_dynamic-update-slice_fusion), channel_id=1, source_target_pairs={{0,3},{1,0},{2,1},{3,2},{4,7},{5,4},{6,5},{7,6},{8,11},{9,8},{10,9... | collective-permute-start | bytes 98312 | tf_op jit(solution)/shard_map/ppermute | solution.py:1028
  601.6 24.7 %collective-permute-start.33 = (bf16[1024,512]{1,0:T(8,128)(2,1)}, bf16[1024,512]{1,0:T(8,128)(2,1)S(1)}, u32[]{:S(2)}, u32[]{:S(2)}) collective-permute-start(bf16[1024,512]{1,0:T(8,128)(2,1)} %get-tuple-element.128), channel_id=1, source_target_pairs={{0,1},{1,2},{2,3},{3,0},{4,5},{5,6},{6,7},{7,4},{8,9},{9,10},{10,1... | collective-permute-start | bytes 3145736 | tf_op jit(solution)/shard_map/ppermute | solution.py:1028
  616.8 55.0 %collective-permute-start.40 = (bf16[2,128,2944]{2,1,0:T(8,128)(2,1)}, bf16[2,128,2944]{2,1,0:T(8,128)(2,1)}, u32[]{:S(2)}, u32[]{:S(2)}) collective-permute-start(bf16[2,128,2944]{2,1,0:T(8,128)(2,1)} %get-tuple-element.143.refs_6_), channel_id=1, source_target_pairs={{0,8},{4,12},{8,0},{12,4},{1,9},{5,13},{9,1},{13,5},{2,10},{6,14},... | collective-permute-start | bytes 4521992 | tf_op jit(solution)/shard_map/ppermute | solution.py:1031
  627.3 44.5 %copy-start.7 = (bf16[2,128,2944]{2,1,0:T(8,128)(2,1)S(1)}, bf16[2,128,2944]{2,1,0:T(8,128)(2,1)}, u32[]{:S(2)}) copy-start(bf16[2,128,2944]{2,1,0:T(8,128)(2,1)} %get-tuple-element.142.refs_5_) | copy-start | bytes 4521988
  629.8 2.8 collective-permute-start.41
  629.9 46.6 %collective-permute-start.39 = (bf16[2,128,2944]{2,1,0:T(8,128)(2,1)S(1)}, bf16[2,128,2944]{2,1,0:T(8,128)(2,1)S(1)}, u32[]{:S(2)}, u32[]{:S(2)}) collective-permute-start(bf16[2,128,2944]{2,1,0:T(8,128)(2,1)S(1)} %copy-done.17), channel_id=1, source_target_pairs={{0,16},{16,0},{1,17},{17,1},{2,18},{18,2},{3,19},{19,3},{4,20},{20... | collective-permute-start | bytes 4521992 | tf_op jit(solution)/shard_map/ppermute | solution.py:1051
  631.4 46.5 %collective-permute-start.38 = (bf16[1024,512]{1,0:T(8,128)(2,1)}, bf16[1024,512]{1,0:T(8,128)(2,1)S(1)}, u32[]{:S(2)}, u32[]{:S(2)}) collective-permute-start(bf16[1024,512]{1,0:T(8,128)(2,1)} %ring_add.5.refs_1_), channel_id=1, source_target_pairs={{0,1},{1,2},{2,3},{3,0},{4,5},{5,6},{6,7},{7,4},{8,9},{9,10},{10,1... | collective-permute-start | bytes 3145736 | tf_op jit(solution)/shard_map/ppermute | solution.py:1028
  634.1 42.4 %copy-start.1 = (bf16[2,128,2944]{2,1,0:T(8,128)(2,1)S(1)}, bf16[2,128,2944]{2,1,0:T(8,128)(2,1)}, u32[]{:S(2)}) copy-start(bf16[2,128,2944]{2,1,0:T(8,128)(2,1)} %get-tuple-element.140.refs_3_) | copy-start | bytes 4521988
  674.5 18.8 %collective-permute-start.49 = (bf16[128,2944]{1,0:T(8,128)(2,1)}, bf16[128,2944]{1,0:T(8,128)(2,1)}, u32[]{:S(2)}, u32[]{:S(2)}) collective-permute-start(bf16[128,2944]{1,0:T(8,128)(2,1)} %slice_bitcast_fusion.4), channel_id=1, source_target_pairs={{0,16},{16,0},{1,17},{17,1},{2,18},{18,2},{3,19},{19,3},{4,20},{20... | collective-permute-start | bytes 2261000 | tf_op jit(solution)/shard_map/ppermute | solution.py:1051
  681.5 4.2 collective-permute-start.46
  683.7 18.3 %collective-permute-start.48 = (bf16[128,2944]{1,0:T(8,128)(2,1)}, bf16[128,2944]{1,0:T(8,128)(2,1)}, u32[]{:S(2)}, u32[]{:S(2)}) collective-permute-start(bf16[128,2944]{1,0:T(8,128)(2,1)} %slice_bitcast_fusion.6), channel_id=1, source_target_pairs={{0,8},{4,12},{8,0},{12,4},{1,9},{5,13},{9,1},{13,5},{2,10},{6,14},... | collective-permute-start | bytes 2261000 | tf_op jit(solution)/shard_map/ppermute | solution.py:1031
  684.4 50.9 %collective-permute-start.42 = (bf16[1024,512]{1,0:T(8,128)(2,1)}, bf16[1024,512]{1,0:T(8,128)(2,1)}, u32[]{:S(2)}, u32[]{:S(2)}) collective-permute-start(bf16[1024,512]{1,0:T(8,128)(2,1)} %ring_add.6.refs_1_), channel_id=1, source_target_pairs={{0,1},{1,2},{2,3},{3,0},{4,5},{5,6},{6,7},{7,4},{8,9},{9,10},{10,1... | collective-permute-start | bytes 3145736 | tf_op jit(solution)/shard_map/ppermute | solution.py:1028
  706.8 19.2 %collective-permute-start.43 = (bf16[256,512]{0,1:T(8,128)(2,1)S(1)}, bf16[256,512]{0,1:T(8,128)(2,1)S(1)}, u32[]{:S(2)}, u32[]{:S(2)}) collective-permute-start(bf16[256,512]{0,1:T(8,128)(2,1)S(1)} %get-tuple-element.208), channel_id=1, source_target_pairs={{0,1},{1,2},{2,3},{3,0},{4,5},{5,6},{6,7},{7,4},{8,9},{9,10},{10,1... | collective-permute-start | bytes 786440 | tf_op jit(solution)/shard_map/ppermute | solution.py:1028
  708.0 22.0 %collective-permute-start.44 = (bf16[256,512]{0,1:T(8,128)(2,1)S(1)}, bf16[256,512]{0,1:T(8,128)(2,1)S(1)}, u32[]{:S(2)}, u32[]{:S(2)}) collective-permute-start(bf16[256,512]{0,1:T(8,128)(2,1)S(1)} %get-tuple-element.210), channel_id=1, source_target_pairs={{0,2},{1,3},{2,0},{3,1},{4,6},{5,7},{6,4},{7,5},{8,10},{9,11},{10,... | collective-permute-start | bytes 786440 | tf_op jit(solution)/shard_map/ppermute | solution.py:1028
  711.4 22.1 %collective-permute-start.45 = (bf16[256,512]{0,1:T(8,128)(2,1)S(1)}, bf16[256,512]{0,1:T(8,128)(2,1)S(1)}, u32[]{:S(2)}, u32[]{:S(2)}) collective-permute-start(bf16[256,512]{0,1:T(8,128)(2,1)S(1)} %get-tuple-element.209), channel_id=1, source_target_pairs={{0,3},{1,0},{2,1},{3,2},{4,7},{5,4},{6,5},{7,6},{8,11},{9,8},{10,9... | collective-permute-start | bytes 786440 | tf_op jit(solution)/shard_map/ppermute | solution.py:1028
  737.8 8.1 %collective-permute-start.47 = (f32[1,9728]{1,0:T(1,128)}, f32[1,9728]{1,0:T(1,128)S(1)}, u32[]{:S(2)}, u32[]{:S(2)}) collective-permute-start(f32[1,9728]{1,0:T(1,128)} %tie.29), channel_id=1, source_target_pairs={{0,16},{16,0},{1,17},{17,1},{2,18},{18,2},{3,19},{19,3},{4,20},{20... | collective-permute-start | bytes 116744 | tf_op jit(solution)/shard_map/ppermute | solution.py:1240
  (45 other events, 321.2 us)
Sparse Core Ops, SparseCore 0:
  11.2 46.6 all-gather.3
  59.8 113.7 all-gather.5
  176.1 54.3 all-gather.7
  424.8 66.5 reduce-scatter.5
  495.1 77.1 reduce-scatter.3
  575.6 93.8 reduce-scatter.7

commit v3 on v2

--- a/solution.py
+++ b/solution.py
@@ -1248,7 +1248,7 @@
     small = jnp.concatenate([bias_grad, small], axis=1)
     travelling, ring_steps = partial[1 % tp], []
     once = square_once(parts) if square else ()
-    needed = [[total_gate, total_up, small, *parts], [*once], []]
+    needed = [[total_gate, total_up, small, *parts], [], [*once]]
     for step in range(1, tp):
         travelling = add(
             shift(travelling, 1), partial[(step + 1) % tp], *(needed[step - 1] if step < 4 else [])

time: 764 us -> 770 us (level)
  Pallas kernels: 293 us -> 309 us
    ppermute x12, waiting for transfers between devices: 93.9 us -> 58.6 us  [swap(): return lax.ppermute(value, 'ctx', [(i, i ^ step) for i in range(nctx)])]
    ppermute x33, waiting for transfers between devices: 148 us -> 167 us  [shift(): return lax.ppermute(value, 'tp', [(i, (i + step) % tp) for i in range(tp)])]
    ppermute x2, waiting for transfers between devices: 6.68 us -> 20.4 us  [cross(): return lax.ppermute(value, 'fsdp', [(i, i ^ 1) for i in range(nfsdp)])]
    pallas_call x1, Pallas kernels: 50.1 us -> 58.5 us  [attend_back(): pl.pallas_call(functools.partial(attend_back_kernel, nctx, heads, len(pie...]
    unnamed x110 -> x108, local copies, waits for them, and re-layouts: 24.8 us -> 23.9 us
  transfers between devices with their start and end apart: 58 -> 58, of which waited for: 27 -> 30; matrix products, arithmetic and copies ran while one was open for 7% -> 8% of each run, Pallas kernels for 36% -> 37%
where the time goes in v3:
time: 770 us; the launch traced here: 767 us
  Pallas kernels  309 us (40%)
  waiting for transfers between devices  289 us (38%)
  starting transfers between devices  74.2 us (10%)
  local copies, waits for them, and re-layouts  42.9 us (6%)
  other arithmetic  37.2 us (5%)
  between operations  15 us (2%)
    ppermute x33, waiting for transfers between devices, shift(): return lax.ppermute(value, 'tp', [(i, (i + step) % tp) for i in range(tp)])  167 us
    pallas_call x4, Pallas kernels, feed(): pl.pallas_call(functools.partial(feed_kernel, tuple(cuts), parts, tp, ste...  70.8 us
    ppermute x12, waiting for transfers between devices, swap(): return lax.ppermute(value, 'ctx', [(i, i ^ step) for i in range(nctx)])  58.6 us
    pallas_call x1, Pallas kernels, attend_back(): pl.pallas_call(functools.partial(attend_back_kernel, nctx, heads, len(pie...  58.5 us
    ppermute x33, starting transfers between devices, shift(): return lax.ppermute(value, 'tp', [(i, (i + step) % tp) for i in range(tp)])  56.6 us
    pallas_call x1, Pallas kernels, attend(): pl.pallas_call(functools.partial(attend_kernel, nctx, heads, len(pieces),...  40.6 us
    pallas_call x3, Pallas kernels, blame(): pl.pallas_call(kernel, grid=(steps,), in_specs=in_specs + anywhere(len(ne...  28.1 us
    pallas_call x2, Pallas kernels, blame_halves(): pl.pallas_call(kernel, grid_spec=grid_spec, out_shape=[jax.ShapeDtypeStru...  27 us
  transfers between devices with their start and end apart: 58, of which 30 were waited for; matrix products, arithmetic and copies ran while one was open for 8% of the time, Pallas kernels for 37%

profile of v3, /device:TPU:8, one launch (start us, length us, event | category | flops | bytes accessed | tf_op | source)
XLA Modules:
  0.0 767.1 jit_solution(13192521357511652425)
XLA Ops:
  7.2 2.3 copy.131.refs_0_
  11.1 3.2 pack.1.refs_1_
  19.6 13.8 %collective-permute-done.refs_0_ = bf16[640,512]{1,0:T(8,128)(2,1)S(1)} collective-permute-done((bf16[640,512]{1,0:T(8,128)(2,1)S(1)}, bf16[640,512]{1,0:T(8,128)(2,1)S(1)}, u32[]{:S(2)}, u32[]{:S(2)}) %collective-permute-start) | collective-permute-done | bytes 655392 | tf_op jit(solution)/shard_map/ppermute | solution.py:1028
  35.8 11.6 %collective-permute-done.3.refs_0_ = bf16[640,512]{1,0:T(8,128)(2,1)S(1)} collective-permute-done((bf16[640,512]{1,0:T(8,128)(2,1)S(1)}, bf16[640,512]{1,0:T(8,128)(2,1)S(1)}, u32[]{:S(2)}, u32[]{:S(2)}) %collective-permute-start.3) | collective-permute-done | bytes 655392 | tf_op jit(solution)/shard_map/ppermute | solution.py:1028
  50.1 11.5 %collective-permute-done.1.refs_2_ = bf16[640,512]{1,0:T(8,128)(2,1)} collective-permute-done((bf16[640,512]{1,0:T(8,128)(2,1)}, bf16[640,512]{1,0:T(8,128)(2,1)}, u32[]{:S(2)}, u32[]{:S(2)}) %collective-permute-start.1) | collective-permute-done | bytes 655392 | tf_op jit(solution)/shard_map/ppermute | solution.py:1028
  63.2 12.4 %collective-permute-done.4.refs_6_ = bf16[640,512]{1,0:T(8,128)(2,1)S(1)} collective-permute-done((bf16[640,512]{1,0:T(8,128)(2,1)}, bf16[640,512]{1,0:T(8,128)(2,1)S(1)}, u32[]{:S(2)}, u32[]{:S(2)}) %collective-permute-start.4) | collective-permute-done | bytes 655392 | tf_op jit(solution)/shard_map/ppermute | solution.py:1028
  78.6 3.2 fusion.4
  81.8 7.8 %collective-permute-done.2.refs_3_.refs_1_ = bf16[640,512]{1,0:T(8,128)(2,1)S(1)} collective-permute-done((bf16[640,512]{1,0:T(8,128)(2,1)}, bf16[640,512]{1,0:T(8,128)(2,1)S(1)}, u32[]{:S(2)}, u32[]{:S(2)}) %collective-permute-start.2) | collective-permute-done | bytes 655392 | tf_op jit(solution)/shard_map/ppermute | solution.py:1028
  89.6 12.9 %collective-permute-done.5.refs_7_.refs_2_ = bf16[640,512]{1,0:T(8,128)(2,1)S(1)} collective-permute-done((bf16[640,512]{1,0:T(8,128)(2,1)S(1)}, bf16[640,512]{1,0:T(8,128)(2,1)S(1)}, u32[]{:S(2)}, u32[]{:S(2)}) %collective-permute-start.5) | collective-permute-done | bytes 655392 | tf_op jit(solution)/shard_map/ppermute | solution.py:1028
  103.4 21.5 %project.1 = (bf16[1024,2048]{1,0:T(8,128)(2,1)}, bf16[1024,2048]{1,0:T(8,128)(2,1)}, bf16[1024,1024]{1,0:T(8,128)(2,1)}, bf16[1024,384]{1,0:T(8,128)(2,1)}, bf1...) custom-call(s32[3]{0:T(128)} %pad_add_fusion.1.place, ...), custom_call_target="tpu_custom_call" | custom-call | flops 6000000000 | tf_op jit(solution)/shard_map/project/pallas_call | solution.py:225
  131.3 11.8 %collective-permute-done.10.refs_5_ = bf16[512,512]{1,0:T(8,128)(2,1)S(1)} collective-permute-done((bf16[512,512]{1,0:T(8,128)(2,1)S(1)}, bf16[512,512]{1,0:T(8,128)(2,1)S(1)}, u32[]{:S(2)}, u32[]{:S(2)}) %collective-permute-start.10) | collective-permute-done | bytes 524320 | tf_op jit(solution)/shard_map/ppermute | solution.py:1028
  144.4 9.9 %collective-permute-done.8.refs_1_ = bf16[512,512]{1,0:T(8,128)(2,1)S(1)} collective-permute-done((bf16[512,512]{1,0:T(8,128)(2,1)S(1)}, bf16[512,512]{1,0:T(8,128)(2,1)S(1)}, u32[]{:S(2)}, u32[]{:S(2)}) %collective-permute-start.8) | collective-permute-done | bytes 524320 | tf_op jit(solution)/shard_map/ppermute | solution.py:1028
  156.2 26.9 %collective-permute-done.7 = bf16[2,1024,384]{2,1,0:T(8,128)(2,1)} collective-permute-done((bf16[2,1024,384]{2,1,0:T(8,128)(2,1)}, bf16[2,1024,384]{2,1,0:T(8,128)(2,1)}, u32[]{:S(2)}, u32[]{:S(2)}) %collective-permute-start.7) | collective-permute-done | bytes 1572896 | tf_op jit(solution)/shard_map/ppermute | solution.py:1031
  183.1 2.9 slice_bitcast_fusion.2
  191.8 40.6 %attend.1 = (bf16[4096,128]{1,0:T(8,128)(2,1)}, bf16[4096,128]{1,0:T(8,128)(2,1)}, f32[2,4096]{1,0:T(2,128)}) custom-call(s32[1]{0:T(128)} %bitcast.1.place, s32[8]{0:T(128)} %fusion.27.lows, s32[8]{0:T(128)} %multiply_add_fusion.ends, s32[2,4096]{1,0:T(2,128)} %pad_add_fusion.bounds, bf16[1024,384]{1,0:T(8,128)(2,1)} %get-tuple-element.79.refs_0_, ...), custom_call_target="tpu_custom_call" | custom-call | flops 20000000000 | tf_op jit(solution)/shard_map/attend/pallas_call | solution.py:360
  233.4 4.2 all-to-all-start
  237.6 24.2 %all-to-all-done = bf16[16,256,128]{2,1,0:T(8,128)(2,1)S(1)} async-done(((bf16[16,256,128]{2,1,0:T(8,128)(2,1)}), bf16[16,256,128]{2,1,0:T(8,128)(2,1)S(1)}, u32[]{:S(2)}, u32[]{:S(2)}) %all-to-all-start) | async-done | bytes 1048608 | tf_op jit(solution)/shard_map/all_to_all | solution.py:1131
  262.7 9.5 %mix.1 = (bf16[256,2048]{1,0:T(8,128)(2,1)}, f32[256,2048]{1,0:T(8,128)}, bf16[256,2048]{1,0:T(8,128)(2,1)}) custom-call(s32[3]{0:T(128)} %pad_add_fusion.1.place, bf16[4,4,256,128]{3,2,1,0:T(8,128)(2,1)} %bitcast.124, bf16[4,2048,512]{2,1,0:T(8,128)(2,1)} %all-gather.8.cloned.1.call-done.weight.refs_7_, ...), custom_call_target="tpu_custom_call" | custom-call | flops 5000000000 | tf_op jit(solution)/shard_map/mix/pallas_call | solution.py:533
  272.9 6.0 join.1
  278.9 17.7 %feed.4 = (bf16[1024,2048]{1,0:T(8,128)(2,1)}, bf16[1024,1408]{1,0:T(8,128)(2,1)}, bf16[1024,1408]{1,0:T(8,128)(2,1)}, bf16[1024,1408]{1,0:T(8,128)(2,1)}, bf16[...) custom-call(s32[3]{0:T(128)} %pad_add_fusion.1.place, ...), custom_call_target="tpu_custom_call" | custom-call | flops 10000000000 | tf_op jit(solution)/shard_map/feed/pallas_call | solution.py:623
  300.2 17.7 %feed.5 = (bf16[1024,2048]{1,0:T(8,128)(2,1)}, bf16[1024,1408]{1,0:T(8,128)(2,1)}, bf16[1024,1408]{1,0:T(8,128)(2,1)}, bf16[1024,1408]{1,0:T(8,128)(2,1)}, bf16[...) custom-call(s32[3]{0:T(128)} %pad_add_fusion.1.place, ...), custom_call_target="tpu_custom_call", output_to_operand_aliasing={{0}: (5, {}), {1}: (6, {}), {2}: (7, {}), {3}: (8, {}), {4}... | custom-call | flops 10000000000 | tf_op jit(solution)/shard_map/feed/pallas_call | solution.py:623
  317.9 3.0 collective-permute-start.19
  320.9 3.0 collective-permute-start.18
  323.9 3.6 collective-permute-done.16.low
  328.5 17.7 %feed.6 = (bf16[1024,2048]{1,0:T(8,128)(2,1)}, bf16[1024,1408]{1,0:T(8,128)(2,1)}, bf16[1024,1408]{1,0:T(8,128)(2,1)}, bf16[1024,1408]{1,0:T(8,128)(2,1)}, bf16[...) custom-call(s32[3]{0:T(128)} %pad_add_fusion.1.place, ...), custom_call_target="tpu_custom_call", output_to_operand_aliasing={{0}: (5, {}), {1}: (6, {}), {2}: (7, {}), {3}: (8, {}), {4}... | custom-call | flops 10000000000 | tf_op jit(solution)/shard_map/feed/pallas_call | solution.py:623
  351.2 3.7 collective-permute-start.20
  354.8 17.6 %collective-permute-done.17.low = bf16[256,2048]{1,0:T(8,128)(2,1)S(1)} collective-permute-done((bf16[256,2048]{1,0:T(8,128)(2,1)S(1)}, bf16[256,2048]{1,0:T(8,128)(2,1)S(1)}, u32[]{:S(2)}, u32[]{:S(2)}) %collective-permute-start.17) | collective-permute-done | bytes 1048608 | tf_op jit(solution)/shard_map/ppermute | solution.py:1028
  373.4 17.7 %feed.7 = (bf16[1024,2048]{1,0:T(8,128)(2,1)}, bf16[1024,1408]{1,0:T(8,128)(2,1)}, bf16[1024,1408]{1,0:T(8,128)(2,1)}, bf16[1024,1408]{1,0:T(8,128)(2,1)}, bf16[...) custom-call(s32[3]{0:T(128)} %pad_add_fusion.1.place, ...), custom_call_target="tpu_custom_call", output_to_operand_aliasing={{0}: (5, {}), {1}: (6, {}), {2}: (7, {}), {3}: (8, {}), {4}... | custom-call | flops 10000000000 | tf_op jit(solution)/shard_map/feed/pallas_call | solution.py:623
  396.5 10.6 %blame.4.refs_9_.refs_0_ = bf16[2048,1408]{1,0:T(8,128)(2,1)} custom-call(bf16[1024,2048]{1,0:T(8,128)(2,1)} %get-tuple-element.112.left, bf16[1024,1408]{1,0:T(8,128)(2,1)} %get-tuple-element.114.right, bf16[128,2048]{1,0:T(8,128)(2,1)} %copy-done.35, bf16[128,2048]{1,0:T(8,128)(2,1)} %copy-done.34), custom_call_target="tpu_custom_call" | custom-call | flops 6000000000 | tf_op jit(solution)/shard_map/blame/pallas_call | solution.py:726
  407.1 10.6 %blame.3.refs_8_.refs_0_ = bf16[2048,1408]{1,0:T(8,128)(2,1)} custom-call(bf16[1024,2048]{1,0:T(8,128)(2,1)} %get-tuple-element.112.left, bf16[1024,1408]{1,0:T(8,128)(2,1)} %get-tuple-element.113.right, bf16[128,2048]{1,0:T(8,128)(2,1)} %copy-done.35, bf16[128,2048]{1,0:T(8,128)(2,1)} %copy-done.34), custom_call_target="tpu_custom_call" | custom-call | flops 6000000000 | tf_op jit(solution)/shard_map/blame/pallas_call | solution.py:726
  418.7 11.7 %turn.1 = (bf16[4,4,256,128]{3,2,1,0:T(8,128)(2,1)}, f32[256,2048]{1,0:T(8,128)}, bf16[256,2048]{1,0:T(8,128)(2,1)}, f32[1,2048]{1,0:T(1,128)}, f32[1,2048]{1,0:T(1,128)}, /*index=5*/bf16[256,1024]{1,0:T(8,128)(2,1)}) custom-call(s32[3]{0:T(128)} %pad_add_fusion.1.place, bf16[128,2048]{1,0:T(8,128)(2,1)} %copy-done.33, bf16[128,2048]{1,0:T(8,128)(2,1)} %copy-done.32, ...), custom_call_target="tpu_custom_call" | custom-call | flops 6000000000 | tf_op jit(solution)/shard_map/turn/pallas_call | solution.py:798
  431.0 8.2 %all-to-all-start.1 = ((bf16[16,256,128]{2,1,0:T(8,128)(2,1)}), bf16[16,256,128]{2,1,0:T(8,128)(2,1)}, u32[]{:S(2)}, u32[]{:S(2)}) async-start(bf16[16,256,128]{2,1,0:T(8,128)(2,1)} %bitcast.123), calls=%async_computation.1 | async-start | bytes 2097152 | tf_op jit(solution)/shard_map/all_to_all | solution.py:1184
  439.9 6.9 blame.5.refs_6_.refs_0_
  446.7 16.8 %all-to-all-done.1 = bf16[16,256,128]{2,1,0:T(8,128)(2,1)} async-done(((bf16[16,256,128]{2,1,0:T(8,128)(2,1)}), bf16[16,256,128]{2,1,0:T(8,128)(2,1)}, u32[]{:S(2)}, u32[]{:S(2)}) %all-to-all-start.1) | async-done | bytes 1048608 | tf_op jit(solution)/shard_map/all_to_all | solution.py:1184
  463.6 2.6 dynamic-slice_bitcast_fusion
  466.7 58.5 %attend_back.1 = (bf16[1024,384]{1,0:T(8,128)(2,1)}, bf16[1024,384]{1,0:T(8,128)(2,1)}, bf16[2,1024,384]{2,1,0:T(8,128)(2,1)}) custom-call(s32[1]{0:T(128)} %bitcast.1.place, s32[8]{0:T(128)} %fusion.27.lows, s32[8]{0:T(128)} %multiply_add_fusion.ends, s32[2,4096]{1,0:T(2,128)} %pad_add_fusion.bounds, f32[2,4096]{1,0:T(2,128)} %get-tuple-element.119.logs, ...), custom_call_target="tpu_custom_call" | custom-call | flops 24999999488 | tf_op jit(solution)/shard_map/attend_back/pallas_call | solution.py:476
  526.6 2.5 fusion.1
  529.1 2.5 collective-permute-start.25
  532.3 13.3 %blame_halves.2 = (bf16[2,128,2944]{2,1,0:T(8,128)(2,1)}, bf16[2,128,2944]{2,1,0:T(8,128)(2,1)}, bf16[2,128,2944]{2,1,0:T(8,128)(2,1)}, bf16[2,128,2944]{2,1,0:T(8,128)(2,1)}) custom-call(s32[4]{0:T(128)} %pad_add_fusion.2.place, bf16[4,1024,512]{2,1,0:T(8,128)(2,1)} %get-tuple-element.86.cot.refs_5_.left_here, ...), custom_call_target="tpu_custom_call" | custom-call | flops 6000000000 | tf_op jit(solution)/shard_map/blame_halves/pallas_call | solution.py:698
  545.5 8.8 %collective-permute-done.25.left = bf16[1024,512]{1,0:T(8,128)(2,1)} collective-permute-done((bf16[1024,512]{1,0:T(8,128)(2,1)}, bf16[1024,512]{1,0:T(8,128)(2,1)}, u32[]{:S(2)}, u32[]{:S(2)}) %collective-permute-start.25) | collective-permute-done | bytes 1048608 | tf_op jit(solution)/shard_map/ppermute | solution.py:1028
  554.3 2.5 ring_add.4.refs_1_
  556.8 2.3 collective-permute-start.28
  559.2 21.8 %collective-permute-done.30 = bf16[2,1024,384]{2,1,0:T(8,128)(2,1)} collective-permute-done((bf16[2,1024,384]{2,1,0:T(8,128)(2,1)}, bf16[2,1024,384]{2,1,0:T(8,128)(2,1)}, u32[]{:S(2)}, u32[]{:S(2)}) %collective-permute-start.30) | collective-permute-done | bytes 1572896 | tf_op jit(solution)/shard_map/ppermute | solution.py:1031
  580.9 2.7 slice_bitcast_fusion
  583.7 2.5 fusion.refs_11_
  587.3 21.7 %finish.1 = (bf16[1024,512]{1,0:T(8,128)(2,1)}, bf16[1024,512]{1,0:T(8,128)(2,1)}, bf16[1024,512]{1,0:T(8,128)(2,1)}, bf16[1024,512]{1,0:T(8,128)(2,1)}, bf16[10...) custom-call(s32[3]{0:T(128)} %pad_add_fusion.1.place, ...), custom_call_target="tpu_custom_call" | custom-call | flops 7000000000 | tf_op jit(solution)/shard_map/finish/pallas_call | solution.py:910
  612.2 4.2 collective-permute-start.35
  622.1 13.7 %blame_halves.3 = (bf16[2,128,2944]{2,1,0:T(8,128)(2,1)}, bf16[2,128,2944]{2,1,0:T(8,128)(2,1)}, bf16[2,128,2944]{2,1,0:T(8,128)(2,1)}, bf16[2,128,2944]{2,1,0:T(8,128)(2,1)}) custom-call(s32[4]{0:T(128)} %pad_add_fusion.2.place, ...), custom_call_target="tpu_custom_call", output_to_operand_aliasing={{0}: (5, {}), {1}: (6, {}), {2}: (7, {}), {3}: (8, {})} | custom-call | flops 6000000000 | tf_op jit(solution)/shard_map/blame_halves/pallas_call | solution.py:698
  642.9 2.4 ring_add.5.refs_1_
  650.0 20.9 %collective-permute-done.38.left = bf16[1024,512]{1,0:T(8,128)(2,1)S(1)} collective-permute-done((bf16[1024,512]{1,0:T(8,128)(2,1)}, bf16[1024,512]{1,0:T(8,128)(2,1)S(1)}, u32[]{:S(2)}, u32[]{:S(2)}) %collective-permute-start.38) | collective-permute-done | bytes 1048608 | tf_op jit(solution)/shard_map/ppermute | solution.py:1028
  671.8 2.6 ring_add.6.refs_1_
  674.5 6.9 collective-permute-done.42
  684.2 10.3 %collective-permute-done.41 = bf16[2,128,2944]{2,1,0:T(8,128)(2,1)} collective-permute-done((bf16[2,128,2944]{2,1,0:T(8,128)(2,1)}, bf16[2,128,2944]{2,1,0:T(8,128)(2,1)}, u32[]{:S(2)}, u32[]{:S(2)}) %collective-permute-start.41) | collective-permute-done | bytes 1507360 | tf_op jit(solution)/shard_map/ppermute | solution.py:1051
  700.0 10.2 %collective-permute-done.49 = bf16[128,2944]{1,0:T(8,128)(2,1)} collective-permute-done((bf16[128,2944]{1,0:T(8,128)(2,1)}, bf16[128,2944]{1,0:T(8,128)(2,1)}, u32[]{:S(2)}, u32[]{:S(2)}) %collective-permute-start.49) | collective-permute-done | bytes 753696 | tf_op jit(solution)/shard_map/ppermute | solution.py:1051
  710.2 2.4 convert_add_fusion.2
  712.7 3.0 collective-permute-done.48
  715.6 2.4 convert_add_fusion.3
  718.0 2.4 copy.88
  722.6 2.6 collective-permute-start.44
  728.4 12.2 %collective-permute-done.43 = bf16[256,512]{0,1:T(8,128)(2,1)S(1)} collective-permute-done((bf16[256,512]{0,1:T(8,128)(2,1)S(1)}, bf16[256,512]{0,1:T(8,128)(2,1)S(1)}, u32[]{:S(2)}, u32[]{:S(2)}) %collective-permute-start.43) | collective-permute-done | bytes 262176 | tf_op jit(solution)/shard_map/ppermute | solution.py:1028
  740.6 3.1 collective-permute-done.44
  743.7 3.2 collective-permute-done.45
  748.8 2.4 ring_add.7.refs_1_
  753.6 3.0 copy.92
  (273 shorter events, 99.6 us)
Async XLA Ops:
  7.2 95.3 %all-gather.4.cloned.1.call-start = ((), (), s32[]{:S(2)}) async-start(), calls=%async_computation.5 | async-start | bytes 7077888 | tf_op jit(solution)/shard_map/all_gather | solution.py:1070
  11.1 180.7 %all-gather.6.cloned.1.call-start = ((), (), s32[]{:S(2)}) async-start(), calls=%async_computation.6 | async-start | bytes 19464192 | tf_op jit(solution)/shard_map/all_gather | solution.py:1072
  14.3 223.3 %all-gather.8.cloned.1.call-start = ((), (), s32[]{:S(2)}) async-start(), calls=%async_computation.7 | async-start | bytes 9437184 | tf_op jit(solution)/shard_map/all_gather | solution.py:1111
  15.7 17.7 %collective-permute-start = (bf16[640,512]{1,0:T(8,128)(2,1)S(1)}, bf16[640,512]{1,0:T(8,128)(2,1)S(1)}, u32[]{:S(2)}, u32[]{:S(2)}) collective-permute-start(bf16[640,512]{1,0:T(8,128)(2,1)S(1)} %pad_maximum_fusion.1.refs_0_), channel_id=1, source_target_pairs={{0,1},{1,2},{2,3},{3,0},{4,5},{5,6},{6,7},{7,4},{8,9},{9,10},{10,1... | collective-permute-start | bytes 1966088 | tf_op jit(solution)/shard_map/ppermute | solution.py:1028
  17.4 30.9 %copy-start.24 = (bf16[640,512]{1,0:T(8,128)(2,1)}, bf16[640,512]{1,0:T(8,128)(2,1)S(1)}, u32[]{:S(2)}) copy-start(bf16[640,512]{1,0:T(8,128)(2,1)S(1)} %pad_maximum_fusion.2.refs_4_) | copy-start | bytes 1966084
  17.4 30.0 %collective-permute-start.3 = (bf16[640,512]{1,0:T(8,128)(2,1)S(1)}, bf16[640,512]{1,0:T(8,128)(2,1)S(1)}, u32[]{:S(2)}, u32[]{:S(2)}) collective-permute-start(bf16[640,512]{1,0:T(8,128)(2,1)S(1)} %pad_maximum_fusion.2.refs_4_), channel_id=1, source_target_pairs={{0,1},{1,2},{2,3},{3,0},{4,5},{5,6},{6,7},{7,4},{8,9},{9,10},{10,1... | collective-permute-start | bytes 1966088 | tf_op jit(solution)/shard_map/ppermute | solution.py:1028
  34.3 43.4 %copy-start.38 = (f32[3,512]{1,0:T(4,128)S(1)}, f32[3,512]{1,0:T(4,128)}, u32[]{:S(2)}) copy-start(f32[3,512]{1,0:T(4,128)} %param.19) | copy-start | bytes 18436
  34.3 27.3 %collective-permute-start.1 = (bf16[640,512]{1,0:T(8,128)(2,1)}, bf16[640,512]{1,0:T(8,128)(2,1)}, u32[]{:S(2)}, u32[]{:S(2)}) collective-permute-start(bf16[640,512]{1,0:T(8,128)(2,1)} %tie.15.refs_1_), channel_id=1, source_target_pairs={{0,1},{1,2},{2,3},{3,0},{4,5},{5,6},{6,7},{7,4},{8,9},{9,10},{10,1... | collective-permute-start | bytes 1966088 | tf_op jit(solution)/shard_map/ppermute | solution.py:1028
  48.3 27.2 %collective-permute-start.4 = (bf16[640,512]{1,0:T(8,128)(2,1)}, bf16[640,512]{1,0:T(8,128)(2,1)S(1)}, u32[]{:S(2)}, u32[]{:S(2)}) collective-permute-start(bf16[640,512]{1,0:T(8,128)(2,1)} %tie.16.refs_5_), channel_id=1, source_target_pairs={{0,1},{1,2},{2,3},{3,0},{4,5},{5,6},{6,7},{7,4},{8,9},{9,10},{10,1... | collective-permute-start | bytes 1966088 | tf_op jit(solution)/shard_map/ppermute | solution.py:1028
  61.6 28.0 %collective-permute-start.2 = (bf16[640,512]{1,0:T(8,128)(2,1)}, bf16[640,512]{1,0:T(8,128)(2,1)S(1)}, u32[]{:S(2)}, u32[]{:S(2)}) collective-permute-start(bf16[640,512]{1,0:T(8,128)(2,1)} %collective-permute-done.1.refs_2_), channel_id=1, source_target_pairs={{0,1},{1,2},{2,3},{3,0},{4,5},{5,6},{6,7},{7,4},{8,9},{9,10},{10,1... | collective-permute-start | bytes 1966088 | tf_op jit(solution)/shard_map/ppermute | solution.py:1028
  75.5 26.9 %collective-permute-start.5 = (bf16[640,512]{1,0:T(8,128)(2,1)S(1)}, bf16[640,512]{1,0:T(8,128)(2,1)S(1)}, u32[]{:S(2)}, u32[]{:S(2)}) collective-permute-start(bf16[640,512]{1,0:T(8,128)(2,1)S(1)} %collective-permute-done.4.refs_6_), channel_id=1, source_target_pairs={{0,1},{1,2},{2,3},{3,0},{4,5},{5,6},{6,7},{7,4},{8,9},{9,10},{10,1... | collective-permute-start | bytes 1966088 | tf_op jit(solution)/shard_map/ppermute | solution.py:1028
  124.9 58.2 %collective-permute-start.7 = (bf16[2,1024,384]{2,1,0:T(8,128)(2,1)}, bf16[2,1024,384]{2,1,0:T(8,128)(2,1)}, u32[]{:S(2)}, u32[]{:S(2)}) collective-permute-start(bf16[2,1024,384]{2,1,0:T(8,128)(2,1)} %get-tuple-element.81), channel_id=1, source_target_pairs={{0,8},{4,12},{8,0},{12,4},{1,9},{5,13},{9,1},{13,5},{2,10},{6,14},... | collective-permute-start | bytes 4718600 | tf_op jit(solution)/shard_map/ppermute | solution.py:1031
  127.9 59.1 %copy-start.13 = (bf16[512,512]{1,0:T(8,128)(2,1)}, bf16[512,512]{1,0:T(8,128)(2,1)S(1)}, u32[]{:S(2)}) copy-start(bf16[512,512]{1,0:T(8,128)(2,1)S(1)} %get-tuple-element.211.refs_4_) | copy-start | bytes 1572868
  127.9 59.1 %copy-start.14 = (bf16[512,512]{1,0:T(8,128)(2,1)}, bf16[512,512]{1,0:T(8,128)(2,1)S(1)}, u32[]{:S(2)}) copy-start(bf16[512,512]{1,0:T(8,128)(2,1)S(1)} %get-tuple-element.212.refs_0_) | copy-start | bytes 1572868
  127.9 15.2 %collective-permute-start.10 = (bf16[512,512]{1,0:T(8,128)(2,1)S(1)}, bf16[512,512]{1,0:T(8,128)(2,1)S(1)}, u32[]{:S(2)}, u32[]{:S(2)}) collective-permute-start(bf16[512,512]{1,0:T(8,128)(2,1)S(1)} %get-tuple-element.211.refs_4_), channel_id=1, source_target_pairs={{0,1},{1,2},{2,3},{3,0},{4,5},{5,6},{6,7},{7,4},{8,9},{9,10},{10,1... | collective-permute-start | bytes 1572872 | tf_op jit(solution)/shard_map/ppermute | solution.py:1028
  129.6 24.8 %collective-permute-start.8 = (bf16[512,512]{1,0:T(8,128)(2,1)S(1)}, bf16[512,512]{1,0:T(8,128)(2,1)S(1)}, u32[]{:S(2)}, u32[]{:S(2)}) collective-permute-start(bf16[512,512]{1,0:T(8,128)(2,1)S(1)} %get-tuple-element.212.refs_0_), channel_id=1, source_target_pairs={{0,1},{1,2},{2,3},{3,0},{4,5},{5,6},{6,7},{7,4},{8,9},{9,10},{10,1... | collective-permute-start | bytes 1572872 | tf_op jit(solution)/shard_map/ppermute | solution.py:1028
  143.1 43.9 %copy-start.30 = (bf16[512,512]{1,0:T(8,128)(2,1)}, bf16[512,512]{1,0:T(8,128)(2,1)S(1)}, u32[]{:S(2)}) copy-start(bf16[512,512]{1,0:T(8,128)(2,1)S(1)} %collective-permute-done.10.refs_5_) | copy-start | bytes 1572868
  143.1 42.9 %collective-permute-start.11 = (bf16[512,512]{1,0:T(8,128)(2,1)S(1)}, bf16[512,512]{1,0:T(8,128)(2,1)S(1)}, u32[]{:S(2)}, u32[]{:S(2)}) collective-permute-start(bf16[512,512]{1,0:T(8,128)(2,1)S(1)} %collective-permute-done.10.refs_5_), channel_id=1, source_target_pairs={{0,1},{1,2},{2,3},{3,0},{4,5},{5,6},{6,7},{7,4},{8,9},{9,10},{10,1... | collective-permute-start | bytes 1572872 | tf_op jit(solution)/shard_map/ppermute | solution.py:1028
  154.3 32.7 %copy-start.31 = (bf16[512,512]{1,0:T(8,128)(2,1)}, bf16[512,512]{1,0:T(8,128)(2,1)S(1)}, u32[]{:S(2)}) copy-start(bf16[512,512]{1,0:T(8,128)(2,1)S(1)} %collective-permute-done.8.refs_1_) | copy-start | bytes 1572868
  154.3 31.7 %collective-permute-start.9 = (bf16[512,512]{1,0:T(8,128)(2,1)S(1)}, bf16[512,512]{1,0:T(8,128)(2,1)S(1)}, u32[]{:S(2)}, u32[]{:S(2)}) collective-permute-start(bf16[512,512]{1,0:T(8,128)(2,1)S(1)} %collective-permute-done.8.refs_1_), channel_id=1, source_target_pairs={{0,1},{1,2},{2,3},{3,0},{4,5},{5,6},{6,7},{7,4},{8,9},{9,10},{10,1... | collective-permute-start | bytes 1572872 | tf_op jit(solution)/shard_map/ppermute | solution.py:1028
  156.2 35.6 %collective-permute-start.6 = (bf16[1024,384]{1,0:T(8,128)(2,1)}, bf16[1024,384]{1,0:T(8,128)(2,1)}, u32[]{:S(2)}, u32[]{:S(2)}) collective-permute-start(bf16[1024,384]{1,0:T(8,128)(2,1)} %get-tuple-element.80), channel_id=1, source_target_pairs={{0,4},{4,0},{8,12},{12,8},{1,5},{5,1},{9,13},{13,9},{2,6},{6,2},{1... | collective-permute-start | bytes 2359304 | tf_op jit(solution)/shard_map/ppermute | solution.py:1031
  187.0 4.7 collective-permute-start.12
  188.8 43.6 %collective-permute-start.13 = (bf16[512,512]{1,0:T(8,128)(2,1)}, bf16[512,512]{1,0:T(8,128)(2,1)S(1)}, u32[]{:S(2)}, u32[]{:S(2)}) collective-permute-start(bf16[512,512]{1,0:T(8,128)(2,1)} %copy-done.12), channel_id=1, source_target_pairs={{0,1},{1,2},{2,3},{3,0},{4,5},{5,6},{6,7},{7,4},{8,9},{9,10},{10,1... | collective-permute-start | bytes 1572872 | tf_op jit(solution)/shard_map/ppermute | solution.py:1028
  190.3 42.1 %collective-permute-start.14 = (bf16[512,512]{1,0:T(8,128)(2,1)}, bf16[512,512]{1,0:T(8,128)(2,1)S(1)}, u32[]{:S(2)}, u32[]{:S(2)}) collective-permute-start(bf16[512,512]{1,0:T(8,128)(2,1)} %copy-done.11), channel_id=1, source_target_pairs={{0,1},{1,2},{2,3},{3,0},{4,5},{5,6},{6,7},{7,4},{8,9},{9,10},{10,1... | collective-permute-start | bytes 1572872 | tf_op jit(solution)/shard_map/ppermute | solution.py:1028
  233.4 28.4 %all-to-all-start = ((bf16[16,256,128]{2,1,0:T(8,128)(2,1)}), bf16[16,256,128]{2,1,0:T(8,128)(2,1)S(1)}, u32[]{:S(2)}, u32[]{:S(2)}) async-start(bf16[16,256,128]{2,1,0:T(8,128)(2,1)} %bitcast.118), calls=%async_computation | async-start | bytes 2097152 | tf_op jit(solution)/shard_map/all_to_all | solution.py:1131
  237.5 399.0 %reduce-scatter.6.cloned.1.call-start = ((), (), s32[]{:S(2)}) async-start(), calls=%async_computation.9 | async-start | bytes 6488064 | tf_op jit(solution)/shard_map/reduce_scatter | solution.py:1048
  272.3 26.0 %collective-permute-start.15 = (bf16[256,2048]{1,0:T(8,128)(2,1)}, bf16[256,2048]{1,0:T(8,128)(2,1)S(1)}, u32[]{:S(2)}, u32[]{:S(2)}) collective-permute-start(bf16[256,2048]{1,0:T(8,128)(2,1)} %get-tuple-element.85.low), channel_id=1, source_target_pairs={{0,1},{1,2},{2,3},{3,0},{4,5},{5,6},{6,7},{7,4},{8,9},{9,10},{10,1... | collective-permute-start | bytes 3145736 | tf_op jit(solution)/shard_map/ppermute | solution.py:1028
  299.3 28.2 %collective-permute-start.16 = (bf16[256,2048]{1,0:T(8,128)(2,1)}, bf16[256,2048]{1,0:T(8,128)(2,1)S(1)}, u32[]{:S(2)}, u32[]{:S(2)}) collective-permute-start(bf16[256,2048]{1,0:T(8,128)(2,1)} %tie.20.low), channel_id=1, source_target_pairs={{0,1},{1,2},{2,3},{3,0},{4,5},{5,6},{6,7},{7,4},{8,9},{9,10},{10,1... | collective-permute-start | bytes 3145736 | tf_op jit(solution)/shard_map/ppermute | solution.py:1028
  317.9 28.3 %collective-permute-start.19 = (bf16[128,2048]{1,0:T(8,128)(2,1)}, bf16[128,2048]{1,0:T(8,128)(2,1)S(1)}, u32[]{:S(2)}, u32[]{:S(2)}) collective-permute-start(bf16[128,2048]{1,0:T(8,128)(2,1)} %get-tuple-element.106), channel_id=1, source_target_pairs={{0,1},{1,2},{2,3},{3,0},{4,5},{5,6},{6,7},{7,4},{8,9},{9,10},{10,1... | collective-permute-start | bytes 1572872 | tf_op jit(solution)/shard_map/ppermute | solution.py:1028
  320.9 29.1 %collective-permute-start.18 = (bf16[128,2048]{1,0:T(8,128)(2,1)}, bf16[128,2048]{1,0:T(8,128)(2,1)S(1)}, u32[]{:S(2)}, u32[]{:S(2)}) collective-permute-start(bf16[128,2048]{1,0:T(8,128)(2,1)} %get-tuple-element.104), channel_id=1, source_target_pairs={{0,1},{1,2},{2,3},{3,0},{4,5},{5,6},{6,7},{7,4},{8,9},{9,10},{10,1... | collective-permute-start | bytes 1572872 | tf_op jit(solution)/shard_map/ppermute | solution.py:1028
  327.5 44.9 %collective-permute-start.17 = (bf16[256,2048]{1,0:T(8,128)(2,1)S(1)}, bf16[256,2048]{1,0:T(8,128)(2,1)S(1)}, u32[]{:S(2)}, u32[]{:S(2)}) collective-permute-start(bf16[256,2048]{1,0:T(8,128)(2,1)S(1)} %collective-permute-done.16.low), channel_id=1, source_target_pairs={{0,1},{1,2},{2,3},{3,0},{4,5},{5,6},{6,7},{7,4},{8,9},{9,10},{10,1... | collective-permute-start | bytes 3145736 | tf_op jit(solution)/shard_map/ppermute | solution.py:1028
  347.4 43.8 %collective-permute-start.22 = (bf16[128,2048]{1,0:T(8,128)(2,1)S(1)}, bf16[128,2048]{1,0:T(8,128)(2,1)S(1)}, u32[]{:S(2)}, u32[]{:S(2)}) collective-permute-start(bf16[128,2048]{1,0:T(8,128)(2,1)S(1)} %add_convert_fusion.4.refs_6_), channel_id=1, source_target_pairs={{0,1},{1,2},{2,3},{3,0},{4,5},{5,6},{6,7},{7,4},{8,9},{9,10},{10,1... | collective-permute-start | bytes 1572872 | tf_op jit(solution)/shard_map/ppermute | solution.py:1028
  351.2 42.0 %collective-permute-start.20 = (bf16[128,2048]{1,0:T(8,128)(2,1)S(1)}, bf16[128,2048]{1,0:T(8,128)(2,1)S(1)}, u32[]{:S(2)}, u32[]{:S(2)}) collective-permute-start(bf16[128,2048]{1,0:T(8,128)(2,1)S(1)} %add_convert_fusion.5.refs_5_), channel_id=1, source_target_pairs={{0,1},{1,2},{2,3},{3,0},{4,5},{5,6},{6,7},{7,4},{8,9},{9,10},{10,1... | collective-permute-start | bytes 1572872 | tf_op jit(solution)/shard_map/ppermute | solution.py:1028
  392.3 25.4 %collective-permute-start.23 = (bf16[128,2048]{1,0:T(8,128)(2,1)S(1)}, bf16[128,2048]{1,0:T(8,128)(2,1)S(1)}, u32[]{:S(2)}, u32[]{:S(2)}) collective-permute-start(bf16[128,2048]{1,0:T(8,128)(2,1)S(1)} %add_convert_fusion.2.refs_1_), channel_id=1, source_target_pairs={{0,1},{1,2},{2,3},{3,0},{4,5},{5,6},{6,7},{7,4},{8,9},{9,10},{10,1... | collective-permute-start | bytes 1572872 | tf_op jit(solution)/shard_map/ppermute | solution.py:1028
  394.3 23.4 %collective-permute-start.21 = (bf16[128,2048]{1,0:T(8,128)(2,1)S(1)}, bf16[128,2048]{1,0:T(8,128)(2,1)S(1)}, u32[]{:S(2)}, u32[]{:S(2)}) collective-permute-start(bf16[128,2048]{1,0:T(8,128)(2,1)S(1)} %add_convert_fusion.3.refs_0_), channel_id=1, source_target_pairs={{0,1},{1,2},{2,3},{3,0},{4,5},{5,6},{6,7},{7,4},{8,9},{9,10},{10,1... | collective-permute-start | bytes 1572872 | tf_op jit(solution)/shard_map/ppermute | solution.py:1028
  430.4 208.4 %reduce-scatter.4.cloned.1.call-start = ((), (), s32[]{:S(2)}) async-start(), calls=%async_computation.8 | async-start | bytes 6488064 | tf_op jit(solution)/shard_map/reduce_scatter | solution.py:1048
  431.0 32.6 %all-to-all-start.1 = ((bf16[16,256,128]{2,1,0:T(8,128)(2,1)}), bf16[16,256,128]{2,1,0:T(8,128)(2,1)}, u32[]{:S(2)}, u32[]{:S(2)}) async-start(bf16[16,256,128]{2,1,0:T(8,128)(2,1)} %bitcast.123), calls=%async_computation.1 | async-start | bytes 2097152 | tf_op jit(solution)/shard_map/all_to_all | solution.py:1184
  439.2 278.8 %reduce-scatter.8.cloned.1.call-start = ((), (), s32[]{:S(2)}) async-start(), calls=%async_computation.10 | async-start | bytes 9437184 | tf_op jit(solution)/shard_map/reduce_scatter | solution.py:1048
  439.3 92.9 %collective-permute-start.26 = (bf16[1024,1024]{1,0:T(8,128)(2,1)}, bf16[1024,1024]{1,0:T(8,128)(2,1)}, u32[]{:S(2)}, u32[]{:S(2)}) collective-permute-start(bf16[1024,1024]{1,0:T(8,128)(2,1)} %get-tuple-element.116), channel_id=1, source_target_pairs={{0,4},{4,0},{8,12},{12,8},{1,5},{5,1},{9,13},{13,9},{2,6},{6,2},{1... | collective-permute-start | bytes 6291464 | tf_op jit(solution)/shard_map/ppermute | solution.py:1031
  439.5 92.7 %collective-permute-start.27 = (bf16[1024,1408]{1,0:T(8,128)(2,1)S(1)}, bf16[1024,1408]{1,0:T(8,128)(2,1)}, u32[]{:S(2)}, u32[]{:S(2)}) collective-permute-start(bf16[1024,1408]{1,0:T(8,128)(2,1)S(1)} %copy-done), channel_id=1, source_target_pairs={{0,4},{4,0},{8,12},{12,8},{1,5},{5,1},{9,13},{13,9},{2,6},{6,2},{1... | collective-permute-start | bytes 8650760 | tf_op jit(solution)/shard_map/ppermute | solution.py:1031
  466.2 60.4 %collective-permute-start.24 = (bf16[1024,512]{1,0:T(8,128)(2,1)S(1)}, bf16[1024,512]{1,0:T(8,128)(2,1)S(1)}, u32[]{:S(2)}, u32[]{:S(2)}) collective-permute-start(bf16[1024,512]{1,0:T(8,128)(2,1)S(1)} %get-tuple-element.203), channel_id=1, source_target_pairs={{0,1},{1,2},{2,3},{3,0},{4,5},{5,6},{6,7},{7,4},{8,9},{9,10},{10,1... | collective-permute-start | bytes 3145736 | tf_op jit(solution)/shard_map/ppermute | solution.py:1028
  525.2 55.7 %collective-permute-start.30 = (bf16[2,1024,384]{2,1,0:T(8,128)(2,1)}, bf16[2,1024,384]{2,1,0:T(8,128)(2,1)}, u32[]{:S(2)}, u32[]{:S(2)}) collective-permute-start(bf16[2,1024,384]{2,1,0:T(8,128)(2,1)} %get-tuple-element.125), channel_id=1, source_target_pairs={{0,8},{4,12},{8,0},{12,4},{1,9},{5,13},{9,1},{13,5},{2,10},{6,14},... | collective-permute-start | bytes 4718600 | tf_op jit(solution)/shard_map/ppermute | solution.py:1031
  529.1 25.2 %collective-permute-start.25 = (bf16[1024,512]{1,0:T(8,128)(2,1)}, bf16[1024,512]{1,0:T(8,128)(2,1)}, u32[]{:S(2)}, u32[]{:S(2)}) collective-permute-start(bf16[1024,512]{1,0:T(8,128)(2,1)} %fusion.1), channel_id=1, source_target_pairs={{0,1},{1,2},{2,3},{3,0},{4,5},{5,6},{6,7},{7,4},{8,9},{9,10},{10,1... | collective-permute-start | bytes 3145736 | tf_op jit(solution)/shard_map/ppermute | solution.py:1028
  531.6 54.6 %collective-permute-start.32 = (bf16[1024,1024]{1,0:T(8,128)(2,1)}, bf16[1024,1024]{1,0:T(8,128)(2,1)}, u32[]{:S(2)}, u32[]{:S(2)}) collective-permute-start(bf16[1024,1024]{1,0:T(8,128)(2,1)} %get-tuple-element.127), channel_id=1, source_target_pairs={{0,4},{4,0},{8,12},{12,8},{1,5},{5,1},{9,13},{13,9},{2,6},{6,2},{1... | collective-permute-start | bytes 6291464 | tf_op jit(solution)/shard_map/ppermute | solution.py:1031
  556.8 26.8 %collective-permute-start.28 = (bf16[1024,512]{1,0:T(8,128)(2,1)}, bf16[1024,512]{1,0:T(8,128)(2,1)S(1)}, u32[]{:S(2)}, u32[]{:S(2)}) collective-permute-start(bf16[1024,512]{1,0:T(8,128)(2,1)} %ring_add.4.refs_1_), channel_id=1, source_target_pairs={{0,1},{1,2},{2,3},{3,0},{4,5},{5,6},{6,7},{7,4},{8,9},{9,10},{10,1... | collective-permute-start | bytes 3145736 | tf_op jit(solution)/shard_map/ppermute | solution.py:1028
  559.1 27.0 %collective-permute-start.29 = (bf16[1024,384]{1,0:T(8,128)(2,1)S(1)}, bf16[1024,384]{1,0:T(8,128)(2,1)S(1)}, u32[]{:S(2)}, u32[]{:S(2)}) collective-permute-start(bf16[1024,384]{1,0:T(8,128)(2,1)S(1)} %copy-done.46), channel_id=1, source_target_pairs={{0,4},{4,0},{8,12},{12,8},{1,5},{5,1},{9,13},{13,9},{2,6},{6,2},{1... | collective-permute-start | bytes 2359304 | tf_op jit(solution)/shard_map/ppermute | solution.py:1031
  583.7 2.5 collective-permute-start.31
  609.0 11.3 %collective-permute-start.37 = (bf16[1024,1536]{1,0:T(8,128)(2,1)}, bf16[1024,1536]{1,0:T(8,128)(2,1)S(1)}, u32[]{:S(2)}, u32[]{:S(2)}) collective-permute-start(bf16[1024,1536]{1,0:T(8,128)(2,1)} %get-tuple-element.136.right_here), channel_id=1, source_target_pairs={{0,4},{4,0},{8,12},{12,8},{1,5},{5,1},{9,13},{13,9},{2,6},{6,2},{1... | collective-permute-start | bytes 9437192 | tf_op jit(solution)/shard_map/ppermute | solution.py:1031
  610.6 7.8 %collective-permute-start.34 = (f32[1,8192]{1,0:T(1,128)S(1)}, f32[1,8192]{1,0:T(1,128)S(1)}, u32[]{:S(2)}, u32[]{:S(2)}) collective-permute-start(f32[1,8192]{1,0:T(1,128)S(1)} %constant_dynamic-update-slice_fusion), channel_id=1, source_target_pairs={{0,1},{1,2},{2,3},{3,0},{4,5},{5,6},{6,7},{7,4},{8,9},{9,10},{10,1... | collective-permute-start | bytes 98312 | tf_op jit(solution)/shard_map/ppermute | solution.py:1028
  612.2 7.0 collective-permute-start.35
  616.4 3.9 collective-permute-start.36
  616.4 25.6 %collective-permute-start.33 = (bf16[1024,512]{1,0:T(8,128)(2,1)}, bf16[1024,512]{1,0:T(8,128)(2,1)S(1)}, u32[]{:S(2)}, u32[]{:S(2)}) collective-permute-start(bf16[1024,512]{1,0:T(8,128)(2,1)} %get-tuple-element.128), channel_id=1, source_target_pairs={{0,1},{1,2},{2,3},{3,0},{4,5},{5,6},{6,7},{7,4},{8,9},{9,10},{10,1... | collective-permute-start | bytes 3145736 | tf_op jit(solution)/shard_map/ppermute | solution.py:1028
  635.8 45.6 %collective-permute-start.42 = (bf16[2,128,2944]{2,1,0:T(8,128)(2,1)}, bf16[2,128,2944]{2,1,0:T(8,128)(2,1)}, u32[]{:S(2)}, u32[]{:S(2)}) collective-permute-start(bf16[2,128,2944]{2,1,0:T(8,128)(2,1)} %get-tuple-element.143.refs_6_), channel_id=1, source_target_pairs={{0,8},{4,12},{8,0},{12,4},{1,9},{5,13},{9,1},{13,5},{2,10},{6,14},... | collective-permute-start | bytes 4521992 | tf_op jit(solution)/shard_map/ppermute | solution.py:1031
  645.4 25.5 %collective-permute-start.38 = (bf16[1024,512]{1,0:T(8,128)(2,1)}, bf16[1024,512]{1,0:T(8,128)(2,1)S(1)}, u32[]{:S(2)}, u32[]{:S(2)}) collective-permute-start(bf16[1024,512]{1,0:T(8,128)(2,1)} %ring_add.5.refs_1_), channel_id=1, source_target_pairs={{0,1},{1,2},{2,3},{3,0},{4,5},{5,6},{6,7},{7,4},{8,9},{9,10},{10,1... | collective-permute-start | bytes 3145736 | tf_op jit(solution)/shard_map/ppermute | solution.py:1028
  647.1 1.4 collective-permute-start.39
  647.1 47.3 %collective-permute-start.41 = (bf16[2,128,2944]{2,1,0:T(8,128)(2,1)}, bf16[2,128,2944]{2,1,0:T(8,128)(2,1)}, u32[]{:S(2)}, u32[]{:S(2)}) collective-permute-start(bf16[2,128,2944]{2,1,0:T(8,128)(2,1)} %get-tuple-element.141.refs_4_), channel_id=1, source_target_pairs={{0,16},{16,0},{1,17},{17,1},{2,18},{18,2},{3,19},{19,3},{4,20},{20... | collective-permute-start | bytes 4521992 | tf_op jit(solution)/shard_map/ppermute | solution.py:1051
  674.4 25.0 %collective-permute-start.46 = (f32[1,9728]{1,0:T(1,128)}, f32[1,9728]{1,0:T(1,128)S(1)}, u32[]{:S(2)}, u32[]{:S(2)}) collective-permute-start(f32[1,9728]{1,0:T(1,128)} %tie.28), channel_id=1, source_target_pairs={{0,8},{4,12},{8,0},{12,4},{1,9},{5,13},{9,1},{13,5},{2,10},{6,14},... | collective-permute-start | bytes 116744 | tf_op jit(solution)/shard_map/ppermute | solution.py:1240
  684.1 26.1 %collective-permute-start.49 = (bf16[128,2944]{1,0:T(8,128)(2,1)}, bf16[128,2944]{1,0:T(8,128)(2,1)}, u32[]{:S(2)}, u32[]{:S(2)}) collective-permute-start(bf16[128,2944]{1,0:T(8,128)(2,1)} %slice_bitcast_fusion.4), channel_id=1, source_target_pairs={{0,16},{16,0},{1,17},{17,1},{2,18},{18,2},{3,19},{19,3},{4,20},{20... | collective-permute-start | bytes 2261000 | tf_op jit(solution)/shard_map/ppermute | solution.py:1051
  697.2 18.4 %collective-permute-start.48 = (bf16[128,2944]{1,0:T(8,128)(2,1)}, bf16[128,2944]{1,0:T(8,128)(2,1)}, u32[]{:S(2)}, u32[]{:S(2)}) collective-permute-start(bf16[128,2944]{1,0:T(8,128)(2,1)} %slice_bitcast_fusion.6), channel_id=1, source_target_pairs={{0,8},{4,12},{8,0},{12,4},{1,9},{5,13},{9,1},{13,5},{2,10},{6,14},... | collective-permute-start | bytes 2261000 | tf_op jit(solution)/shard_map/ppermute | solution.py:1031
  697.2 51.6 %collective-permute-start.40 = (bf16[1024,512]{1,0:T(8,128)(2,1)}, bf16[1024,512]{1,0:T(8,128)(2,1)}, u32[]{:S(2)}, u32[]{:S(2)}) collective-permute-start(bf16[1024,512]{1,0:T(8,128)(2,1)} %ring_add.6.refs_1_), channel_id=1, source_target_pairs={{0,1},{1,2},{2,3},{3,0},{4,5},{5,6},{6,7},{7,4},{8,9},{9,10},{10,1... | collective-permute-start | bytes 3145736 | tf_op jit(solution)/shard_map/ppermute | solution.py:1028
  721.6 19.0 %collective-permute-start.43 = (bf16[256,512]{0,1:T(8,128)(2,1)S(1)}, bf16[256,512]{0,1:T(8,128)(2,1)S(1)}, u32[]{:S(2)}, u32[]{:S(2)}) collective-permute-start(bf16[256,512]{0,1:T(8,128)(2,1)S(1)} %get-tuple-element.208), channel_id=1, source_target_pairs={{0,1},{1,2},{2,3},{3,0},{4,5},{5,6},{6,7},{7,4},{8,9},{9,10},{10,1... | collective-permute-start | bytes 786440 | tf_op jit(solution)/shard_map/ppermute | solution.py:1028
  722.6 21.1 %collective-permute-start.44 = (bf16[256,512]{0,1:T(8,128)(2,1)S(1)}, bf16[256,512]{0,1:T(8,128)(2,1)S(1)}, u32[]{:S(2)}, u32[]{:S(2)}) collective-permute-start(bf16[256,512]{0,1:T(8,128)(2,1)S(1)} %get-tuple-element.210), channel_id=1, source_target_pairs={{0,2},{1,3},{2,0},{3,1},{4,6},{5,7},{6,4},{7,5},{8,10},{9,11},{10,... | collective-permute-start | bytes 786440 | tf_op jit(solution)/shard_map/ppermute | solution.py:1028
  725.3 21.7 %collective-permute-start.45 = (bf16[256,512]{0,1:T(8,128)(2,1)S(1)}, bf16[256,512]{0,1:T(8,128)(2,1)S(1)}, u32[]{:S(2)}, u32[]{:S(2)}) collective-permute-start(bf16[256,512]{0,1:T(8,128)(2,1)S(1)} %get-tuple-element.209), channel_id=1, source_target_pairs={{0,3},{1,0},{2,1},{3,2},{4,7},{5,4},{6,5},{7,6},{8,11},{9,8},{10,9... | collective-permute-start | bytes 786440 | tf_op jit(solution)/shard_map/ppermute | solution.py:1028
  751.3 7.5 collective-permute-start.47
  (44 other events, 328.9 us)
Sparse Core Ops, SparseCore 0:
  11.2 46.6 all-gather.3
  59.8 113.7 all-gather.5
  176.1 54.3 all-gather.7
  430.5 64.3 reduce-scatter.5
  498.5 82.2 reduce-scatter.3
  584.1 101.1 reduce-scatter.7

commit v4 on v3

--- a/solution.py
+++ b/solution.py
@@ -1050,9 +1050,8 @@
     def cross(value):
         return lax.ppermute(value, "fsdp", [(i, i ^ 1) for i in range(nfsdp)])
 
-    def square_once(parts):
-        near, far, low, high = parts
-        return total(near, cross(far)), total(low, swap(high, 2))
+    def square_once(parts, coming, last):
+        return total(tie(parts[0], last), coming[0]), total(tie(parts[2], last), coming[1])
 
     def square_twice(first, second):
         first = first[0].astype(F32) + swap(first[1], 2).astype(F32)
@@ -1247,27 +1246,26 @@
     small = sum([shift(small, step) for step in range(1, tp)], small)
     small = jnp.concatenate([bias_grad, small], axis=1)
     travelling, ring_steps = partial[1 % tp], []
-    once = square_once(parts) if square else ()
-    needed = [[total_gate, total_up, small, *parts], [], [*once]]
+    coming = [cross(parts[1]), swap(parts[3], 2)] if square else []
+    needed = [[total_gate, total_up, small, *parts], [], coming]
     for step in range(1, tp):
         travelling = add(
             shift(travelling, 1), partial[(step + 1) % tp], *(needed[step - 1] if step < 4 else [])
         )
         if step == 1:
-            out_parts = jnp.swapaxes(
-                tie(total_out, travelling).reshape(-1, tp, head_width), 0, 1
-            )
-            total_out = pick(out_parts, tensor_index).astype(F32)
-            for ahead in range(1, tp):
-                total_out = total_out + shift(pick(out_parts, (tensor_index + ahead) % tp), ahead).astype(F32)
-            total_out = total_out.T
-            needed[2].append(total_out)
-        if step < 3:
-            bits = powers(0, min(nctx, 2)) if step == 1 else powers(1, nctx)
-            small = exchange(tie(small, travelling), "ctx", bits, nctx)
-            needed[step].append(small)
-    small = exchange(tie(small, travelling), "fsdp", powers(0, nfsdp), nfsdp)
+            small = exchange(tie(small, travelling), "ctx", powers(0, min(nctx, 2)), nctx)
+            needed[1].append(small)
     grad_inputs = travelling
+    once = square_once(parts, coming, travelling) if square else ()
+    small = exchange(tie(small, travelling), "ctx", powers(1, nctx), nctx)
+    small = exchange(small, "fsdp", powers(0, nfsdp), nfsdp)
+
+    out_parts = jnp.swapaxes(tie(total_out, travelling).reshape(-1, tp, head_width), 0, 1)
+    total_out = pick(out_parts, tensor_index).astype(F32)
+    for step in range(1, tp):
+        total_out = total_out + shift(pick(out_parts, (tensor_index + step) % tp), step).astype(F32)
+    total_out = total_out.T
+
     if square:
         totals = square_twice(*once)
         total_down, total_qkv = totals[:, :inner].T, totals[:, inner:]

time: 770 us -> 766 us (level)
  Pallas kernels: 309 us -> 293 us
  local copies, waits for them, and re-layouts: 42.9 us -> 54.8 us
  other arithmetic: 37.2 us -> 29.5 us
    ppermute x3, waiting for transfers between devices: 1.43 us -> 13.2 us  [exchange(): lax.ppermute(value, axis, [(i, i ^ step) for i in range(size)])]
    another operation x0 -> x4, local copies, waits for them, and re-layouts: none -> 10.9 us
    ppermute x33, waiting for transfers between devices: 167 us -> 159 us  [shift(): return lax.ppermute(value, 'tp', [(i, (i + step) % tp) for i in range(tp)])]
    pallas_call x1, Pallas kernels: 58.5 us -> 50.2 us  [attend_back(): pl.pallas_call(functools.partial(attend_back_kernel, nctx, heads, len(pie...]
    unnamed x108 -> x117, local copies, waits for them, and re-layouts: 23.9 us -> 26.9 us
  transfers between devices with their start and end apart: 58 -> 58, of which waited for: 30 -> 33; matrix products, arithmetic and copies ran while one was open for 8% -> 7% of each run, Pallas kernels for 37% -> 36%
where the time goes in v4:
time: 766 us; the launch traced here: 756 us
  Pallas kernels  293 us (38%)
  waiting for transfers between devices  284 us (37%)
  starting transfers between devices  79.5 us (10%)
  local copies, waits for them, and re-layouts  54.8 us (7%)
  other arithmetic  29.5 us (4%)
  between operations  15.1 us (2%)
    ppermute x33, waiting for transfers between devices, shift(): return lax.ppermute(value, 'tp', [(i, (i + step) % tp) for i in range(tp)])  159 us
    pallas_call x4, Pallas kernels, feed(): pl.pallas_call(functools.partial(feed_kernel, tuple(cuts), parts, tp, ste...  70.8 us
    ppermute x33, starting transfers between devices, shift(): return lax.ppermute(value, 'tp', [(i, (i + step) % tp) for i in range(tp)])  57.1 us
    ppermute x12, waiting for transfers between devices, swap(): return lax.ppermute(value, 'ctx', [(i, i ^ step) for i in range(nctx)])  52.6 us
    pallas_call x1, Pallas kernels, attend_back(): pl.pallas_call(functools.partial(attend_back_kernel, nctx, heads, len(pie...  50.2 us
    pallas_call x1, Pallas kernels, attend(): pl.pallas_call(functools.partial(attend_kernel, nctx, heads, len(pieces),...  34.8 us
    pallas_call x3, Pallas kernels, blame(): pl.pallas_call(kernel, grid=(steps,), in_specs=in_specs + anywhere(len(ne...  27.9 us
    pallas_call x2, Pallas kernels, blame_halves(): pl.pallas_call(kernel, grid_spec=grid_spec, out_shape=[jax.ShapeDtypeStru...  27.6 us
  transfers between devices with their start and end apart: 58, of which 33 were waited for; matrix products, arithmetic and copies ran while one was open for 7% of the time, Pallas kernels for 36%

profile of v4, /device:TPU:8, one launch (start us, length us, event | category | flops | bytes accessed | tf_op | source)
XLA Modules:
  0.0 756.1 jit_solution(6591546769194634576)
XLA Ops:
  7.2 2.3 copy.146.refs_0_
  11.1 3.2 pack.1.refs_1_
  19.7 13.8 %collective-permute-done.refs_0_ = bf16[640,512]{1,0:T(8,128)(2,1)S(1)} collective-permute-done((bf16[640,512]{1,0:T(8,128)(2,1)S(1)}, bf16[640,512]{1,0:T(8,128)(2,1)S(1)}, u32[]{:S(2)}, u32[]{:S(2)}) %collective-permute-start) | collective-permute-done | bytes 655392 | tf_op jit(solution)/shard_map/ppermute | solution.py:1028
  35.9 11.6 %collective-permute-done.3.refs_0_ = bf16[640,512]{1,0:T(8,128)(2,1)S(1)} collective-permute-done((bf16[640,512]{1,0:T(8,128)(2,1)S(1)}, bf16[640,512]{1,0:T(8,128)(2,1)S(1)}, u32[]{:S(2)}, u32[]{:S(2)}) %collective-permute-start.3) | collective-permute-done | bytes 655392 | tf_op jit(solution)/shard_map/ppermute | solution.py:1028
  50.1 11.5 %collective-permute-done.1.refs_2_ = bf16[640,512]{1,0:T(8,128)(2,1)} collective-permute-done((bf16[640,512]{1,0:T(8,128)(2,1)}, bf16[640,512]{1,0:T(8,128)(2,1)}, u32[]{:S(2)}, u32[]{:S(2)}) %collective-permute-start.1) | collective-permute-done | bytes 655392 | tf_op jit(solution)/shard_map/ppermute | solution.py:1028
  63.2 12.4 %collective-permute-done.4.refs_6_ = bf16[640,512]{1,0:T(8,128)(2,1)S(1)} collective-permute-done((bf16[640,512]{1,0:T(8,128)(2,1)}, bf16[640,512]{1,0:T(8,128)(2,1)S(1)}, u32[]{:S(2)}, u32[]{:S(2)}) %collective-permute-start.4) | collective-permute-done | bytes 655392 | tf_op jit(solution)/shard_map/ppermute | solution.py:1028
  78.6 3.2 fusion.4
  81.8 7.8 %collective-permute-done.2.refs_3_.refs_1_ = bf16[640,512]{1,0:T(8,128)(2,1)S(1)} collective-permute-done((bf16[640,512]{1,0:T(8,128)(2,1)}, bf16[640,512]{1,0:T(8,128)(2,1)S(1)}, u32[]{:S(2)}, u32[]{:S(2)}) %collective-permute-start.2) | collective-permute-done | bytes 655392 | tf_op jit(solution)/shard_map/ppermute | solution.py:1028
  89.6 12.9 %collective-permute-done.5.refs_7_.refs_2_ = bf16[640,512]{1,0:T(8,128)(2,1)S(1)} collective-permute-done((bf16[640,512]{1,0:T(8,128)(2,1)S(1)}, bf16[640,512]{1,0:T(8,128)(2,1)S(1)}, u32[]{:S(2)}, u32[]{:S(2)}) %collective-permute-start.5) | collective-permute-done | bytes 655392 | tf_op jit(solution)/shard_map/ppermute | solution.py:1028
  103.4 21.5 %project.1 = (bf16[1024,2048]{1,0:T(8,128)(2,1)}, bf16[1024,2048]{1,0:T(8,128)(2,1)}, bf16[1024,1024]{1,0:T(8,128)(2,1)}, bf16[1024,384]{1,0:T(8,128)(2,1)}, bf1...) custom-call(s32[3]{0:T(128)} %pad_add_fusion.1.place, ...), custom_call_target="tpu_custom_call" | custom-call | flops 6000000000 | tf_op jit(solution)/shard_map/project/pallas_call | solution.py:225
  131.3 11.8 %collective-permute-done.10.refs_5_ = bf16[512,512]{1,0:T(8,128)(2,1)S(1)} collective-permute-done((bf16[512,512]{1,0:T(8,128)(2,1)S(1)}, bf16[512,512]{1,0:T(8,128)(2,1)S(1)}, u32[]{:S(2)}, u32[]{:S(2)}) %collective-permute-start.10) | collective-permute-done | bytes 524320 | tf_op jit(solution)/shard_map/ppermute | solution.py:1028
  144.4 9.9 %collective-permute-done.8.refs_1_ = bf16[512,512]{1,0:T(8,128)(2,1)S(1)} collective-permute-done((bf16[512,512]{1,0:T(8,128)(2,1)S(1)}, bf16[512,512]{1,0:T(8,128)(2,1)S(1)}, u32[]{:S(2)}, u32[]{:S(2)}) %collective-permute-start.8) | collective-permute-done | bytes 524320 | tf_op jit(solution)/shard_map/ppermute | solution.py:1028
  156.2 27.0 %collective-permute-done.7 = bf16[2,1024,384]{2,1,0:T(8,128)(2,1)} collective-permute-done((bf16[2,1024,384]{2,1,0:T(8,128)(2,1)}, bf16[2,1024,384]{2,1,0:T(8,128)(2,1)}, u32[]{:S(2)}, u32[]{:S(2)}) %collective-permute-start.7) | collective-permute-done | bytes 1572896 | tf_op jit(solution)/shard_map/ppermute | solution.py:1031
  183.1 2.9 slice_bitcast_fusion.2
  192.5 34.8 %attend.1 = (bf16[4096,128]{1,0:T(8,128)(2,1)}, bf16[4096,128]{1,0:T(8,128)(2,1)}, f32[2,4096]{1,0:T(2,128)}) custom-call(s32[1]{0:T(128)} %bitcast.1.place, s32[8]{0:T(128)} %fusion.27.lows, s32[8]{0:T(128)} %multiply_add_fusion.ends, s32[2,4096]{1,0:T(2,128)} %pad_add_fusion.bounds, bf16[1024,384]{1,0:T(8,128)(2,1)} %get-tuple-element.79.refs_0_, ...), custom_call_target="tpu_custom_call" | custom-call | flops 20000000000 | tf_op jit(solution)/shard_map/attend/pallas_call | solution.py:360
  228.3 4.2 all-to-all-start
  232.6 24.2 %all-to-all-done = bf16[16,256,128]{2,1,0:T(8,128)(2,1)S(1)} async-done(((bf16[16,256,128]{2,1,0:T(8,128)(2,1)}), bf16[16,256,128]{2,1,0:T(8,128)(2,1)S(1)}, u32[]{:S(2)}, u32[]{:S(2)}) %all-to-all-start) | async-done | bytes 1048608 | tf_op jit(solution)/shard_map/all_to_all | solution.py:1130
  257.7 9.5 %mix.1 = (bf16[256,2048]{1,0:T(8,128)(2,1)}, f32[256,2048]{1,0:T(8,128)}, bf16[256,2048]{1,0:T(8,128)(2,1)}) custom-call(s32[3]{0:T(128)} %pad_add_fusion.1.place, bf16[4,4,256,128]{3,2,1,0:T(8,128)(2,1)} %bitcast.118, bf16[4,2048,512]{2,1,0:T(8,128)(2,1)} %all-gather.8.cloned.1.call-done.weight.refs_7_, ...), custom_call_target="tpu_custom_call" | custom-call | flops 5000000000 | tf_op jit(solution)/shard_map/mix/pallas_call | solution.py:533
  267.8 6.0 join.1
  273.8 17.7 %feed.4 = (bf16[1024,2048]{1,0:T(8,128)(2,1)}, bf16[1024,1408]{1,0:T(8,128)(2,1)}, bf16[1024,1408]{1,0:T(8,128)(2,1)}, bf16[1024,1408]{1,0:T(8,128)(2,1)}, bf16[...) custom-call(s32[3]{0:T(128)} %pad_add_fusion.1.place, ...), custom_call_target="tpu_custom_call" | custom-call | flops 10000000000 | tf_op jit(solution)/shard_map/feed/pallas_call | solution.py:623
  295.1 17.7 %feed.5 = (bf16[1024,2048]{1,0:T(8,128)(2,1)}, bf16[1024,1408]{1,0:T(8,128)(2,1)}, bf16[1024,1408]{1,0:T(8,128)(2,1)}, bf16[1024,1408]{1,0:T(8,128)(2,1)}, bf16[...) custom-call(s32[3]{0:T(128)} %pad_add_fusion.1.place, ...), custom_call_target="tpu_custom_call", output_to_operand_aliasing={{0}: (5, {}), {1}: (6, {}), {2}: (7, {}), {3}: (8, {}), {4}... | custom-call | flops 10000000000 | tf_op jit(solution)/shard_map/feed/pallas_call | solution.py:623
  312.8 3.0 collective-permute-start.19
  315.8 3.0 collective-permute-start.18
  318.9 3.6 collective-permute-done.16.low
  323.4 17.7 %feed.6 = (bf16[1024,2048]{1,0:T(8,128)(2,1)}, bf16[1024,1408]{1,0:T(8,128)(2,1)}, bf16[1024,1408]{1,0:T(8,128)(2,1)}, bf16[1024,1408]{1,0:T(8,128)(2,1)}, bf16[...) custom-call(s32[3]{0:T(128)} %pad_add_fusion.1.place, ...), custom_call_target="tpu_custom_call", output_to_operand_aliasing={{0}: (5, {}), {1}: (6, {}), {2}: (7, {}), {3}: (8, {}), {4}... | custom-call | flops 10000000000 | tf_op jit(solution)/shard_map/feed/pallas_call | solution.py:623
  345.1 3.7 collective-permute-start.20
  348.8 18.6 %collective-permute-done.17.low = bf16[256,2048]{1,0:T(8,128)(2,1)S(1)} collective-permute-done((bf16[256,2048]{1,0:T(8,128)(2,1)S(1)}, bf16[256,2048]{1,0:T(8,128)(2,1)S(1)}, u32[]{:S(2)}, u32[]{:S(2)}) %collective-permute-start.17) | collective-permute-done | bytes 1048608 | tf_op jit(solution)/shard_map/ppermute | solution.py:1028
  368.4 17.7 %feed.7 = (bf16[1024,2048]{1,0:T(8,128)(2,1)}, bf16[1024,1408]{1,0:T(8,128)(2,1)}, bf16[1024,1408]{1,0:T(8,128)(2,1)}, bf16[1024,1408]{1,0:T(8,128)(2,1)}, bf16[...) custom-call(s32[3]{0:T(128)} %pad_add_fusion.1.place, ...), custom_call_target="tpu_custom_call", output_to_operand_aliasing={{0}: (5, {}), {1}: (6, {}), {2}: (7, {}), {3}: (8, {}), {4}... | custom-call | flops 10000000000 | tf_op jit(solution)/shard_map/feed/pallas_call | solution.py:623
  390.5 10.6 %blame.4.refs_9_.refs_0_ = bf16[2048,1408]{1,0:T(8,128)(2,1)} custom-call(bf16[1024,2048]{1,0:T(8,128)(2,1)} %get-tuple-element.112.left, bf16[1024,1408]{1,0:T(8,128)(2,1)} %get-tuple-element.114.right, bf16[128,2048]{1,0:T(8,128)(2,1)} %copy-done.40, bf16[128,2048]{1,0:T(8,128)(2,1)} %copy-done.39), custom_call_target="tpu_custom_call" | custom-call | flops 6000000000 | tf_op jit(solution)/shard_map/blame/pallas_call | solution.py:726
  401.1 10.6 %blame.3.refs_8_.refs_0_ = bf16[2048,1408]{1,0:T(8,128)(2,1)} custom-call(bf16[1024,2048]{1,0:T(8,128)(2,1)} %get-tuple-element.112.left, bf16[1024,1408]{1,0:T(8,128)(2,1)} %get-tuple-element.113.right, bf16[128,2048]{1,0:T(8,128)(2,1)} %copy-done.40, bf16[128,2048]{1,0:T(8,128)(2,1)} %copy-done.39), custom_call_target="tpu_custom_call" | custom-call | flops 6000000000 | tf_op jit(solution)/shard_map/blame/pallas_call | solution.py:726
  412.7 11.7 %turn.1 = (bf16[4,4,256,128]{3,2,1,0:T(8,128)(2,1)}, f32[256,2048]{1,0:T(8,128)}, bf16[256,2048]{1,0:T(8,128)(2,1)}, f32[1,2048]{1,0:T(1,128)}, f32[1,2048]{1,0:T(1,128)}, /*index=5*/bf16[256,1024]{1,0:T(8,128)(2,1)}) custom-call(s32[3]{0:T(128)} %pad_add_fusion.1.place, bf16[128,2048]{1,0:T(8,128)(2,1)} %copy-done.38, bf16[128,2048]{1,0:T(8,128)(2,1)} %copy-done.35, ...), custom_call_target="tpu_custom_call" | custom-call | flops 6000000000 | tf_op jit(solution)/shard_map/turn/pallas_call | solution.py:798
  424.9 8.2 %all-to-all-start.1 = ((bf16[16,256,128]{2,1,0:T(8,128)(2,1)}), bf16[16,256,128]{2,1,0:T(8,128)(2,1)}, u32[]{:S(2)}, u32[]{:S(2)}) async-start(bf16[16,256,128]{2,1,0:T(8,128)(2,1)} %bitcast.117), calls=%async_computation.1 | async-start | bytes 2097152 | tf_op jit(solution)/shard_map/all_to_all | solution.py:1183
  433.8 6.7 blame.5.refs_6_.refs_0_
  440.5 17.0 %all-to-all-done.1 = bf16[16,256,128]{2,1,0:T(8,128)(2,1)} async-done(((bf16[16,256,128]{2,1,0:T(8,128)(2,1)}), bf16[16,256,128]{2,1,0:T(8,128)(2,1)}, u32[]{:S(2)}, u32[]{:S(2)}) %all-to-all-start.1) | async-done | bytes 1048608 | tf_op jit(solution)/shard_map/all_to_all | solution.py:1183
  457.5 2.6 dynamic-slice_bitcast_fusion
  460.7 50.2 %attend_back.1 = (bf16[1024,384]{1,0:T(8,128)(2,1)}, bf16[1024,384]{1,0:T(8,128)(2,1)}, bf16[2,1024,384]{2,1,0:T(8,128)(2,1)}) custom-call(s32[1]{0:T(128)} %bitcast.1.place, s32[8]{0:T(128)} %fusion.27.lows, s32[8]{0:T(128)} %multiply_add_fusion.ends, s32[2,4096]{1,0:T(2,128)} %pad_add_fusion.bounds, f32[2,4096]{1,0:T(2,128)} %get-tuple-element.119.logs, ...), custom_call_target="tpu_custom_call" | custom-call | flops 24999999488 | tf_op jit(solution)/shard_map/attend_back/pallas_call | solution.py:476
  513.8 2.5 collective-permute-start.25
  517.0 14.0 %blame_halves.2 = (bf16[2,128,2944]{2,1,0:T(8,128)(2,1)}, bf16[2,128,2944]{2,1,0:T(8,128)(2,1)}, bf16[2,128,2944]{2,1,0:T(8,128)(2,1)}, bf16[2,128,2944]{2,1,0:T(8,128)(2,1)}) custom-call(s32[4]{0:T(128)} %pad_add_fusion.2.place, bf16[4,1024,512]{2,1,0:T(8,128)(2,1)} %get-tuple-element.86.cot.refs_5_.left_here, ...), custom_call_target="tpu_custom_call" | custom-call | flops 6000000000 | tf_op jit(solution)/shard_map/blame_halves/pallas_call | solution.py:698
  531.0 7.6 %collective-permute-done.25.left = bf16[1024,512]{1,0:T(8,128)(2,1)S(1)} collective-permute-done((bf16[1024,512]{1,0:T(8,128)(2,1)S(1)}, bf16[1024,512]{1,0:T(8,128)(2,1)S(1)}, u32[]{:S(2)}, u32[]{:S(2)}) %collective-permute-start.25) | collective-permute-done | bytes 1048608 | tf_op jit(solution)/shard_map/ppermute | solution.py:1028
  539.6 2.5 ring_add.4.refs_1_
  542.1 2.5 collective-permute-start.28
  544.6 21.8 %collective-permute-done.30 = bf16[2,1024,384]{2,1,0:T(8,128)(2,1)S(1)} collective-permute-done((bf16[2,1024,384]{2,1,0:T(8,128)(2,1)}, bf16[2,1024,384]{2,1,0:T(8,128)(2,1)S(1)}, u32[]{:S(2)}, u32[]{:S(2)}) %collective-permute-start.30) | collective-permute-done | bytes 1572896 | tf_op jit(solution)/shard_map/ppermute | solution.py:1031
  568.3 2.5 fusion.refs_11_
  571.9 19.8 %finish.1 = (bf16[1024,512]{1,0:T(8,128)(2,1)}, bf16[1024,512]{1,0:T(8,128)(2,1)}, bf16[1024,512]{1,0:T(8,128)(2,1)}, bf16[1024,512]{1,0:T(8,128)(2,1)}, bf16[10...) custom-call(s32[3]{0:T(128)} %pad_add_fusion.1.place, ...), custom_call_target="tpu_custom_call" | custom-call | flops 7000000000 | tf_op jit(solution)/shard_map/finish/pallas_call | solution.py:910
  593.2 3.0 collective-permute-start.34
  596.3 3.1 collective-permute-start.35
  606.4 13.6 %blame_halves.3 = (bf16[2,128,2944]{2,1,0:T(8,128)(2,1)}, bf16[2,128,2944]{2,1,0:T(8,128)(2,1)}, bf16[2,128,2944]{2,1,0:T(8,128)(2,1)}, bf16[2,128,2944]{2,1,0:T(8,128)(2,1)}) custom-call(s32[4]{0:T(128)} %pad_add_fusion.2.place, ...), custom_call_target="tpu_custom_call", output_to_operand_aliasing={{0}: (5, {}), {1}: (6, {}), {2}: (7, {}), {3}: (8, {})} | custom-call | flops 6000000000 | tf_op jit(solution)/shard_map/blame_halves/pallas_call | solution.py:698
  620.0 2.3 convert_element_type.158.refs_1_
  627.0 2.4 ring_add.5.refs_1_
  636.1 17.4 %collective-permute-done.38.left = bf16[1024,512]{1,0:T(8,128)(2,1)} collective-permute-done((bf16[1024,512]{1,0:T(8,128)(2,1)}, bf16[1024,512]{1,0:T(8,128)(2,1)}, u32[]{:S(2)}, u32[]{:S(2)}) %collective-permute-start.38) | collective-permute-done | bytes 1048608 | tf_op jit(solution)/shard_map/ppermute | solution.py:1028
  653.5 2.5 ring_add.6
  658.2 18.0 %collective-permute-done.41.refs_0_ = bf16[2,128,2944]{2,1,0:T(8,128)(2,1)S(1)} collective-permute-done((bf16[2,128,2944]{2,1,0:T(8,128)(2,1)}, bf16[2,128,2944]{2,1,0:T(8,128)(2,1)S(1)}, u32[]{:S(2)}, u32[]{:S(2)}) %collective-permute-start.41) | collective-permute-done | bytes 1507360 | tf_op jit(solution)/shard_map/ppermute | solution.py:1051
  677.4 3.4 collective-permute-done.40.left
  680.9 2.4 ring_add.7.refs_1_
  688.4 3.1 collective-permute-done.43
  693.5 8.7 %collective-permute-done.44 = f32[1,9728]{1,0:T(1,128)S(1)} collective-permute-done((f32[1,9728]{1,0:T(1,128)S(1)}, f32[1,9728]{1,0:T(1,128)S(1)}, u32[]{:S(2)}, u32[]{:S(2)}) %collective-permute-start.44) | collective-permute-done | bytes 38944 | tf_op jit(solution)/shard_map/ppermute | solution.py:1239
  704.8 2.6 collective-permute-done.45
  710.1 2.9 copy.105
  713.0 2.6 reshape.310
  715.6 6.0 constant_dynamic-slice_fusion.3
  727.1 4.0 collective-permute-start.48
  737.6 3.6 collective-permute-done.47
  741.2 2.8 collective-permute-done.48
  744.0 3.1 collective-permute-done.49
  (286 shorter events, 109.5 us)
Async XLA Ops:
  7.2 95.3 %all-gather.4.cloned.1.call-start = ((), (), s32[]{:S(2)}) async-start(), calls=%async_computation.5 | async-start | bytes 7077888 | tf_op jit(solution)/shard_map/all_gather | solution.py:1069
  11.1 180.6 %all-gather.6.cloned.1.call-start = ((), (), s32[]{:S(2)}) async-start(), calls=%async_computation.6 | async-start | bytes 19464192 | tf_op jit(solution)/shard_map/all_gather | solution.py:1071
  14.3 218.2 %all-gather.8.cloned.1.call-start = ((), (), s32[]{:S(2)}) async-start(), calls=%async_computation.7 | async-start | bytes 9437184 | tf_op jit(solution)/shard_map/all_gather | solution.py:1110
  15.8 17.7 %collective-permute-start = (bf16[640,512]{1,0:T(8,128)(2,1)S(1)}, bf16[640,512]{1,0:T(8,128)(2,1)S(1)}, u32[]{:S(2)}, u32[]{:S(2)}) collective-permute-start(bf16[640,512]{1,0:T(8,128)(2,1)S(1)} %pad_maximum_fusion.1.refs_0_), channel_id=1, source_target_pairs={{0,1},{1,2},{2,3},{3,0},{4,5},{5,6},{6,7},{7,4},{8,9},{9,10},{10,1... | collective-permute-start | bytes 1966088 | tf_op jit(solution)/shard_map/ppermute | solution.py:1028
  17.4 30.0 %collective-permute-start.3 = (bf16[640,512]{1,0:T(8,128)(2,1)S(1)}, bf16[640,512]{1,0:T(8,128)(2,1)S(1)}, u32[]{:S(2)}, u32[]{:S(2)}) collective-permute-start(bf16[640,512]{1,0:T(8,128)(2,1)S(1)} %pad_maximum_fusion.2.refs_4_), channel_id=1, source_target_pairs={{0,1},{1,2},{2,3},{3,0},{4,5},{5,6},{6,7},{7,4},{8,9},{9,10},{10,1... | collective-permute-start | bytes 1966088 | tf_op jit(solution)/shard_map/ppermute | solution.py:1028
  34.3 43.4 %copy-start.43 = (f32[3,512]{1,0:T(4,128)S(1)}, f32[3,512]{1,0:T(4,128)}, u32[]{:S(2)}) copy-start(f32[3,512]{1,0:T(4,128)} %param.19) | copy-start | bytes 18436
  34.3 27.3 %collective-permute-start.1 = (bf16[640,512]{1,0:T(8,128)(2,1)}, bf16[640,512]{1,0:T(8,128)(2,1)}, u32[]{:S(2)}, u32[]{:S(2)}) collective-permute-start(bf16[640,512]{1,0:T(8,128)(2,1)} %tie.16.refs_1_), channel_id=1, source_target_pairs={{0,1},{1,2},{2,3},{3,0},{4,5},{5,6},{6,7},{7,4},{8,9},{9,10},{10,1... | collective-permute-start | bytes 1966088 | tf_op jit(solution)/shard_map/ppermute | solution.py:1028
  48.3 27.2 %collective-permute-start.4 = (bf16[640,512]{1,0:T(8,128)(2,1)}, bf16[640,512]{1,0:T(8,128)(2,1)S(1)}, u32[]{:S(2)}, u32[]{:S(2)}) collective-permute-start(bf16[640,512]{1,0:T(8,128)(2,1)} %tie.17.refs_5_), channel_id=1, source_target_pairs={{0,1},{1,2},{2,3},{3,0},{4,5},{5,6},{6,7},{7,4},{8,9},{9,10},{10,1... | collective-permute-start | bytes 1966088 | tf_op jit(solution)/shard_map/ppermute | solution.py:1028
  61.6 28.0 %collective-permute-start.2 = (bf16[640,512]{1,0:T(8,128)(2,1)}, bf16[640,512]{1,0:T(8,128)(2,1)S(1)}, u32[]{:S(2)}, u32[]{:S(2)}) collective-permute-start(bf16[640,512]{1,0:T(8,128)(2,1)} %collective-permute-done.1.refs_2_), channel_id=1, source_target_pairs={{0,1},{1,2},{2,3},{3,0},{4,5},{5,6},{6,7},{7,4},{8,9},{9,10},{10,1... | collective-permute-start | bytes 1966088 | tf_op jit(solution)/shard_map/ppermute | solution.py:1028
  75.6 26.9 %copy-start.53 = (bf16[640,512]{1,0:T(8,128)(2,1)}, bf16[640,512]{1,0:T(8,128)(2,1)S(1)}, u32[]{:S(2)}) copy-start(bf16[640,512]{1,0:T(8,128)(2,1)S(1)} %collective-permute-done.4.refs_6_) | copy-start | bytes 1966084
  75.6 26.9 %collective-permute-start.5 = (bf16[640,512]{1,0:T(8,128)(2,1)S(1)}, bf16[640,512]{1,0:T(8,128)(2,1)S(1)}, u32[]{:S(2)}, u32[]{:S(2)}) collective-permute-start(bf16[640,512]{1,0:T(8,128)(2,1)S(1)} %collective-permute-done.4.refs_6_), channel_id=1, source_target_pairs={{0,1},{1,2},{2,3},{3,0},{4,5},{5,6},{6,7},{7,4},{8,9},{9,10},{10,1... | collective-permute-start | bytes 1966088 | tf_op jit(solution)/shard_map/ppermute | solution.py:1028
  124.9 58.2 %collective-permute-start.7 = (bf16[2,1024,384]{2,1,0:T(8,128)(2,1)}, bf16[2,1024,384]{2,1,0:T(8,128)(2,1)}, u32[]{:S(2)}, u32[]{:S(2)}) collective-permute-start(bf16[2,1024,384]{2,1,0:T(8,128)(2,1)} %get-tuple-element.81), channel_id=1, source_target_pairs={{0,8},{4,12},{8,0},{12,4},{1,9},{5,13},{9,1},{13,5},{2,10},{6,14},... | collective-permute-start | bytes 4718600 | tf_op jit(solution)/shard_map/ppermute | solution.py:1031
  127.8 58.2 %copy-start.15 = (bf16[512,512]{1,0:T(8,128)(2,1)}, bf16[512,512]{1,0:T(8,128)(2,1)S(1)}, u32[]{:S(2)}) copy-start(bf16[512,512]{1,0:T(8,128)(2,1)S(1)} %get-tuple-element.212.refs_4_) | copy-start | bytes 1572868
  127.8 58.2 %copy-start.16 = (bf16[512,512]{1,0:T(8,128)(2,1)}, bf16[512,512]{1,0:T(8,128)(2,1)S(1)}, u32[]{:S(2)}) copy-start(bf16[512,512]{1,0:T(8,128)(2,1)S(1)} %get-tuple-element.213.refs_0_) | copy-start | bytes 1572868
  127.8 15.3 %collective-permute-start.10 = (bf16[512,512]{1,0:T(8,128)(2,1)S(1)}, bf16[512,512]{1,0:T(8,128)(2,1)S(1)}, u32[]{:S(2)}, u32[]{:S(2)}) collective-permute-start(bf16[512,512]{1,0:T(8,128)(2,1)S(1)} %get-tuple-element.212.refs_4_), channel_id=1, source_target_pairs={{0,1},{1,2},{2,3},{3,0},{4,5},{5,6},{6,7},{7,4},{8,9},{9,10},{10,1... | collective-permute-start | bytes 1572872 | tf_op jit(solution)/shard_map/ppermute | solution.py:1028
  129.5 24.8 %collective-permute-start.8 = (bf16[512,512]{1,0:T(8,128)(2,1)S(1)}, bf16[512,512]{1,0:T(8,128)(2,1)S(1)}, u32[]{:S(2)}, u32[]{:S(2)}) collective-permute-start(bf16[512,512]{1,0:T(8,128)(2,1)S(1)} %get-tuple-element.213.refs_0_), channel_id=1, source_target_pairs={{0,1},{1,2},{2,3},{3,0},{4,5},{5,6},{6,7},{7,4},{8,9},{9,10},{10,1... | collective-permute-start | bytes 1572872 | tf_op jit(solution)/shard_map/ppermute | solution.py:1028
  143.1 42.9 %copy-start.33 = (bf16[512,512]{1,0:T(8,128)(2,1)}, bf16[512,512]{1,0:T(8,128)(2,1)S(1)}, u32[]{:S(2)}) copy-start(bf16[512,512]{1,0:T(8,128)(2,1)S(1)} %collective-permute-done.10.refs_5_) | copy-start | bytes 1572868
  143.1 42.9 %collective-permute-start.11 = (bf16[512,512]{1,0:T(8,128)(2,1)S(1)}, bf16[512,512]{1,0:T(8,128)(2,1)S(1)}, u32[]{:S(2)}, u32[]{:S(2)}) collective-permute-start(bf16[512,512]{1,0:T(8,128)(2,1)S(1)} %collective-permute-done.10.refs_5_), channel_id=1, source_target_pairs={{0,1},{1,2},{2,3},{3,0},{4,5},{5,6},{6,7},{7,4},{8,9},{9,10},{10,1... | collective-permute-start | bytes 1572872 | tf_op jit(solution)/shard_map/ppermute | solution.py:1028
  154.3 31.7 %copy-start.34 = (bf16[512,512]{1,0:T(8,128)(2,1)}, bf16[512,512]{1,0:T(8,128)(2,1)S(1)}, u32[]{:S(2)}) copy-start(bf16[512,512]{1,0:T(8,128)(2,1)S(1)} %collective-permute-done.8.refs_1_) | copy-start | bytes 1572868
  154.3 31.7 %collective-permute-start.9 = (bf16[512,512]{1,0:T(8,128)(2,1)S(1)}, bf16[512,512]{1,0:T(8,128)(2,1)S(1)}, u32[]{:S(2)}, u32[]{:S(2)}) collective-permute-start(bf16[512,512]{1,0:T(8,128)(2,1)S(1)} %collective-permute-done.8.refs_1_), channel_id=1, source_target_pairs={{0,1},{1,2},{2,3},{3,0},{4,5},{5,6},{6,7},{7,4},{8,9},{9,10},{10,1... | collective-permute-start | bytes 1572872 | tf_op jit(solution)/shard_map/ppermute | solution.py:1028
  156.1 35.5 %collective-permute-start.6 = (bf16[1024,384]{1,0:T(8,128)(2,1)}, bf16[1024,384]{1,0:T(8,128)(2,1)}, u32[]{:S(2)}, u32[]{:S(2)}) collective-permute-start(bf16[1024,384]{1,0:T(8,128)(2,1)} %get-tuple-element.80), channel_id=1, source_target_pairs={{0,4},{4,0},{8,12},{12,8},{1,5},{5,1},{9,13},{13,9},{2,6},{6,2},{1... | collective-permute-start | bytes 2359304 | tf_op jit(solution)/shard_map/ppermute | solution.py:1031
  187.0 4.7 collective-permute-start.12
  188.7 38.6 %collective-permute-start.13 = (bf16[512,512]{1,0:T(8,128)(2,1)}, bf16[512,512]{1,0:T(8,128)(2,1)S(1)}, u32[]{:S(2)}, u32[]{:S(2)}) collective-permute-start(bf16[512,512]{1,0:T(8,128)(2,1)} %copy-done.14), channel_id=1, source_target_pairs={{0,1},{1,2},{2,3},{3,0},{4,5},{5,6},{6,7},{7,4},{8,9},{9,10},{10,1... | collective-permute-start | bytes 1572872 | tf_op jit(solution)/shard_map/ppermute | solution.py:1028
  190.2 37.2 %collective-permute-start.14 = (bf16[512,512]{1,0:T(8,128)(2,1)}, bf16[512,512]{1,0:T(8,128)(2,1)S(1)}, u32[]{:S(2)}, u32[]{:S(2)}) collective-permute-start(bf16[512,512]{1,0:T(8,128)(2,1)} %copy-done.13), channel_id=1, source_target_pairs={{0,1},{1,2},{2,3},{3,0},{4,5},{5,6},{6,7},{7,4},{8,9},{9,10},{10,1... | collective-permute-start | bytes 1572872 | tf_op jit(solution)/shard_map/ppermute | solution.py:1028
  228.3 28.4 %all-to-all-start = ((bf16[16,256,128]{2,1,0:T(8,128)(2,1)}), bf16[16,256,128]{2,1,0:T(8,128)(2,1)S(1)}, u32[]{:S(2)}, u32[]{:S(2)}) async-start(bf16[16,256,128]{2,1,0:T(8,128)(2,1)} %bitcast.114), calls=%async_computation | async-start | bytes 2097152 | tf_op jit(solution)/shard_map/all_to_all | solution.py:1130
  232.5 387.5 %reduce-scatter.6.cloned.1.call-start = ((), (), s32[]{:S(2)}) async-start(), calls=%async_computation.9 | async-start | bytes 6488064 | tf_op jit(solution)/shard_map/reduce_scatter | solution.py:1048
  267.2 26.0 %collective-permute-start.15 = (bf16[256,2048]{1,0:T(8,128)(2,1)}, bf16[256,2048]{1,0:T(8,128)(2,1)S(1)}, u32[]{:S(2)}, u32[]{:S(2)}) collective-permute-start(bf16[256,2048]{1,0:T(8,128)(2,1)} %get-tuple-element.85.low), channel_id=1, source_target_pairs={{0,1},{1,2},{2,3},{3,0},{4,5},{5,6},{6,7},{7,4},{8,9},{9,10},{10,1... | collective-permute-start | bytes 3145736 | tf_op jit(solution)/shard_map/ppermute | solution.py:1028
  294.2 28.2 %collective-permute-start.16 = (bf16[256,2048]{1,0:T(8,128)(2,1)}, bf16[256,2048]{1,0:T(8,128)(2,1)S(1)}, u32[]{:S(2)}, u32[]{:S(2)}) collective-permute-start(bf16[256,2048]{1,0:T(8,128)(2,1)} %tie.21.low), channel_id=1, source_target_pairs={{0,1},{1,2},{2,3},{3,0},{4,5},{5,6},{6,7},{7,4},{8,9},{9,10},{10,1... | collective-permute-start | bytes 3145736 | tf_op jit(solution)/shard_map/ppermute | solution.py:1028
  312.8 28.4 %collective-permute-start.19 = (bf16[128,2048]{1,0:T(8,128)(2,1)}, bf16[128,2048]{1,0:T(8,128)(2,1)S(1)}, u32[]{:S(2)}, u32[]{:S(2)}) collective-permute-start(bf16[128,2048]{1,0:T(8,128)(2,1)} %get-tuple-element.106), channel_id=1, source_target_pairs={{0,1},{1,2},{2,3},{3,0},{4,5},{5,6},{6,7},{7,4},{8,9},{9,10},{10,1... | collective-permute-start | bytes 1572872 | tf_op jit(solution)/shard_map/ppermute | solution.py:1028
  315.8 29.1 %collective-permute-start.18 = (bf16[128,2048]{1,0:T(8,128)(2,1)}, bf16[128,2048]{1,0:T(8,128)(2,1)S(1)}, u32[]{:S(2)}, u32[]{:S(2)}) collective-permute-start(bf16[128,2048]{1,0:T(8,128)(2,1)} %get-tuple-element.104), channel_id=1, source_target_pairs={{0,1},{1,2},{2,3},{3,0},{4,5},{5,6},{6,7},{7,4},{8,9},{9,10},{10,1... | collective-permute-start | bytes 1572872 | tf_op jit(solution)/shard_map/ppermute | solution.py:1028
  322.5 44.9 %collective-permute-start.17 = (bf16[256,2048]{1,0:T(8,128)(2,1)S(1)}, bf16[256,2048]{1,0:T(8,128)(2,1)S(1)}, u32[]{:S(2)}, u32[]{:S(2)}) collective-permute-start(bf16[256,2048]{1,0:T(8,128)(2,1)S(1)} %collective-permute-done.16.low), channel_id=1, source_target_pairs={{0,1},{1,2},{2,3},{3,0},{4,5},{5,6},{6,7},{7,4},{8,9},{9,10},{10,1... | collective-permute-start | bytes 3145736 | tf_op jit(solution)/shard_map/ppermute | solution.py:1028
  342.4 43.7 %collective-permute-start.22 = (bf16[128,2048]{1,0:T(8,128)(2,1)S(1)}, bf16[128,2048]{1,0:T(8,128)(2,1)S(1)}, u32[]{:S(2)}, u32[]{:S(2)}) collective-permute-start(bf16[128,2048]{1,0:T(8,128)(2,1)S(1)} %add_convert_fusion.4.refs_6_), channel_id=1, source_target_pairs={{0,1},{1,2},{2,3},{3,0},{4,5},{5,6},{6,7},{7,4},{8,9},{9,10},{10,1... | collective-permute-start | bytes 1572872 | tf_op jit(solution)/shard_map/ppermute | solution.py:1028
  345.1 43.0 %collective-permute-start.20 = (bf16[128,2048]{1,0:T(8,128)(2,1)S(1)}, bf16[128,2048]{1,0:T(8,128)(2,1)S(1)}, u32[]{:S(2)}, u32[]{:S(2)}) collective-permute-start(bf16[128,2048]{1,0:T(8,128)(2,1)S(1)} %add_convert_fusion.5.refs_5_), channel_id=1, source_target_pairs={{0,1},{1,2},{2,3},{3,0},{4,5},{5,6},{6,7},{7,4},{8,9},{9,10},{10,1... | collective-permute-start | bytes 1572872 | tf_op jit(solution)/shard_map/ppermute | solution.py:1028
  387.3 24.3 %collective-permute-start.23 = (bf16[128,2048]{1,0:T(8,128)(2,1)S(1)}, bf16[128,2048]{1,0:T(8,128)(2,1)S(1)}, u32[]{:S(2)}, u32[]{:S(2)}) collective-permute-start(bf16[128,2048]{1,0:T(8,128)(2,1)S(1)} %add_convert_fusion.2.refs_1_), channel_id=1, source_target_pairs={{0,1},{1,2},{2,3},{3,0},{4,5},{5,6},{6,7},{7,4},{8,9},{9,10},{10,1... | collective-permute-start | bytes 1572872 | tf_op jit(solution)/shard_map/ppermute | solution.py:1028
  388.2 23.5 %collective-permute-start.21 = (bf16[128,2048]{1,0:T(8,128)(2,1)S(1)}, bf16[128,2048]{1,0:T(8,128)(2,1)S(1)}, u32[]{:S(2)}, u32[]{:S(2)}) collective-permute-start(bf16[128,2048]{1,0:T(8,128)(2,1)S(1)} %add_convert_fusion.3.refs_0_), channel_id=1, source_target_pairs={{0,1},{1,2},{2,3},{3,0},{4,5},{5,6},{6,7},{7,4},{8,9},{9,10},{10,1... | collective-permute-start | bytes 1572872 | tf_op jit(solution)/shard_map/ppermute | solution.py:1028
  424.3 198.0 %reduce-scatter.4.cloned.1.call-start = ((), (), s32[]{:S(2)}) async-start(), calls=%async_computation.8 | async-start | bytes 6488064 | tf_op jit(solution)/shard_map/reduce_scatter | solution.py:1048
  424.9 32.6 %all-to-all-start.1 = ((bf16[16,256,128]{2,1,0:T(8,128)(2,1)}), bf16[16,256,128]{2,1,0:T(8,128)(2,1)}, u32[]{:S(2)}, u32[]{:S(2)}) async-start(bf16[16,256,128]{2,1,0:T(8,128)(2,1)} %bitcast.117), calls=%async_computation.1 | async-start | bytes 2097152 | tf_op jit(solution)/shard_map/all_to_all | solution.py:1183
  433.2 279.8 %reduce-scatter.8.cloned.1.call-start = ((), (), s32[]{:S(2)}) async-start(), calls=%async_computation.10 | async-start | bytes 9437184 | tf_op jit(solution)/shard_map/reduce_scatter | solution.py:1048
  433.2 83.7 %collective-permute-start.26 = (bf16[1024,1024]{1,0:T(8,128)(2,1)}, bf16[1024,1024]{1,0:T(8,128)(2,1)}, u32[]{:S(2)}, u32[]{:S(2)}) collective-permute-start(bf16[1024,1024]{1,0:T(8,128)(2,1)} %get-tuple-element.116), channel_id=1, source_target_pairs={{0,4},{4,0},{8,12},{12,8},{1,5},{5,1},{9,13},{13,9},{2,6},{6,2},{1... | collective-permute-start | bytes 6291464 | tf_op jit(solution)/shard_map/ppermute | solution.py:1031
  433.5 83.5 %collective-permute-start.27 = (bf16[1024,1408]{1,0:T(8,128)(2,1)S(1)}, bf16[1024,1408]{1,0:T(8,128)(2,1)}, u32[]{:S(2)}, u32[]{:S(2)}) collective-permute-start(bf16[1024,1408]{1,0:T(8,128)(2,1)S(1)} %copy-done), channel_id=1, source_target_pairs={{0,4},{4,0},{8,12},{12,8},{1,5},{5,1},{9,13},{13,9},{2,6},{6,2},{1... | collective-permute-start | bytes 8650760 | tf_op jit(solution)/shard_map/ppermute | solution.py:1031
  460.2 52.1 %collective-permute-start.24 = (bf16[1024,512]{1,0:T(8,128)(2,1)S(1)}, bf16[1024,512]{1,0:T(8,128)(2,1)S(1)}, u32[]{:S(2)}, u32[]{:S(2)}) collective-permute-start(bf16[1024,512]{1,0:T(8,128)(2,1)S(1)} %get-tuple-element.203), channel_id=1, source_target_pairs={{0,1},{1,2},{2,3},{3,0},{4,5},{5,6},{6,7},{7,4},{8,9},{9,10},{10,1... | collective-permute-start | bytes 3145736 | tf_op jit(solution)/shard_map/ppermute | solution.py:1028
  510.9 55.5 %collective-permute-start.30 = (bf16[2,1024,384]{2,1,0:T(8,128)(2,1)}, bf16[2,1024,384]{2,1,0:T(8,128)(2,1)S(1)}, u32[]{:S(2)}, u32[]{:S(2)}) collective-permute-start(bf16[2,1024,384]{2,1,0:T(8,128)(2,1)} %get-tuple-element.125), channel_id=1, source_target_pairs={{0,8},{4,12},{8,0},{12,4},{1,9},{5,13},{9,1},{13,5},{2,10},{6,14},... | collective-permute-start | bytes 4718600 | tf_op jit(solution)/shard_map/ppermute | solution.py:1031
  513.8 24.8 %collective-permute-start.25 = (bf16[1024,512]{1,0:T(8,128)(2,1)S(1)}, bf16[1024,512]{1,0:T(8,128)(2,1)S(1)}, u32[]{:S(2)}, u32[]{:S(2)}) collective-permute-start(bf16[1024,512]{1,0:T(8,128)(2,1)S(1)} %fusion.1), channel_id=1, source_target_pairs={{0,1},{1,2},{2,3},{3,0},{4,5},{5,6},{6,7},{7,4},{8,9},{9,10},{10,1... | collective-permute-start | bytes 3145736 | tf_op jit(solution)/shard_map/ppermute | solution.py:1028
  516.3 54.4 %collective-permute-start.32 = (bf16[1024,1024]{1,0:T(8,128)(2,1)}, bf16[1024,1024]{1,0:T(8,128)(2,1)}, u32[]{:S(2)}, u32[]{:S(2)}) collective-permute-start(bf16[1024,1024]{1,0:T(8,128)(2,1)} %get-tuple-element.127), channel_id=1, source_target_pairs={{0,4},{4,0},{8,12},{12,8},{1,5},{5,1},{9,13},{13,9},{2,6},{6,2},{1... | collective-permute-start | bytes 6291464 | tf_op jit(solution)/shard_map/ppermute | solution.py:1031
  542.1 26.2 %collective-permute-start.28 = (bf16[1024,512]{1,0:T(8,128)(2,1)}, bf16[1024,512]{1,0:T(8,128)(2,1)S(1)}, u32[]{:S(2)}, u32[]{:S(2)}) collective-permute-start(bf16[1024,512]{1,0:T(8,128)(2,1)} %ring_add.4.refs_1_), channel_id=1, source_target_pairs={{0,1},{1,2},{2,3},{3,0},{4,5},{5,6},{6,7},{7,4},{8,9},{9,10},{10,1... | collective-permute-start | bytes 3145736 | tf_op jit(solution)/shard_map/ppermute | solution.py:1028
  544.6 26.2 %collective-permute-start.29 = (bf16[1024,384]{1,0:T(8,128)(2,1)S(1)}, bf16[1024,384]{1,0:T(8,128)(2,1)S(1)}, u32[]{:S(2)}, u32[]{:S(2)}) collective-permute-start(bf16[1024,384]{1,0:T(8,128)(2,1)S(1)} %copy-done.50), channel_id=1, source_target_pairs={{0,4},{4,0},{8,12},{12,8},{1,5},{5,1},{9,13},{13,9},{2,6},{6,2},{1... | collective-permute-start | bytes 2359304 | tf_op jit(solution)/shard_map/ppermute | solution.py:1031
  567.6 3.2 collective-permute-start.31
  591.7 13.0 %collective-permute-start.37 = (bf16[1024,1536]{1,0:T(8,128)(2,1)}, bf16[1024,1536]{1,0:T(8,128)(2,1)S(1)}, u32[]{:S(2)}, u32[]{:S(2)}) collective-permute-start(bf16[1024,1536]{1,0:T(8,128)(2,1)} %get-tuple-element.136.right_here), channel_id=1, source_target_pairs={{0,4},{4,0},{8,12},{12,8},{1,5},{5,1},{9,13},{13,9},{2,6},{6,2},{1... | collective-permute-start | bytes 9437192 | tf_op jit(solution)/shard_map/ppermute | solution.py:1031
  593.2 8.1 %collective-permute-start.34 = (f32[1,8192]{1,0:T(1,128)S(1)}, f32[1,8192]{1,0:T(1,128)S(1)}, u32[]{:S(2)}, u32[]{:S(2)}) collective-permute-start(f32[1,8192]{1,0:T(1,128)S(1)} %constant_dynamic-update-slice_fusion), channel_id=1, source_target_pairs={{0,1},{1,2},{2,3},{3,0},{4,5},{5,6},{6,7},{7,4},{8,9},{9,10},{10,1... | collective-permute-start | bytes 98312 | tf_op jit(solution)/shard_map/ppermute | solution.py:1028
  596.3 5.5 collective-permute-start.35
  599.3 3.9 collective-permute-start.36
  601.3 24.7 %collective-permute-start.33 = (bf16[1024,512]{1,0:T(8,128)(2,1)}, bf16[1024,512]{1,0:T(8,128)(2,1)S(1)}, u32[]{:S(2)}, u32[]{:S(2)}) collective-permute-start(bf16[1024,512]{1,0:T(8,128)(2,1)} %get-tuple-element.128), channel_id=1, source_target_pairs={{0,1},{1,2},{2,3},{3,0},{4,5},{5,6},{6,7},{7,4},{8,9},{9,10},{10,1... | collective-permute-start | bytes 3145736 | tf_op jit(solution)/shard_map/ppermute | solution.py:1028
  629.4 24.0 %collective-permute-start.38 = (bf16[1024,512]{1,0:T(8,128)(2,1)}, bf16[1024,512]{1,0:T(8,128)(2,1)}, u32[]{:S(2)}, u32[]{:S(2)}) collective-permute-start(bf16[1024,512]{1,0:T(8,128)(2,1)} %ring_add.5.refs_1_), channel_id=1, source_target_pairs={{0,1},{1,2},{2,3},{3,0},{4,5},{5,6},{6,7},{7,4},{8,9},{9,10},{10,1... | collective-permute-start | bytes 3145736 | tf_op jit(solution)/shard_map/ppermute | solution.py:1028
  630.6 45.6 %collective-permute-start.41 = (bf16[2,128,2944]{2,1,0:T(8,128)(2,1)}, bf16[2,128,2944]{2,1,0:T(8,128)(2,1)S(1)}, u32[]{:S(2)}, u32[]{:S(2)}) collective-permute-start(bf16[2,128,2944]{2,1,0:T(8,128)(2,1)} %get-tuple-element.141.refs_4_), channel_id=1, source_target_pairs={{0,16},{16,0},{1,17},{17,1},{2,18},{18,2},{3,19},{19,3},{4,20},{20... | collective-permute-start | bytes 4521992 | tf_op jit(solution)/shard_map/ppermute | solution.py:1051
  632.1 45.4 %collective-permute-start.42 = (bf16[2,128,2944]{2,1,0:T(8,128)(2,1)}, bf16[2,128,2944]{2,1,0:T(8,128)(2,1)S(1)}, u32[]{:S(2)}, u32[]{:S(2)}) collective-permute-start(bf16[2,128,2944]{2,1,0:T(8,128)(2,1)} %get-tuple-element.143.refs_6_), channel_id=1, source_target_pairs={{0,8},{4,12},{8,0},{12,4},{1,9},{5,13},{9,1},{13,5},{2,10},{6,14},... | collective-permute-start | bytes 4521992 | tf_op jit(solution)/shard_map/ppermute | solution.py:1031
  633.2 1.4 collective-permute-start.39
  655.9 24.9 %collective-permute-start.40 = (bf16[1024,512]{1,0:T(8,128)(2,1)}, bf16[1024,512]{1,0:T(8,128)(2,1)}, u32[]{:S(2)}, u32[]{:S(2)}) collective-permute-start(bf16[1024,512]{1,0:T(8,128)(2,1)} %ring_add.6), channel_id=1, source_target_pairs={{0,1},{1,2},{2,3},{3,0},{4,5},{5,6},{6,7},{7,4},{8,9},{9,10},{10,1... | collective-permute-start | bytes 3145736 | tf_op jit(solution)/shard_map/ppermute | solution.py:1028
  685.6 17.9 %collective-permute-start.46 = (bf16[128,2944]{1,0:T(8,128)(2,1)S(1)}, bf16[128,2944]{1,0:T(8,128)(2,1)}, u32[]{:S(2)}, u32[]{:S(2)}) collective-permute-start(bf16[128,2944]{1,0:T(8,128)(2,1)S(1)} %slice_bitcast_fusion.4), channel_id=1, source_target_pairs={{0,16},{16,0},{1,17},{17,1},{2,18},{18,2},{3,19},{19,3},{4,20},{20... | collective-permute-start | bytes 2261000 | tf_op jit(solution)/shard_map/ppermute | solution.py:1051
  687.2 4.3 collective-permute-start.43
  691.5 10.7 %collective-permute-start.44 = (f32[1,9728]{1,0:T(1,128)S(1)}, f32[1,9728]{1,0:T(1,128)S(1)}, u32[]{:S(2)}, u32[]{:S(2)}) collective-permute-start(f32[1,9728]{1,0:T(1,128)S(1)} %add.234), channel_id=1, source_target_pairs={{0,16},{16,0},{1,17},{17,1},{2,18},{18,2},{3,19},{19,3},{4,20},{20... | collective-permute-start | bytes 116744 | tf_op jit(solution)/shard_map/ppermute | solution.py:1239
  692.7 14.7 %collective-permute-start.45 = (bf16[128,2944]{1,0:T(8,128)(2,1)}, bf16[128,2944]{1,0:T(8,128)(2,1)}, u32[]{:S(2)}, u32[]{:S(2)}) collective-permute-start(bf16[128,2944]{1,0:T(8,128)(2,1)} %slice_bitcast_fusion.6), channel_id=1, source_target_pairs={{0,8},{4,12},{8,0},{12,4},{1,9},{5,13},{9,1},{13,5},{2,10},{6,14},... | collective-permute-start | bytes 2261000 | tf_op jit(solution)/shard_map/ppermute | solution.py:1031
  723.5 17.7 %collective-permute-start.47 = (bf16[256,512]{0,1:T(8,128)(2,1)}, bf16[256,512]{0,1:T(8,128)(2,1)}, u32[]{:S(2)}, u32[]{:S(2)}) collective-permute-start(bf16[256,512]{0,1:T(8,128)(2,1)} %bitcast.120), channel_id=1, source_target_pairs={{0,1},{1,2},{2,3},{3,0},{4,5},{5,6},{6,7},{7,4},{8,9},{9,10},{10,1... | collective-permute-start | bytes 786440 | tf_op jit(solution)/shard_map/ppermute | solution.py:1028
  727.1 16.9 %collective-permute-start.48 = (bf16[256,512]{0,1:T(8,128)(2,1)}, bf16[256,512]{0,1:T(8,128)(2,1)}, u32[]{:S(2)}, u32[]{:S(2)}) collective-permute-start(bf16[256,512]{0,1:T(8,128)(2,1)} %bitcast.121), channel_id=1, source_target_pairs={{0,2},{1,3},{2,0},{3,1},{4,6},{5,7},{6,4},{7,5},{8,10},{9,11},{10,... | collective-permute-start | bytes 786440 | tf_op jit(solution)/shard_map/ppermute | solution.py:1028
  732.2 14.9 %collective-permute-start.49 = (bf16[256,512]{0,1:T(8,128)(2,1)}, bf16[256,512]{0,1:T(8,128)(2,1)S(1)}, u32[]{:S(2)}, u32[]{:S(2)}) collective-permute-start(bf16[256,512]{0,1:T(8,128)(2,1)} %bitcast.122), channel_id=1, source_target_pairs={{0,3},{1,0},{2,1},{3,2},{4,7},{5,4},{6,5},{7,6},{8,11},{9,8},{10,9... | collective-permute-start | bytes 786440 | tf_op jit(solution)/shard_map/ppermute | solution.py:1028
  (48 other events, 231.9 us)
Sparse Core Ops, SparseCore 0:
  11.2 46.6 all-gather.3
  59.8 113.7 all-gather.5
  176.1 54.3 all-gather.7
  424.5 66.6 reduce-scatter.5
  494.8 77.1 reduce-scatter.3
  575.3 85.1 reduce-scatter.7
